TPU v7x, 128 devices: a whole 4x4x4 slice. The times are simulated.
128 devices in a mesh: occ: 4 (over z_lo, core), aux: 32 (over y, z_hi, x).
Axes of the slice: x: 4, y: 4, z: 4 (z_hi: 2, z_lo: 2; z = z_hi * 2 + z_lo), core: 2. Of those that a mesh axis runs over, the one named last changes fastest.
Arguments:
- three_index: bfloat16 [768, 32, 20480], P(None, 'occ', 'aux'), may hold values from -6 to 6
- tile_mask: int32 [4, 6], replicated, may hold values from 0 to 1, as said below
- occ_density: bfloat16 [32, 32], replicated, may hold values from -1 to 1
- virt_density: bfloat16 [768, 768], replicated, may hold values from -0.21875 to 0.21875
Outputs:
- gamma: bfloat16 [768, 32, 20480], P('aux', 'occ')
Inputs may be any that keep to these rules, and one draw needn't show every extreme that they name: `tile_mask`: each slab's row holds between 2 and 4 ones, and some slab's row holds exactly 4.
All inputs are finite; a program needn't handle non-finite values.
Results may differ from a plain program's by a relative error of at most 0.001.
Values may be sent and summed in bfloat16 or wider, within the bound.
No kernel may reach another device: no remote copies, remote signals or barrier semaphores. Data moves between devices by JAX's collectives and lax.ppermute only.
A program may use at most 256 MiB of HBM per device.

v0:
```python
import jax
import jax.numpy as jnp
from jax import lax
from jax.sharding import PartitionSpec as P

VT = 6


def from_behind(shard, axis, by):
    peers = lax.axis_size(axis)
    return lax.ppermute(shard, axis, [(i, (i + by) % peers) for i in range(peers)])


def tile_flags_of(tile_mask, source_slab):
    return lax.dynamic_index_in_dim(tile_mask, source_slab, 0, keepdims=False)


def local(three_index, tile_mask, occ_density, virt_density):
    virt_count, occ_rows, aux_cols = three_index.shape
    tile_width = virt_count // VT
    slab_count = lax.axis_size("occ")
    my_slab = lax.axis_index("occ")
    own_flags = jnp.repeat(tile_flags_of(tile_mask, my_slab), tile_width)
    own_block = three_index * own_flags.astype(jnp.bfloat16)[:, None, None]
    my_density = lax.dynamic_slice_in_dim(occ_density, my_slab * occ_rows, occ_rows, 0)

    def occupied_term(slab_block, source_slab):
        density_cols = lax.dynamic_slice_in_dim(my_density, source_slab * occ_rows, occ_rows, 1)
        return jnp.einsum(
            "ij,ajp->aip", density_cols, slab_block, preferred_element_type=jnp.float32
        )

    total = jnp.dot(
        virt_density,
        own_block.reshape(virt_count, occ_rows * aux_cols),
        preferred_element_type=jnp.float32,
    )
    total = total.reshape(virt_count, occ_rows, aux_cols) + occupied_term(own_block, my_slab)
    moving = own_block
    for distance in range(1, slab_count):
        moving = from_behind(moving, "occ", 1)
        total = total + occupied_term(moving, (my_slab - distance) % slab_count)
    gamma_local = total.astype(jnp.bfloat16)
    return lax.all_to_all(gamma_local, "aux", split_axis=0, concat_axis=2, tiled=True)


def solution(mesh):
    return jax.shard_map(
        local,
        mesh=mesh,
        in_specs=(P(None, "occ", "aux"), P(), P(), P()),
        out_specs=P("aux", "occ", None),
        check_vma=False,
    )
```

profile of v0, /device:TPU:2, one launch (start us, length us, event | category | flops | bytes accessed | tf_op | source)
XLA Modules:
  0.0 406.3 jit_solution(5472211689032034657)
XLA Ops:
  0.0 0.0 copy-start
  0.0 0.8 convert_bitcast_fusion
  0.8 0.1 broadcast_bitcast_fusion
  0.9 5.3 %broadcast_multiply_fusion = bf16[768,8,640]{2,1,0:T(8,128)(2,1)S(1)} fusion(bf16[768,8,640]{2,1,0:T(8,128)(2,1)} %param.4, bf16[768]{0:T(1024)(128)(2,1)S(1)} %broadcast_bitcast_fusion), kind=kLoop, calls=%fused_computation.5 | loop fusion | flops 3932160 | bytes 15730176 | tf_op jit(solution)/shard_map/mul | solution.py:24
  6.2 0.0 copy-start.2
  6.2 3.1 copy-done.2
  9.3 0.0 collective-permute-start
  9.3 87.3 %collective-permute-done = bf16[768,8,640]{2,1,0:T(8,128)(2,1)S(1)} collective-permute-done((bf16[768,8,640]{2,1,0:T(8,128)(2,1)S(1)}, bf16[768,8,640]{2,1,0:T(8,128)(2,1)S(1)}, u32[]{:S(2)}, u32[]{:S(2)}) %collective-permute-start) | collective-permute-done | bytes 7864352 | tf_op jit(solution)/shard_map/ppermute | solution.py:11
  96.6 0.0 copy-start.3
  96.6 3.2 copy-done.3
  99.8 0.0 collective-permute-start.1
  99.8 87.4 %collective-permute-done.1 = bf16[768,8,640]{2,1,0:T(8,128)(2,1)} collective-permute-done((bf16[768,8,640]{2,1,0:T(8,128)(2,1)S(1)}, bf16[768,8,640]{2,1,0:T(8,128)(2,1)}, u32[]{:S(2)}, u32[]{:S(2)}) %collective-permute-start.1) | collective-permute-done | bytes 7864352 | tf_op jit(solution)/shard_map/ppermute | solution.py:11
  187.2 0.0 collective-permute-start.2
  187.2 5.1 %copy.7 = bf16[96,8,8,640]{3,1,2,0:T(8,128)(2,1)S(1)} copy(bf16[96,8,8,640]{3,2,1,0:T(8,128)(2,1)} %bitcast.47) | data formatting | bytes 15728640
  192.3 0.0 copy-done
  192.3 9.9 %fusion.12 = f32[5120,768]{1,0:T(8,128)} fusion(bf16[768,5120]{1,0:T(8,128)(2,1)S(1)} %bitcast.50, bf16[768,768]{1,0:T(8,128)(2,1)S(1)} %copy-done), kind=kOutput, calls=%fused_computation.19 | convolution fusion | flops 6039797760 | bytes 24772608 | tf_op jit(solution)/shard_map/dot_general | solution.py:33
  202.2 0.0 copy-start.4
  202.2 15.9 %copy.5 = f32[768,8,640]{2,1,0:T(8,128)} copy(f32[768,8,640]{0,2,1:T(8,128)} %bitcast.49) | data formatting | bytes 31457280 | tf_op jit(solution)/shard_map/reshape | solution.py:38
  218.0 0.0 copy-done.4
  218.0 11.0 %fusion.6 = f32[768,640,8]{1,2,0:T(8,128)} fusion(bf16[768,8,640]{2,1,0:T(8,128)(2,1)} %copy-done.2, bf16[32,32]{1,0:T(8,128)(2,1)S(1)} %copy-done.4, s32[]{:T(128)S(6)} %select_n.42), kind=kOutput, calls=%fused_computation.11 | convolution fusion | flops 62914560 | bytes 23595012 | tf_op jit(solution)/shard_map/ij,ajp->aip/dot_general | solution.py:29
  229.0 10.9 %fusion.4 = f32[768,640,8]{1,2,0:T(8,128)} fusion(bf16[768,8,640]{2,1,0:T(8,128)(2,1)} %copy-done.3, bf16[32,32]{1,0:T(8,128)(2,1)S(1)} %copy-done.4, s32[]{:T(128)S(6)} %select_n.42, s32[]{:T(128)S(6)} %select_n.45), kind=kOutput, calls=%fused_computation.9 | convolution fusion | flops 62914560 | bytes 23595016 | tf_op jit(solution)/shard_map/ij,ajp->aip/dot_general | solution.py:29
  239.9 11.0 %fusion.2 = f32[768,640,8]{1,2,0:T(8,128)} fusion(bf16[768,8,640]{2,1,0:T(8,128)(2,1)} %collective-permute-done.1, bf16[32,32]{1,0:T(8,128)(2,1)S(1)} %copy-done.4, s32[]{:T(128)S(6)} %select_n.42, s32[]{:T(128)S(6)} %select_n.48), kind=kOutput, calls=%fused_computation.7 | convolution fusion | flops 62914560 | bytes 23595016 | tf_op jit(solution)/shard_map/ij,ajp->aip/dot_general | solution.py:29
  250.9 23.8 %collective-permute-done.2 = bf16[768,8,640]{2,1,0:T(8,128)(2,1)} collective-permute-done((bf16[768,8,640]{2,1,0:T(8,128)(2,1)}, bf16[768,8,640]{2,1,0:T(8,128)(2,1)}, u32[]{:S(2)}, u32[]{:S(2)}) %collective-permute-start.2) | collective-permute-done | bytes 7864352 | tf_op jit(solution)/shard_map/ppermute | solution.py:11
  274.7 26.0 %fusion = bf16[768,8,640]{2,1,0:T(8,128)(2,1)} fusion(f32[768,640,8]{1,2,0:T(8,128)} %fusion.2, f32[768,640,8]{1,2,0:T(8,128)} %fusion.4, f32[768,8,640]{2,1,0:T(8,128)} %copy.5, f32[768,640,8]{1,2,0:T(8,128)} %fusion.6, bf16[768,8,640]{2,1,0:T(8,128)(2,1)} %collective-permute-done.2, bf16[32,32]{1,0:T(8,128)(2,1)S(1)} %copy-done.4, s32[]{:T(128)S(6)} %select_n.42, ...), kind=kOutput, calls=%fused_computation.1 | convolution fusion | flops 82575360 | bytes 78645256 | tf_op jit(solution)/shard_map/ij,ajp->aip/dot_general | solution.py:29
  300.8 101.2 %all_to_all.18 = bf16[768,8,640]{2,1,0:T(8,128)(2,1)S(1)} all-to-all(bf16[768,8,640]{2,1,0:T(8,128)(2,1)} %fusion), channel_id=1, replica_groups=mesh['occ'=4,'aux'=32] {'aux'}, dimensions={0} | all-to-all | bytes 15728640 | tf_op jit(solution)/shard_map/all_to_all | solution.py:44
  401.9 0.0 copy-start.1
  401.9 4.4 %copy.6 = bf16[24,8,32,640]{3,1,2,0:T(8,128)(2,1)} copy(bf16[24,8,32,640]{3,1,0,2:T(8,128)(2,1)S(1)} %bitcast.48) | data formatting | bytes 15728640 | tf_op jit(solution)/shard_map/all_to_all | solution.py:44
  406.3 0.0 copy-done.1
Async XLA Ops:
  0.0 192.3 %copy-start = (bf16[768,768]{1,0:T(8,128)(2,1)S(1)}, bf16[768,768]{1,0:T(8,128)(2,1)}, u32[]{:S(2)}) copy-start(bf16[768,768]{1,0:T(8,128)(2,1)} %param.7) | copy-start | bytes 3538948
  6.2 3.1 copy-start.2
  9.3 87.3 %collective-permute-start = (bf16[768,8,640]{2,1,0:T(8,128)(2,1)S(1)}, bf16[768,8,640]{2,1,0:T(8,128)(2,1)S(1)}, u32[]{:S(2)}, u32[]{:S(2)}) collective-permute-start(bf16[768,8,640]{2,1,0:T(8,128)(2,1)S(1)} %broadcast_multiply_fusion), channel_id=1, source_target_pairs={{0,32},{32,64},{64,96},{96,0},{1,33},{33,65},{65,97},{97,1},{2,34}... | collective-permute-start | bytes 23592968 | tf_op jit(solution)/shard_map/ppermute | solution.py:11
  96.6 3.2 copy-start.3
  99.8 87.4 %collective-permute-start.1 = (bf16[768,8,640]{2,1,0:T(8,128)(2,1)S(1)}, bf16[768,8,640]{2,1,0:T(8,128)(2,1)}, u32[]{:S(2)}, u32[]{:S(2)}) collective-permute-start(bf16[768,8,640]{2,1,0:T(8,128)(2,1)S(1)} %collective-permute-done), channel_id=1, source_target_pairs={{0,32},{32,64},{64,96},{96,0},{1,33},{33,65},{65,97},{97,1},{2,34}... | collective-permute-start | bytes 23592968 | tf_op jit(solution)/shard_map/ppermute | solution.py:11
  187.2 87.6 %collective-permute-start.2 = (bf16[768,8,640]{2,1,0:T(8,128)(2,1)}, bf16[768,8,640]{2,1,0:T(8,128)(2,1)}, u32[]{:S(2)}, u32[]{:S(2)}) collective-permute-start(bf16[768,8,640]{2,1,0:T(8,128)(2,1)} %collective-permute-done.1), channel_id=1, source_target_pairs={{0,32},{32,64},{64,96},{96,0},{1,33},{33,65},{65,97},{97,1},{2,34}... | collective-permute-start | bytes 23592968 | tf_op jit(solution)/shard_map/ppermute | solution.py:11
  202.2 15.9 %copy-start.4 = (bf16[32,32]{1,0:T(8,128)(2,1)S(1)}, bf16[32,32]{1,0:T(8,128)(2,1)}, u32[]{:S(2)}) copy-start(bf16[32,32]{1,0:T(8,128)(2,1)} %param.6) | copy-start | bytes 6148
  401.9 4.4 %copy-start.1 = (bf16[768,768]{1,0:T(8,128)(2,1)S(1)}, bf16[768,768]{1,0:T(8,128)(2,1)}, u32[]{:S(2)}) copy-start(bf16[768,768]{1,0:T(8,128)(2,1)} %param.7) | copy-start | bytes 3538948
where the time goes:
time: 408 us; the launch traced here: 406 us
  waiting for transfers between devices  198 us (49%)
  blocking collectives  101 us (25%)
  matrix products  68.8 us (17%)
  local copies, waits for them, and re-layouts  31.8 us (8%)
  other arithmetic  6.09 us (1%)
    ppermute x3, waiting for transfers between devices, from_behind(): lax.ppermute(shard, axis, [(i, (i + by) % peers) for i in range(peers)])  198 us
    all_to_all x1, blocking collectives, local(): lax.all_to_all(gamma_local, 'aux', split_axis=0, concat_axis=2, tiled=True)  101 us
    dot_general x4, matrix products, occupied_term(): jnp.einsum('ij,ajp->aip', density_cols, slab_block, preferred_element_typ...  58.9 us
    reshape x1, local copies, waits for them, and re-layouts, local(): total.reshape(virt_count, occ_rows, aux_cols)  15.9 us
    unnamed x11, local copies, waits for them, and re-layouts  11.4 us
    dot_general x1, matrix products, local(): jnp.dot(virt_density, own_block.reshape(virt_count, occ_rows * aux_cols),...  9.89 us
  transfers between devices with their start and end apart: 3, of which 3 were waited for; matrix products, arithmetic and copies ran while one was open for 16% of the time, Pallas kernels for 0%

commit v1 on v0

v1 whole, which is shorter than its diff:
```python
import jax
import jax.numpy as jnp
from jax import lax
from jax.experimental import pallas as pl
from jax.experimental.pallas import tpu as pltpu
from jax.sharding import PartitionSpec as P

VT = 6
CAP = 4
OCC = 8
SLABS = 4
FLIPS = (0, 2, 1, 3)
LANES = 128
GROUP = 32
ROWS = GROUP * OCC
FINE = 16
FROWS = FINE * OCC
HALVES = 2
INNER = 4
VMEM = 60 << 20


def iota(shape, dim):
    return lax.broadcasted_iota(jnp.int32, shape, dim)


def one_hot(condition):
    return jnp.where(condition, 1.0, 0.0).astype(jnp.bfloat16)


def dot(left, right):
    return jnp.dot(left, right, preferred_element_type=jnp.float32)


def permutation(back):
    shape = (ROWS, ROWS)
    fine, coarse = (iota(shape, 1), iota(shape, 0)) if back else (iota(shape, 0), iota(shape, 1))
    return one_hot((fine % GROUP == coarse // OCC) & (fine // GROUP == coarse % OCC))


def tile_of(mask_ref, slab, q):
    seen, tile = 0, 0
    for t in range(VT):
        seen = seen + mask_ref[slab, t]
        tile = tile + (seen <= q).astype(jnp.int32)
    return jnp.minimum(tile, VT - 1)


def transpose_rows(perm, columns):
    y = dot(perm, jnp.concatenate(columns, axis=1)).astype(jnp.bfloat16)
    return y[:, :LANES], y[:, LANES:]


def pack_rows(perm, x_ref, outs, first):
    for g in range(0, x_ref.shape[0] // GROUP, 2):
        for c, out in enumerate(outs):
            cols = slice((first + c) * LANES, (first + c + 1) * LANES)
            pair = transpose_rows(perm, [
                x_ref[n * GROUP:(n + 1) * GROUP, :, cols].reshape(ROWS, LANES) for n in (g, g + 1)
            ])
            for n in range(2):
                at = (g + n) * GROUP
                out[:, at:at + GROUP, :] = pair[n].reshape(OCC, GROUP, LANES)


def first_body(mask_ref, ids_ref, x_ref, out):
    pack_rows(permutation(False), x_ref, [out], 0)


def first_pack(mask, ids, three_index):
    tile = three_index.shape[0] // VT
    return pl.pallas_call(
        first_body,
        out_shape=jax.ShapeDtypeStruct((OCC, CAP * tile, LANES), jnp.bfloat16),
        grid_spec=pltpu.PrefetchScalarGridSpec(
            num_scalar_prefetch=2,
            grid=(CAP,),
            in_specs=[
                pl.BlockSpec((tile, OCC, LANES), lambda q, mask, ids: (tile_of(mask, ids[0], q), 0, 0)),
            ],
            out_specs=pl.BlockSpec((OCC, tile, LANES), lambda q, mask, ids: (0, q, 0)),
        ),
        compiler_params=pltpu.CompilerParams(vmem_limit_bytes=VMEM),
        cost_estimate=pl.CostEstimate(flops=1 << 29, bytes_accessed=2 << 20, transcendentals=0),
    )(mask, ids, three_index)


def rest_body(mask_ref, ids_ref, x_ref, v0_ref, v1_ref, d_ref, virt_out, occ_out, table_out, *outs):
    q = pl.program_id(0)
    own = ids_ref[0]
    pack_rows(permutation(False), x_ref, outs, 1)
    for which, v_ref in enumerate((v0_ref, v1_ref)):
        count = 0
        for t in range(VT):
            count = count + mask_ref[own ^ FLIPS[which], t]
        part = v_ref[...].reshape(-1, x_ref.shape[0])
        virt_out[which] = jnp.where(q < count, part, jnp.zeros_like(part))

    @pl.when(q == 0)
    def _():
        tile = x_ref.shape[0]
        for s in range(SLABS):
            seen = 0
            for t in range(VT):
                here = mask_ref[own ^ FLIPS[s], t]
                table_out[s, t] = jnp.where(here > 0, seen * tile, -1)
                seen = seen + here
        width = SLABS * FROWS
        shape = (SLABS * OCC, width)
        col = iota(shape, 1)
        slab = col // FROWS
        source = own
        for s in range(1, SLABS):
            source = jnp.where(slab == s, own ^ FLIPS[s], source)
        pick_cols = one_hot(iota(shape, 0) == source * OCC + col % FROWS // FINE)
        spread = dot(d_ref[...], pick_cols).astype(jnp.bfloat16)
        shape = (FROWS, SLABS * OCC)
        full = (FROWS, width)
        same = iota(full, 0) % FINE == iota(full, 1) % FINE
        for which in range(2):
            pick_rows = one_hot(iota(shape, 1) == (own ^ FLIPS[which]) * OCC + iota(shape, 0) // FINE)
            occ_out[which] = jnp.where(same, dot(pick_rows, spread), 0.0).astype(jnp.bfloat16)


def rest_pack(mask, ids, three_index, by_half, occ_density):
    virt_count, _, cols = three_index.shape
    tile = virt_count // VT
    blocks, _, span, _ = by_half.shape
    half_rows = blocks * span
    count = cols // LANES - 1

    def half_block(which):
        def index(q, mask, ids):
            half = ids[1] if which == 0 else 1 - ids[1]
            return 0, half, 0, tile_of(mask, ids[0] ^ FLIPS[which], q)
        return pl.BlockSpec((blocks, 1, span, tile), index)

    virt, occ, table, *packs = pl.pallas_call(
        rest_body,
        out_shape=[
            jax.ShapeDtypeStruct((2, half_rows, CAP * tile), jnp.bfloat16),
            jax.ShapeDtypeStruct((2, FROWS, SLABS * FROWS), jnp.bfloat16),
            jax.ShapeDtypeStruct((SLABS, VT), jnp.int32),
        ] + [jax.ShapeDtypeStruct((OCC, CAP * tile, LANES), jnp.bfloat16)] * count,
        grid_spec=pltpu.PrefetchScalarGridSpec(
            num_scalar_prefetch=2,
            grid=(CAP,),
            in_specs=[
                pl.BlockSpec((tile, OCC, cols), lambda q, mask, ids: (tile_of(mask, ids[0], q), 0, 0)),
                half_block(0),
                half_block(1),
                pl.BlockSpec(occ_density.shape, lambda q, mask, ids: (0, 0)),
            ],
            out_specs=[
                pl.BlockSpec((2, half_rows, tile), lambda q, mask, ids: (0, 0, q)),
                pl.BlockSpec((2, FROWS, SLABS * FROWS), lambda q, mask, ids: (0, 0, 0)),
                pl.BlockSpec(memory_space=pltpu.SMEM),
            ] + [pl.BlockSpec((OCC, tile, LANES), lambda q, mask, ids: (0, q, 0))] * count,
        ),
        compiler_params=pltpu.CompilerParams(vmem_limit_bytes=VMEM),
        cost_estimate=pl.CostEstimate(flops=3 << 30, bytes_accessed=12 << 20, transcendentals=0),
    )(mask, ids, three_index, by_half, by_half, occ_density)
    return packs, virt, occ, table


def density_body(table_ref, ids_ref, x0, x1, x2, x3, virt_in, occ_in, out, packs, virt_ref, occ_ref, total, mixed, result, in_sems, out_sems):
    depth = x0.shape[1]
    half_rows = virt_ref.shape[1]
    blocks = out.shape[0] // (INNER * HALVES * OCC * 24)
    span = half_rows // blocks
    tile = depth // CAP
    targets = [packs.at[s, :, pl.ds(0, depth), :] for s in range(SLABS)] + [virt_ref, occ_ref]
    arrivals = [
        pltpu.make_async_copy(ref, target, in_sems.at[n])
        for n, (ref, target) in enumerate(zip((x0, x1, x2, x3, virt_in, occ_in), targets))
    ]
    for n in (0, 4, 1, 2, 3, 5):
        arrivals[n].start()
    for s in range(SLABS):
        packs[s, :, depth:depth + FINE, :] = jnp.zeros((OCC, FINE, LANES), jnp.bfloat16)
    perm = permutation(True)
    arrivals[4].wait()
    for which in range(2):
        arrivals[which].wait()
        for i in range(0, OCC, 2):
            both = jnp.concatenate([packs[which, i, :depth], packs[which, i + 1, :depth]], axis=1)
            y = dot(virt_ref[which], both)
            total[which, i] = y[:, :LANES]
            total[which, i + 1] = y[:, LANES:]
    for n in (2, 3, 5):
        arrivals[n].wait()
    departures = []
    for which in range(2):
        half = ids_ref[1] if which == 0 else 1 - ids_ref[1]
        for first in range(0, half_rows, 2 * FINE):
            columns, added = [], []
            for row in (first, first + FINE):
                start = row // span * (HALVES * span) + row % span + half * span
                parts = []
                for s in range(SLABS):
                    base = table_ref[s, start // tile]
                    at = pl.multiple_of(jnp.where(base < 0, depth, base + start % tile), FINE)
                    parts.append(packs[s, :, pl.ds(at, FINE), :].reshape(FROWS, LANES))
                columns.append(jnp.concatenate(parts, axis=0))
                added.append(total[which, :, row:row + FINE, :].reshape(FROWS, LANES))
            y = dot(occ_ref[which], jnp.concatenate(columns, axis=1))
            y = (y + jnp.concatenate(added, axis=1)).astype(jnp.bfloat16)
            for n in range(2):
                row = first + n * FINE
                mixed[which, :, row:row + FINE, :] = y[:, n * LANES:(n + 1) * LANES].reshape(OCC, FINE, LANES)
        for first in range(0, half_rows, 2 * GROUP):
            pair = transpose_rows(perm, [
                mixed[which, :, row:row + GROUP, :].reshape(ROWS, LANES) for row in (first, first + GROUP)
            ])
            for n in range(2):
                at = (first + n * GROUP) * OCC
                result[which, at:at + ROWS, :] = pair[n]
        for b in range(blocks):
            start = pl.multiple_of((b * HALVES + half) * span * OCC, span * OCC)
            copy = pltpu.make_async_copy(
                result.at[which, pl.ds(b * span * OCC, span * OCC), :],
                out.at[pl.ds(start, span * OCC), :],
                out_sems.at[which * blocks + b],
            )
            copy.start()
            departures.append(copy)
    for copy in departures:
        copy.wait()


def density(table, ids, packs, virt, occ):
    depth = packs[0].shape[1]
    half_rows = virt.shape[1]
    rows = 2 * half_rows * OCC
    blocks = rows // (INNER * HALVES * OCC * 24)
    return pl.pallas_call(
        density_body,
        out_shape=jax.ShapeDtypeStruct((rows, LANES), jnp.bfloat16),
        grid_spec=pltpu.PrefetchScalarGridSpec(
            num_scalar_prefetch=2,
            grid=(1,),
            in_specs=[pl.BlockSpec(memory_space=pl.ANY)] * SLABS + [pl.BlockSpec(memory_space=pltpu.HBM)] * 2,
            out_specs=pl.BlockSpec(memory_space=pl.ANY),
            scratch_shapes=[
                pltpu.VMEM((SLABS, OCC, depth + FINE, LANES), jnp.bfloat16),
                pltpu.VMEM(virt.shape, jnp.bfloat16),
                pltpu.VMEM(occ.shape, jnp.bfloat16),
                pltpu.VMEM((2, OCC, half_rows, LANES), jnp.float32),
                pltpu.VMEM((2, OCC, half_rows, LANES), jnp.bfloat16),
                pltpu.VMEM((2, half_rows * OCC, LANES), jnp.bfloat16),
                pltpu.SemaphoreType.DMA((SLABS + 2,)),
                pltpu.SemaphoreType.DMA((2 * blocks,)),
            ],
        ),
        compiler_params=pltpu.CompilerParams(vmem_limit_bytes=24 << 20),
        cost_estimate=pl.CostEstimate(
            flops=2 * LANES * (rows * depth + 3 * rows * ROWS),
            bytes_accessed=2 * LANES * (rows + SLABS * OCC * depth),
            transcendentals=0,
        ),
    )(table, ids, *packs, virt, occ)


def assemble_body(*refs):
    count = len(refs) - 5
    ins, out = refs[:count], refs[count]
    arrived, whole, in_sems, out_sems = refs[count + 1:]
    rows = out.shape[0]
    peers = ins[0].shape[0] // rows
    cols = out.shape[2] // peers
    step = peers // out_sems.shape[0]
    arrivals = [pltpu.make_async_copy(ref, arrived.at[k], in_sems.at[k]) for k, ref in enumerate(ins)]
    for copy in arrivals:
        copy.start()

    def take(k, m):
        whole[:, :, m * cols + k * LANES:m * cols + (k + 1) * LANES] = arrived[k, m * rows:(m + 1) * rows]

    for k in range(count - 1):
        arrivals[k].wait()
        for m in range(peers):
            take(k, m)
    arrivals[-1].wait()
    departures = []
    for n in range(peers // step):
        for m in range(n * step, (n + 1) * step):
            take(count - 1, m)
        part = pl.ds(n * step * cols, step * cols)
        copy = pltpu.make_async_copy(whole.at[:, :, part], out.at[:, :, part], out_sems.at[n])
        copy.start()
        departures.append(copy)
    for copy in departures:
        copy.wait()


def assemble(parts, peers):
    rows = parts[0].shape[0] // peers
    shape = (rows, OCC, peers * len(parts) * LANES)
    return pl.pallas_call(
        assemble_body,
        out_shape=jax.ShapeDtypeStruct(shape, jnp.bfloat16),
        in_specs=[pl.BlockSpec(memory_space=pl.ANY)] * len(parts),
        out_specs=pl.BlockSpec(memory_space=pl.ANY),
        scratch_shapes=[
            pltpu.VMEM((len(parts),) + parts[0].shape, jnp.bfloat16),
            pltpu.VMEM(shape, jnp.bfloat16),
            pltpu.SemaphoreType.DMA((len(parts),)),
            pltpu.SemaphoreType.DMA((8,)),
        ],
        compiler_params=pltpu.CompilerParams(vmem_limit_bytes=VMEM),
        cost_estimate=pl.CostEstimate(
            flops=0, bytes_accessed=4 * rows * OCC * shape[2], transcendentals=0
        ),
    )(*parts)


def exchange_groups(peers):
    groups = []
    for parity in range(2):
        for core in range(2):
            groups.append([
                (2 * (((k // INNER) % HALVES) ^ parity) + core) * peers + k for k in range(peers)
            ])
    return groups


def local(three_index, tile_mask, occ_density, virt_density):
    virt_count = three_index.shape[0]
    peers = lax.axis_size("aux")
    own = lax.axis_index("occ")
    my_half = (lax.axis_index("aux") // INNER) % HALVES
    ids = jnp.stack([own, my_half]).astype(jnp.int32)
    by_half = virt_density.reshape(peers // (HALVES * INNER), HALVES, -1, virt_count)

    head = first_pack(tile_mask, ids, three_index)
    others, *weights = rest_pack(tile_mask, ids, three_index, by_half, occ_density)
    virt, occ, table = (pltpu.with_memory_space_constraint(array, pltpu.HBM) for array in weights)
    mine = [head] + others

    chip_pairs = [(s, s ^ 2) for s in range(SLABS)]
    core_pairs = [(s, s ^ 1) for s in range(SLABS)]
    groups = exchange_groups(peers)
    done, acrosses = [], []
    for k, part in enumerate(mine):
        sent = part
        if k >= 2:
            sent, _ = lax.optimization_barrier((part, acrosses[k - 2]))
        across = lax.ppermute(sent, "occ", chip_pairs)
        across, _ = lax.optimization_barrier((across, gamma if k else mine[1]))
        acrosses.append(across)
        beside = lax.ppermute(part, "occ", core_pairs)
        diagonal = lax.ppermute(across, "occ", core_pairs)
        gamma = density(table, ids, (part, across, beside, diagonal), virt, occ)
        gamma = gamma.reshape(virt_count, OCC, -1)
        done.append(lax.all_to_all(
            gamma, ("occ", "aux"), split_axis=0, concat_axis=0, axis_index_groups=groups, tiled=True
        ))
    return assemble(done, peers)


def solution(mesh):
    return jax.shard_map(
        local,
        mesh=mesh,
        in_specs=(P(None, "occ", "aux"), P(), P(), P()),
        out_specs=P("aux", "occ", None),
        check_vma=False,
    )
```

time: 408 us -> 188 us (0.46)
  waiting for transfers between devices: 198 us -> 76.3 us
  blocking collectives: 101 us -> 24.9 us
  matrix products: 68.8 us -> 0 us
  Pallas kernels: 0 us -> 47.6 us
  starting transfers between devices: 0.01 us -> 36.1 us
  local copies, waits for them, and re-layouts: 31.8 us -> 0.02 us
  other arithmetic: 6.09 us -> 0.61 us
    ppermute x3 -> x15, waiting for transfers between devices: 198 us -> 35.7 us  [the longest x5 26.9 us: local(): across = lax.ppermute(sent, 'occ', chip_pairs)]
    all_to_all x1, blocking collectives: 101 us -> 24.9 us  [local(): lax.all_to_all(gamma, ('occ', 'aux'), split_axis=0, concat_axis=0, axis_i...]
    dot_general x5 -> x0, matrix products: 68.8 us -> none  [the longest x4 58.9 us: occupied_term(): jnp.einsum('ij,ajp->aip', density_cols, slab_block, preferred_element_typ...]
    pallas_call x0 -> x8, Pallas kernels: none -> 47.6 us  [the longest x5 30.4 us: density(): pl.pallas_call(density_body, out_shape=jax.ShapeDtypeStruct((rows, LANES)...]
    all_to_all x0 -> x4, waiting for transfers between devices: none -> 40.6 us  [local(): lax.all_to_all(gamma, ('occ', 'aux'), split_axis=0, concat_axis=0, axis_i...]
    all_to_all x0 -> x4, starting transfers between devices: none -> 26.1 us  [local(): lax.all_to_all(gamma, ('occ', 'aux'), split_axis=0, concat_axis=0, axis_i...]
    reshape x1 -> x0, local copies, waits for them, and re-layouts: 15.9 us -> none  [local(): total.reshape(virt_count, occ_rows, aux_cols)]
    unnamed x11 -> x12, local copies, waits for them, and re-layouts: 11.4 us -> 0.02 us
  transfers between devices with their start and end apart: 3 -> 19, of which waited for: 3 -> 16; matrix products, arithmetic and copies ran while one was open for 16% -> 0% of each run, Pallas kernels for 0% -> 20%
where the time goes in v1:
time: 188 us; the launch traced here: 186 us
  waiting for transfers between devices  76.3 us (41%)
  Pallas kernels  47.6 us (25%)
  starting transfers between devices  36.1 us (19%)
  blocking collectives  24.9 us (13%)
    all_to_all x4, waiting for transfers between devices, local(): lax.all_to_all(gamma, ('occ', 'aux'), split_axis=0, concat_axis=0, axis_i...  40.6 us
    pallas_call x5, Pallas kernels, density(): pl.pallas_call(density_body, out_shape=jax.ShapeDtypeStruct((rows, LANES)...  30.4 us
    ppermute x5, waiting for transfers between devices, local(): across = lax.ppermute(sent, 'occ', chip_pairs)  26.9 us
    all_to_all x4, starting transfers between devices, local(): lax.all_to_all(gamma, ('occ', 'aux'), split_axis=0, concat_axis=0, axis_i...  26.1 us
    all_to_all x1, blocking collectives, local(): lax.all_to_all(gamma, ('occ', 'aux'), split_axis=0, concat_axis=0, axis_i...  24.9 us
    ppermute x5, starting transfers between devices, local(): across = lax.ppermute(sent, 'occ', chip_pairs)  9.56 us
    pallas_call x1, Pallas kernels, rest_pack(): pl.pallas_call(rest_body, out_shape=[jax.ShapeDtypeStruct((2, half_rows,...  6.69 us
    pallas_call x1, Pallas kernels, assemble(): pl.pallas_call(assemble_body, out_shape=jax.ShapeDtypeStruct(shape, jnp.b...  6.6 us
  transfers between devices with their start and end apart: 19, of which 16 were waited for; matrix products, arithmetic and copies ran while one was open for 0% of the time, Pallas kernels for 20%

profile of v1, /device:TPU:2, one launch (start us, length us, event | category | flops | bytes accessed | tf_op | source)
XLA Modules:
  0.0 185.9 jit_solution(2932425380988305972)
XLA Ops:
  0.0 0.6 pad_add_fusion.ids_ref
  0.6 3.9 %shard_map.47.x0 = bf16[8,512,128]{2,1,0:T(8,128)(2,1)} custom-call(s32[4,6]{1,0:T(4,128)} %mask_ref.3, s32[2]{0:T(128)} %pad_add_fusion.ids_ref, bf16[768,8,640]{2,1,0:T(8,128)(2,1)} %x_ref.3), custom_call_target="tpu_custom_call" | custom-call | flops 536870912 | bytes 2097152 | tf_op jit(solution)/shard_map/pallas_call | solution.py:72
  4.5 2.6 %collective-permute-start = (bf16[8,512,128]{2,1,0:T(8,128)(2,1)}, bf16[8,512,128]{2,1,0:T(8,128)(2,1)S(1)}, u32[]{:S(2)}, u32[]{:S(2)}) collective-permute-start(bf16[8,512,128]{2,1,0:T(8,128)(2,1)} %shard_map.47.x0), channel_id=1, source_target_pairs={{0,64},{32,96},{64,0},{96,32},{1,65},{33,97},{65,1},{97,33},{2,66}... | collective-permute-start | bytes 3145736 | tf_op jit(solution)/shard_map/ppermute | solution.py:348
  7.1 0.0 collective-permute-start.1
  7.1 6.7 %shard_map.46 = (bf16[2,384,512]{2,1,0:T(8,128)(2,1)}, bf16[2,128,512]{2,1,0:T(8,128)(2,1)}, s32[4,6]{1,0:T(4,128)}, bf16[8,512,128]{2,1,0:T(8,128)(2,1)}, bf16[...) custom-call(s32[4,6]{1,0:T(4,128)} %mask_ref.3, s32[2]{0:T(128)} %pad_add_fusion.ids_ref, ...), custom_call_target="tpu_custom_call" | custom-call | flops 3221225472 | bytes 12582912 | tf_op jit(solution)/shard_map/pallas_call | solution.py:138
  13.8 16.7 %collective-permute-done.x1 = bf16[8,512,128]{2,1,0:T(8,128)(2,1)S(1)} collective-permute-done((bf16[8,512,128]{2,1,0:T(8,128)(2,1)}, bf16[8,512,128]{2,1,0:T(8,128)(2,1)S(1)}, u32[]{:S(2)}, u32[]{:S(2)}) %collective-permute-start) | collective-permute-done | bytes 1048608 | tf_op jit(solution)/shard_map/ppermute | solution.py:348
  30.4 0.0 collective-permute-start.2
  30.4 1.7 collective-permute-start.3
  32.2 0.0 collective-permute-done.1.x2
  32.2 0.9 collective-permute-done.2.x3
  33.1 5.8 %shard_map.48 = bf16[6144,128]{1,0:T(8,128)(2,1)} custom-call(s32[4,6]{1,0:T(4,128)} %get-tuple-element.20.table_ref, s32[2]{0:T(128)S(1)} %copy-done.1, bf16[8,512,128]{2,1,0:T(8,128)(2,1)S(1)} %copy-done, bf16[8,512,128]{2,1,0:T(8,128)(2,1)S(1)} %collective-permute-done.x1, bf16[8,512,128]{2,1,0:T(8,128)(2,1)S(1)} %collective-permute-done.1.x2, ...), custom_call_target="tpu_custom_call" | custom-call | flops 2013265920 | bytes 5767168 | tf_op jit(solution)/shard_map/pallas_call | solution.py:236
  38.9 11.1 %all-to-all-start = ((bf16[768,8,128]{2,1,0:T(8,128)(2,1)}), bf16[768,8,128]{2,1,0:T(8,128)(2,1)}, u32[]{:S(2)}, u32[]{:S(2)}) async-start(bf16[768,8,128]{2,1,0:T(8,128)(2,1)} %bitcast.3), calls=%async_computation | async-start | bytes 3145728 | tf_op jit(solution)/shard_map/all_to_all | solution.py:355
  50.0 0.1 collective-permute-start.4
  50.1 6.2 %collective-permute-done.3.x1 = bf16[8,512,128]{2,1,0:T(8,128)(2,1)} collective-permute-done((bf16[8,512,128]{2,1,0:T(8,128)(2,1)}, bf16[8,512,128]{2,1,0:T(8,128)(2,1)}, u32[]{:S(2)}, u32[]{:S(2)}) %collective-permute-start.3) | collective-permute-done | bytes 1048608 | tf_op jit(solution)/shard_map/ppermute | solution.py:348
  56.3 0.0 collective-permute-start.5
  56.3 1.7 collective-permute-start.6
  58.1 0.0 collective-permute-done.4.x2
  58.1 1.1 collective-permute-done.5.x3
  59.2 5.8 %shard_map.49 = bf16[6144,128]{1,0:T(8,128)(2,1)} custom-call(s32[4,6]{1,0:T(4,128)} %get-tuple-element.20.table_ref, s32[2]{0:T(128)S(1)} %copy-done.1, bf16[8,512,128]{2,1,0:T(8,128)(2,1)S(1)} %copy-done.5, bf16[8,512,128]{2,1,0:T(8,128)(2,1)} %collective-permute-done.3.x1, bf16[8,512,128]{2,1,0:T(8,128)(2,1)S(1)} %collective-permute-done.4.x2, ...), custom_call_target="tpu_custom_call" | custom-call | flops 2013265920 | bytes 5767168 | tf_op jit(solution)/shard_map/pallas_call | solution.py:236
  65.0 9.3 %all-to-all-done.refs_0_ = bf16[768,8,128]{2,1,0:T(8,128)(2,1)} async-done(((bf16[768,8,128]{2,1,0:T(8,128)(2,1)}), bf16[768,8,128]{2,1,0:T(8,128)(2,1)}, u32[]{:S(2)}, u32[]{:S(2)}) %all-to-all-start) | async-done | bytes 1572896 | tf_op jit(solution)/shard_map/all_to_all | solution.py:355
  74.4 4.7 %all-to-all-start.1 = ((bf16[768,8,128]{2,1,0:T(8,128)(2,1)}), bf16[768,8,128]{2,1,0:T(8,128)(2,1)}, u32[]{:S(2)}, u32[]{:S(2)}) async-start(bf16[768,8,128]{2,1,0:T(8,128)(2,1)} %bitcast.4), calls=%async_computation.1 | async-start | bytes 3145728 | tf_op jit(solution)/shard_map/all_to_all | solution.py:355
  79.1 0.1 collective-permute-start.7
  79.1 2.9 %collective-permute-done.6.x1 = bf16[8,512,128]{2,1,0:T(8,128)(2,1)} collective-permute-done((bf16[8,512,128]{2,1,0:T(8,128)(2,1)S(1)}, bf16[8,512,128]{2,1,0:T(8,128)(2,1)}, u32[]{:S(2)}, u32[]{:S(2)}) %collective-permute-start.6) | collective-permute-done | bytes 1048608 | tf_op jit(solution)/shard_map/ppermute | solution.py:348
  82.0 0.0 collective-permute-start.8
  82.0 1.7 collective-permute-start.9
  83.8 0.0 collective-permute-done.7.x2
  83.8 1.1 collective-permute-done.8.x3
  84.9 5.8 %shard_map.50 = bf16[6144,128]{1,0:T(8,128)(2,1)} custom-call(s32[4,6]{1,0:T(4,128)} %get-tuple-element.20.table_ref, s32[2]{0:T(128)S(1)} %copy-done.1, bf16[8,512,128]{2,1,0:T(8,128)(2,1)S(1)} %copy-done.4, bf16[8,512,128]{2,1,0:T(8,128)(2,1)} %collective-permute-done.6.x1, bf16[8,512,128]{2,1,0:T(8,128)(2,1)S(1)} %collective-permute-done.7.x2, ...), custom_call_target="tpu_custom_call" | custom-call | flops 2013265920 | bytes 5767168 | tf_op jit(solution)/shard_map/pallas_call | solution.py:236
  90.7 10.6 %all-to-all-done.1.refs_1_ = bf16[768,8,128]{2,1,0:T(8,128)(2,1)} async-done(((bf16[768,8,128]{2,1,0:T(8,128)(2,1)}), bf16[768,8,128]{2,1,0:T(8,128)(2,1)}, u32[]{:S(2)}, u32[]{:S(2)}) %all-to-all-start.1) | async-done | bytes 1572896 | tf_op jit(solution)/shard_map/all_to_all | solution.py:355
  101.3 5.5 %all-to-all-start.2 = ((bf16[768,8,128]{2,1,0:T(8,128)(2,1)}), bf16[768,8,128]{2,1,0:T(8,128)(2,1)}, u32[]{:S(2)}, u32[]{:S(2)}) async-start(bf16[768,8,128]{2,1,0:T(8,128)(2,1)} %bitcast.5), calls=%async_computation.2 | async-start | bytes 3145728 | tf_op jit(solution)/shard_map/all_to_all | solution.py:355
  106.8 0.1 collective-permute-start.10
  106.9 0.8 collective-permute-done.9.x1
  107.7 0.0 collective-permute-start.11
  107.7 1.7 collective-permute-start.12
  109.4 0.1 collective-permute-done.10.x2
  109.6 1.7 collective-permute-done.11.x3
  111.3 5.8 %shard_map.51 = bf16[6144,128]{1,0:T(8,128)(2,1)} custom-call(s32[4,6]{1,0:T(4,128)} %get-tuple-element.20.table_ref, s32[2]{0:T(128)S(1)} %copy-done.1, bf16[8,512,128]{2,1,0:T(8,128)(2,1)S(1)} %copy-done.3, bf16[8,512,128]{2,1,0:T(8,128)(2,1)} %collective-permute-done.9.x1, bf16[8,512,128]{2,1,0:T(8,128)(2,1)S(1)} %collective-permute-done.10.x2, ...), custom_call_target="tpu_custom_call" | custom-call | flops 2013265920 | bytes 5767168 | tf_op jit(solution)/shard_map/pallas_call | solution.py:236
  117.1 11.0 %all-to-all-done.2.refs_2_ = bf16[768,8,128]{2,1,0:T(8,128)(2,1)} async-done(((bf16[768,8,128]{2,1,0:T(8,128)(2,1)}), bf16[768,8,128]{2,1,0:T(8,128)(2,1)}, u32[]{:S(2)}, u32[]{:S(2)}) %all-to-all-start.2) | async-done | bytes 1572896 | tf_op jit(solution)/shard_map/all_to_all | solution.py:355
  128.1 4.7 %all-to-all-start.3 = ((bf16[768,8,128]{2,1,0:T(8,128)(2,1)}), bf16[768,8,128]{2,1,0:T(8,128)(2,1)}, u32[]{:S(2)}, u32[]{:S(2)}) async-start(bf16[768,8,128]{2,1,0:T(8,128)(2,1)} %bitcast.6), calls=%async_computation.3 | async-start | bytes 3145728 | tf_op jit(solution)/shard_map/all_to_all | solution.py:355
  132.9 0.1 collective-permute-start.13
  133.0 0.4 collective-permute-done.12.x1
  133.4 0.1 collective-permute-start.14
  133.5 2.1 %collective-permute-done.13.x2 = bf16[8,512,128]{2,1,0:T(8,128)(2,1)S(1)} collective-permute-done((bf16[8,512,128]{2,1,0:T(8,128)(2,1)S(1)}, bf16[8,512,128]{2,1,0:T(8,128)(2,1)S(1)}, u32[]{:S(2)}, u32[]{:S(2)}) %collective-permute-start.13) | collective-permute-done | bytes 1048608 | tf_op jit(solution)/shard_map/ppermute | solution.py:351
  135.6 1.7 collective-permute-done.14.x3
  137.3 7.2 %shard_map.52 = bf16[6144,128]{1,0:T(8,128)(2,1)S(1)} custom-call(s32[4,6]{1,0:T(4,128)} %get-tuple-element.20.table_ref, s32[2]{0:T(128)S(1)} %copy-done.1, bf16[8,512,128]{2,1,0:T(8,128)(2,1)S(1)} %copy-done.2, bf16[8,512,128]{2,1,0:T(8,128)(2,1)} %collective-permute-done.12.x1, bf16[8,512,128]{2,1,0:T(8,128)(2,1)S(1)} %collective-permute-done.13.x2, ...), custom_call_target="tpu_custom_call" | custom-call | flops 2013265920 | bytes 5767168 | tf_op jit(solution)/shard_map/pallas_call | solution.py:236
  144.5 9.6 %all-to-all-done.3.refs_3_ = bf16[768,8,128]{2,1,0:T(8,128)(2,1)} async-done(((bf16[768,8,128]{2,1,0:T(8,128)(2,1)}), bf16[768,8,128]{2,1,0:T(8,128)(2,1)}, u32[]{:S(2)}, u32[]{:S(2)}) %all-to-all-start.3) | async-done | bytes 1572896 | tf_op jit(solution)/shard_map/all_to_all | solution.py:355
  154.2 24.9 %all_to_all.25.refs_4_ = bf16[768,8,128]{2,1,0:T(8,128)(2,1)} all-to-all(bf16[768,8,128]{2,1,0:T(8,128)(2,1)S(1)} %bitcast.8), channel_id=1, replica_groups={{0,1,2,3,68,69,70,71,8,9,10,11,76,77,78,79,16,17,18,19,84,85,86,87,24,2..., dimensions={0} | all-to-all | bytes 3145728 | tf_op jit(solution)/shard_map/all_to_all | solution.py:355
  179.1 6.6 %shard_map.53 = bf16[24,8,20480]{2,1,0:T(8,128)(2,1)} custom-call(bf16[768,8,128]{2,1,0:T(8,128)(2,1)} %all-to-all-done.refs_0_, bf16[768,8,128]{2,1,0:T(8,128)(2,1)} %all-to-all-done.1.refs_1_, bf16[768,8,128]{2,1,0:T(8,128)(2,1)} %all-to-all-done.2.refs_2_, bf16[768,8,128]{2,1,0:T(8,128)(2,1)} %all-to-all-done.3.refs_3_, ...), custom_call_target="tpu_custom_call" | custom-call | bytes 15728640 | tf_op jit(solution)/shard_map/pallas_call | solution.py:299
  (12 shorter events, 0.0 us)
Async XLA Ops:
  4.5 26.0 %collective-permute-start = (bf16[8,512,128]{2,1,0:T(8,128)(2,1)}, bf16[8,512,128]{2,1,0:T(8,128)(2,1)S(1)}, u32[]{:S(2)}, u32[]{:S(2)}) collective-permute-start(bf16[8,512,128]{2,1,0:T(8,128)(2,1)} %shard_map.47.x0), channel_id=1, source_target_pairs={{0,64},{32,96},{64,0},{96,32},{1,65},{33,97},{65,1},{97,33},{2,66}... | collective-permute-start | bytes 3145736 | tf_op jit(solution)/shard_map/ppermute | solution.py:348
  7.1 25.1 %collective-permute-start.1 = (bf16[8,512,128]{2,1,0:T(8,128)(2,1)}, bf16[8,512,128]{2,1,0:T(8,128)(2,1)S(1)}, u32[]{:S(2)}, u32[]{:S(2)}) collective-permute-start(bf16[8,512,128]{2,1,0:T(8,128)(2,1)} %shard_map.47.x0), channel_id=1, source_target_pairs={{0,32},{32,0},{64,96},{96,64},{1,33},{33,1},{65,97},{97,65},{2,34}... | collective-permute-start | bytes 3145736 | tf_op jit(solution)/shard_map/ppermute | solution.py:351
  7.1 26.0 %copy-start = (bf16[8,512,128]{2,1,0:T(8,128)(2,1)S(1)}, bf16[8,512,128]{2,1,0:T(8,128)(2,1)}, u32[]{:S(2)}) copy-start(bf16[8,512,128]{2,1,0:T(8,128)(2,1)} %shard_map.47.x0) | copy-start | bytes 3145732
  7.1 26.0 %copy-start.1 = (s32[2]{0:T(128)S(1)}, s32[2]{0:T(128)}, u32[]{:S(2)}) copy-start(s32[2]{0:T(128)} %pad_add_fusion.ids_ref) | copy-start | bytes 28
  30.4 2.7 %collective-permute-start.2 = (bf16[8,512,128]{2,1,0:T(8,128)(2,1)S(1)}, bf16[8,512,128]{2,1,0:T(8,128)(2,1)S(1)}, u32[]{:S(2)}, u32[]{:S(2)}) collective-permute-start(bf16[8,512,128]{2,1,0:T(8,128)(2,1)S(1)} %collective-permute-done.x1), channel_id=1, source_target_pairs={{0,32},{32,0},{64,96},{96,64},{1,33},{33,1},{65,97},{97,65},{2,34}... | collective-permute-start | bytes 3145736 | tf_op jit(solution)/shard_map/ppermute | solution.py:352
  30.4 25.9 %collective-permute-start.3 = (bf16[8,512,128]{2,1,0:T(8,128)(2,1)}, bf16[8,512,128]{2,1,0:T(8,128)(2,1)}, u32[]{:S(2)}, u32[]{:S(2)}) collective-permute-start(bf16[8,512,128]{2,1,0:T(8,128)(2,1)} %get-tuple-element.21.x0), channel_id=1, source_target_pairs={{0,64},{32,96},{64,0},{96,32},{1,65},{33,97},{65,1},{97,33},{2,66}... | collective-permute-start | bytes 3145736 | tf_op jit(solution)/shard_map/ppermute | solution.py:348
  38.9 11.1 %copy-start.5 = (bf16[8,512,128]{2,1,0:T(8,128)(2,1)S(1)}, bf16[8,512,128]{2,1,0:T(8,128)(2,1)}, u32[]{:S(2)}) copy-start(bf16[8,512,128]{2,1,0:T(8,128)(2,1)} %get-tuple-element.21.x0) | copy-start | bytes 3145732
  38.9 17.4 %copy-start.4 = (bf16[8,512,128]{2,1,0:T(8,128)(2,1)S(1)}, bf16[8,512,128]{2,1,0:T(8,128)(2,1)}, u32[]{:S(2)}) copy-start(bf16[8,512,128]{2,1,0:T(8,128)(2,1)} %get-tuple-element.27.x0) | copy-start | bytes 3145732
  38.9 35.4 %all-to-all-start = ((bf16[768,8,128]{2,1,0:T(8,128)(2,1)}), bf16[768,8,128]{2,1,0:T(8,128)(2,1)}, u32[]{:S(2)}, u32[]{:S(2)}) async-start(bf16[768,8,128]{2,1,0:T(8,128)(2,1)} %bitcast.3), calls=%async_computation | async-start | bytes 3145728 | tf_op jit(solution)/shard_map/all_to_all | solution.py:355
  50.0 8.0 %collective-permute-start.4 = (bf16[8,512,128]{2,1,0:T(8,128)(2,1)S(1)}, bf16[8,512,128]{2,1,0:T(8,128)(2,1)S(1)}, u32[]{:S(2)}, u32[]{:S(2)}) collective-permute-start(bf16[8,512,128]{2,1,0:T(8,128)(2,1)S(1)} %copy-done.5), channel_id=1, source_target_pairs={{0,32},{32,0},{64,96},{96,64},{1,33},{33,1},{65,97},{97,65},{2,34}... | collective-permute-start | bytes 3145736 | tf_op jit(solution)/shard_map/ppermute | solution.py:351
  56.3 2.9 %collective-permute-start.5 = (bf16[8,512,128]{2,1,0:T(8,128)(2,1)}, bf16[8,512,128]{2,1,0:T(8,128)(2,1)S(1)}, u32[]{:S(2)}, u32[]{:S(2)}) collective-permute-start(bf16[8,512,128]{2,1,0:T(8,128)(2,1)} %collective-permute-done.3.x1), channel_id=1, source_target_pairs={{0,32},{32,0},{64,96},{96,64},{1,33},{33,1},{65,97},{97,65},{2,34}... | collective-permute-start | bytes 3145736 | tf_op jit(solution)/shard_map/ppermute | solution.py:352
  56.3 25.7 %collective-permute-start.6 = (bf16[8,512,128]{2,1,0:T(8,128)(2,1)S(1)}, bf16[8,512,128]{2,1,0:T(8,128)(2,1)}, u32[]{:S(2)}, u32[]{:S(2)}) collective-permute-start(bf16[8,512,128]{2,1,0:T(8,128)(2,1)S(1)} %copy-done.4), channel_id=1, source_target_pairs={{0,64},{32,96},{64,0},{96,32},{1,65},{33,97},{65,1},{97,33},{2,66}... | collective-permute-start | bytes 3145736 | tf_op jit(solution)/shard_map/ppermute | solution.py:348
  74.4 7.7 %copy-start.3 = (bf16[8,512,128]{2,1,0:T(8,128)(2,1)S(1)}, bf16[8,512,128]{2,1,0:T(8,128)(2,1)}, u32[]{:S(2)}) copy-start(bf16[8,512,128]{2,1,0:T(8,128)(2,1)} %get-tuple-element.30.x0) | copy-start | bytes 3145732
  74.4 27.0 %all-to-all-start.1 = ((bf16[768,8,128]{2,1,0:T(8,128)(2,1)}), bf16[768,8,128]{2,1,0:T(8,128)(2,1)}, u32[]{:S(2)}, u32[]{:S(2)}) async-start(bf16[768,8,128]{2,1,0:T(8,128)(2,1)} %bitcast.4), calls=%async_computation.1 | async-start | bytes 3145728 | tf_op jit(solution)/shard_map/all_to_all | solution.py:355
  79.1 4.7 %collective-permute-start.7 = (bf16[8,512,128]{2,1,0:T(8,128)(2,1)S(1)}, bf16[8,512,128]{2,1,0:T(8,128)(2,1)S(1)}, u32[]{:S(2)}, u32[]{:S(2)}) collective-permute-start(bf16[8,512,128]{2,1,0:T(8,128)(2,1)S(1)} %copy-done.4), channel_id=1, source_target_pairs={{0,32},{32,0},{64,96},{96,64},{1,33},{33,1},{65,97},{97,65},{2,34}... | collective-permute-start | bytes 3145736 | tf_op jit(solution)/shard_map/ppermute | solution.py:351
  82.0 2.9 %collective-permute-start.8 = (bf16[8,512,128]{2,1,0:T(8,128)(2,1)}, bf16[8,512,128]{2,1,0:T(8,128)(2,1)S(1)}, u32[]{:S(2)}, u32[]{:S(2)}) collective-permute-start(bf16[8,512,128]{2,1,0:T(8,128)(2,1)} %collective-permute-done.6.x1), channel_id=1, source_target_pairs={{0,32},{32,0},{64,96},{96,64},{1,33},{33,1},{65,97},{97,65},{2,34}... | collective-permute-start | bytes 3145736 | tf_op jit(solution)/shard_map/ppermute | solution.py:352
  82.0 25.7 %collective-permute-start.9 = (bf16[8,512,128]{2,1,0:T(8,128)(2,1)S(1)}, bf16[8,512,128]{2,1,0:T(8,128)(2,1)}, u32[]{:S(2)}, u32[]{:S(2)}) collective-permute-start(bf16[8,512,128]{2,1,0:T(8,128)(2,1)S(1)} %copy-done.3), channel_id=1, source_target_pairs={{0,64},{32,96},{64,0},{96,32},{1,65},{33,97},{65,1},{97,33},{2,66}... | collective-permute-start | bytes 3145736 | tf_op jit(solution)/shard_map/ppermute | solution.py:348
  101.3 6.4 %copy-start.2 = (bf16[8,512,128]{2,1,0:T(8,128)(2,1)S(1)}, bf16[8,512,128]{2,1,0:T(8,128)(2,1)}, u32[]{:S(2)}) copy-start(bf16[8,512,128]{2,1,0:T(8,128)(2,1)} %get-tuple-element.33.x0) | copy-start | bytes 3145732
  101.3 26.8 %all-to-all-start.2 = ((bf16[768,8,128]{2,1,0:T(8,128)(2,1)}), bf16[768,8,128]{2,1,0:T(8,128)(2,1)}, u32[]{:S(2)}, u32[]{:S(2)}) async-start(bf16[768,8,128]{2,1,0:T(8,128)(2,1)} %bitcast.5), calls=%async_computation.2 | async-start | bytes 3145728 | tf_op jit(solution)/shard_map/all_to_all | solution.py:355
  106.8 2.7 %collective-permute-start.10 = (bf16[8,512,128]{2,1,0:T(8,128)(2,1)S(1)}, bf16[8,512,128]{2,1,0:T(8,128)(2,1)S(1)}, u32[]{:S(2)}, u32[]{:S(2)}) collective-permute-start(bf16[8,512,128]{2,1,0:T(8,128)(2,1)S(1)} %copy-done.3), channel_id=1, source_target_pairs={{0,32},{32,0},{64,96},{96,64},{1,33},{33,1},{65,97},{97,65},{2,34}... | collective-permute-start | bytes 3145736 | tf_op jit(solution)/shard_map/ppermute | solution.py:351
  107.7 3.6 %collective-permute-start.11 = (bf16[8,512,128]{2,1,0:T(8,128)(2,1)}, bf16[8,512,128]{2,1,0:T(8,128)(2,1)S(1)}, u32[]{:S(2)}, u32[]{:S(2)}) collective-permute-start(bf16[8,512,128]{2,1,0:T(8,128)(2,1)} %collective-permute-done.9.x1), channel_id=1, source_target_pairs={{0,32},{32,0},{64,96},{96,64},{1,33},{33,1},{65,97},{97,65},{2,34}... | collective-permute-start | bytes 3145736 | tf_op jit(solution)/shard_map/ppermute | solution.py:352
  107.7 25.7 %collective-permute-start.12 = (bf16[8,512,128]{2,1,0:T(8,128)(2,1)S(1)}, bf16[8,512,128]{2,1,0:T(8,128)(2,1)}, u32[]{:S(2)}, u32[]{:S(2)}) collective-permute-start(bf16[8,512,128]{2,1,0:T(8,128)(2,1)S(1)} %copy-done.2), channel_id=1, source_target_pairs={{0,64},{32,96},{64,0},{96,32},{1,65},{33,97},{65,1},{97,33},{2,66}... | collective-permute-start | bytes 3145736 | tf_op jit(solution)/shard_map/ppermute | solution.py:348
  128.1 26.0 %all-to-all-start.3 = ((bf16[768,8,128]{2,1,0:T(8,128)(2,1)}), bf16[768,8,128]{2,1,0:T(8,128)(2,1)}, u32[]{:S(2)}, u32[]{:S(2)}) async-start(bf16[768,8,128]{2,1,0:T(8,128)(2,1)} %bitcast.6), calls=%async_computation.3 | async-start | bytes 3145728 | tf_op jit(solution)/shard_map/all_to_all | solution.py:355
  132.9 2.7 %collective-permute-start.13 = (bf16[8,512,128]{2,1,0:T(8,128)(2,1)S(1)}, bf16[8,512,128]{2,1,0:T(8,128)(2,1)S(1)}, u32[]{:S(2)}, u32[]{:S(2)}) collective-permute-start(bf16[8,512,128]{2,1,0:T(8,128)(2,1)S(1)} %copy-done.2), channel_id=1, source_target_pairs={{0,32},{32,0},{64,96},{96,64},{1,33},{33,1},{65,97},{97,65},{2,34}... | collective-permute-start | bytes 3145736 | tf_op jit(solution)/shard_map/ppermute | solution.py:351
  133.4 4.0 %collective-permute-start.14 = (bf16[8,512,128]{2,1,0:T(8,128)(2,1)}, bf16[8,512,128]{2,1,0:T(8,128)(2,1)S(1)}, u32[]{:S(2)}, u32[]{:S(2)}) collective-permute-start(bf16[8,512,128]{2,1,0:T(8,128)(2,1)} %collective-permute-done.12.x1), channel_id=1, source_target_pairs={{0,32},{32,0},{64,96},{96,64},{1,33},{33,1},{65,97},{97,65},{2,34}... | collective-permute-start | bytes 3145736 | tf_op jit(solution)/shard_map/ppermute | solution.py:352

commit v2 on v1

--- a/solution.py
+++ b/solution.py
@@ -1,3 +1,5 @@
+import functools
+
 import jax
 import jax.numpy as jnp
 from jax import lax
@@ -16,6 +18,7 @@
 FINE = 16
 FROWS = FINE * OCC
 HALVES = 2
+SPAN = 96
 INNER = 4
 VMEM = 60 << 20
 
@@ -63,26 +66,46 @@
                 out[:, at:at + GROUP, :] = pair[n].reshape(OCC, GROUP, LANES)
 
 
-def first_body(mask_ref, ids_ref, x_ref, out):
-    pack_rows(permutation(False), x_ref, [out], 0)
-
-
-def first_pack(mask, ids, three_index):
+def first_body(mask_ref, x_ref, out, tiles, packed, in_sems, out_sems):
+    tile = tiles.shape[1]
+    own = lax.axis_index("occ")
+    arrivals, departures = [], []
+    for q in range(CAP):
+        at = pl.multiple_of(tile_of(mask_ref, own, q) * tile, tile)
+        copy = pltpu.make_async_copy(x_ref.at[pl.ds(at, tile), :, pl.ds(0, LANES)], tiles.at[q], in_sems.at[q])
+        copy.start()
+        arrivals.append(copy)
+    perm = permutation(False)
+    for q in range(CAP):
+        arrivals[q].wait()
+        pack_rows(perm, tiles.at[q], [packed.at[q]], 0)
+        copy = pltpu.make_async_copy(packed.at[q], out.at[:, pl.ds(q * tile, tile), :], out_sems.at[q])
+        copy.start()
+        departures.append(copy)
+    for copy in departures:
+        copy.wait()
+
+
+def first_pack(mask, three_index):
     tile = three_index.shape[0] // VT
     return pl.pallas_call(
         first_body,
         out_shape=jax.ShapeDtypeStruct((OCC, CAP * tile, LANES), jnp.bfloat16),
         grid_spec=pltpu.PrefetchScalarGridSpec(
-            num_scalar_prefetch=2,
-            grid=(CAP,),
-            in_specs=[
-                pl.BlockSpec((tile, OCC, LANES), lambda q, mask, ids: (tile_of(mask, ids[0], q), 0, 0)),
+            num_scalar_prefetch=1,
+            grid=(1,),
+            in_specs=[pl.BlockSpec(memory_space=pl.ANY)],
+            out_specs=pl.BlockSpec(memory_space=pl.ANY),
+            scratch_shapes=[
+                pltpu.VMEM((CAP, tile, OCC, LANES), jnp.bfloat16),
+                pltpu.VMEM((CAP, OCC, tile, LANES), jnp.bfloat16),
+                pltpu.SemaphoreType.DMA((CAP,)),
+                pltpu.SemaphoreType.DMA((CAP,)),
             ],
-            out_specs=pl.BlockSpec((OCC, tile, LANES), lambda q, mask, ids: (0, q, 0)),
         ),
         compiler_params=pltpu.CompilerParams(vmem_limit_bytes=VMEM),
         cost_estimate=pl.CostEstimate(flops=1 << 29, bytes_accessed=2 << 20, transcendentals=0),
-    )(mask, ids, three_index)
+    )(mask, three_index)
 
 
 def rest_body(mask_ref, ids_ref, x_ref, v0_ref, v1_ref, d_ref, virt_out, occ_out, table_out, *outs):
@@ -163,51 +186,81 @@
     return packs, virt, occ, table
 
 
-def density_body(table_ref, ids_ref, x0, x1, x2, x3, virt_in, occ_in, out, packs, virt_ref, occ_ref, total, mixed, result, in_sems, out_sems):
-    depth = x0.shape[1]
+def density_body(slabs, begins, ends, *refs):
+    table_ref, ids_ref, *refs = refs
+    count = len(slabs)
+    sources, (virt_in, occ_in), refs = refs[:count], refs[count:count + 2], refs[count + 2:]
+    if not begins:
+        partial, *refs = refs
+    out, packs, virt_ref, occ_ref, total, mixed, result, in_sems, out_sems = refs
+    depth = sources[0].shape[1]
     half_rows = virt_ref.shape[1]
-    blocks = out.shape[0] // (INNER * HALVES * OCC * 24)
-    span = half_rows // blocks
+    blocks = half_rows // SPAN
     tile = depth // CAP
-    targets = [packs.at[s, :, pl.ds(0, depth), :] for s in range(SLABS)] + [virt_ref, occ_ref]
+    targets = [packs.at[n, :, pl.ds(0, depth), :] for n in range(count)] + [virt_ref, occ_ref]
     arrivals = [
         pltpu.make_async_copy(ref, target, in_sems.at[n])
-        for n, (ref, target) in enumerate(zip((x0, x1, x2, x3, virt_in, occ_in), targets))
+        for n, (ref, target) in enumerate(zip(list(sources) + [virt_in, occ_in], targets))
     ]
-    for n in (0, 4, 1, 2, 3, 5):
+    if not begins:
+        arrivals.append(pltpu.make_async_copy(partial, total, in_sems.at[count + 2]))
+    for n in [0, count] + list(range(1, count)) + list(range(count + 1, len(arrivals))):
         arrivals[n].start()
-    for s in range(SLABS):
-        packs[s, :, depth:depth + FINE, :] = jnp.zeros((OCC, FINE, LANES), jnp.bfloat16)
-    perm = permutation(True)
-    arrivals[4].wait()
-    for which in range(2):
-        arrivals[which].wait()
+    for n in range(count):
+        packs[n, :, depth:depth + FINE, :] = jnp.zeros((OCC, FINE, LANES), jnp.bfloat16)
+    perm = permutation(True) if ends else None
+    waited = set()
+
+    def arrived(n):
+        if n not in waited:
+            waited.add(n)
+            arrivals[n].wait()
+
+    arrived(count)
+    if not begins:
+        arrived(count + 2)
+    for n, slab in enumerate(slabs):
+        if slab >= 2:
+            continue
+        arrived(n)
         for i in range(0, OCC, 2):
-            both = jnp.concatenate([packs[which, i, :depth], packs[which, i + 1, :depth]], axis=1)
-            y = dot(virt_ref[which], both)
-            total[which, i] = y[:, :LANES]
-            total[which, i + 1] = y[:, LANES:]
-    for n in (2, 3, 5):
-        arrivals[n].wait()
+            both = jnp.concatenate([packs[n, i, :depth], packs[n, i + 1, :depth]], axis=1)
+            y = dot(virt_ref[slab], both)
+            for j in range(2):
+                part = y[:, j * LANES:(j + 1) * LANES]
+                total[slab, i + j] = part if begins else part + total[slab, i + j]
+    for n in range(len(arrivals)):
+        arrived(n)
+    fresh = [which for which in range(2) if begins and which not in slabs]
     departures = []
     for which in range(2):
         half = ids_ref[1] if which == 0 else 1 - ids_ref[1]
+        weights = jnp.concatenate([occ_ref[which][:, s * FROWS:(s + 1) * FROWS] for s in slabs], axis=1)
         for first in range(0, half_rows, 2 * FINE):
-            columns, added = [], []
+            columns = []
             for row in (first, first + FINE):
-                start = row // span * (HALVES * span) + row % span + half * span
+                start = row // SPAN * (HALVES * SPAN) + row % SPAN + half * SPAN
                 parts = []
-                for s in range(SLABS):
+                for n, s in enumerate(slabs):
                     base = table_ref[s, start // tile]
                     at = pl.multiple_of(jnp.where(base < 0, depth, base + start % tile), FINE)
-                    parts.append(packs[s, :, pl.ds(at, FINE), :].reshape(FROWS, LANES))
+                    parts.append(packs[n, :, pl.ds(at, FINE), :].reshape(FROWS, LANES))
                 columns.append(jnp.concatenate(parts, axis=0))
-                added.append(total[which, :, row:row + FINE, :].reshape(FROWS, LANES))
-            y = dot(occ_ref[which], jnp.concatenate(columns, axis=1))
-            y = (y + jnp.concatenate(added, axis=1)).astype(jnp.bfloat16)
+            y = dot(weights, jnp.concatenate(columns, axis=1))
             for n in range(2):
                 row = first + n * FINE
-                mixed[which, :, row:row + FINE, :] = y[:, n * LANES:(n + 1) * LANES].reshape(OCC, FINE, LANES)
+                part = y[:, n * LANES:(n + 1) * LANES].reshape(OCC, FINE, LANES)
+                if which not in fresh:
+                    part = part + total[which, :, row:row + FINE, :]
+                if ends:
+                    mixed[which, :, row:row + FINE, :] = part.astype(jnp.bfloat16)
+                else:
+                    total[which, :, row:row + FINE, :] = part
+        if not ends:
+            copy = pltpu.make_async_copy(total.at[which], out.at[which], out_sems.at[which])
+            copy.start()
+            departures.append(copy)
+            continue
         for first in range(0, half_rows, 2 * GROUP):
             pair = transpose_rows(perm, [
                 mixed[which, :, row:row + GROUP, :].reshape(ROWS, LANES) for row in (first, first + GROUP)
@@ -216,10 +269,10 @@
                 at = (first + n * GROUP) * OCC
                 result[which, at:at + ROWS, :] = pair[n]
         for b in range(blocks):
-            start = pl.multiple_of((b * HALVES + half) * span * OCC, span * OCC)
+            start = pl.multiple_of((b * HALVES + half) * SPAN * OCC, SPAN * OCC)
             copy = pltpu.make_async_copy(
-                result.at[which, pl.ds(b * span * OCC, span * OCC), :],
-                out.at[pl.ds(start, span * OCC), :],
+                result.at[which, pl.ds(b * SPAN * OCC, SPAN * OCC), :],
+                out.at[pl.ds(start, SPAN * OCC), :],
                 out_sems.at[which * blocks + b],
             )
             copy.start()
@@ -228,37 +281,40 @@
         copy.wait()
 
 
-def density(table, ids, packs, virt, occ):
+def density(table, ids, slabs, packs, virt, occ, partial=None, ends=True):
     depth = packs[0].shape[1]
     half_rows = virt.shape[1]
     rows = 2 * half_rows * OCC
-    blocks = rows // (INNER * HALVES * OCC * 24)
+    sums = (2, OCC, half_rows, LANES)
+    begins = partial is None
+    share = len(slabs) * LANES
+    extra = [] if begins else [partial]
     return pl.pallas_call(
-        density_body,
-        out_shape=jax.ShapeDtypeStruct((rows, LANES), jnp.bfloat16),
+        functools.partial(density_body, slabs, begins, ends),
+        out_shape=jax.ShapeDtypeStruct((rows, LANES), jnp.bfloat16) if ends else jax.ShapeDtypeStruct(sums, jnp.float32),
         grid_spec=pltpu.PrefetchScalarGridSpec(
             num_scalar_prefetch=2,
             grid=(1,),
-            in_specs=[pl.BlockSpec(memory_space=pl.ANY)] * SLABS + [pl.BlockSpec(memory_space=pltpu.HBM)] * 2,
+            in_specs=[pl.BlockSpec(memory_space=pl.ANY)] * (len(slabs) + 2 + len(extra)),
             out_specs=pl.BlockSpec(memory_space=pl.ANY),
             scratch_shapes=[
-                pltpu.VMEM((SLABS, OCC, depth + FINE, LANES), jnp.bfloat16),
+                pltpu.VMEM((len(slabs), OCC, depth + FINE, LANES), jnp.bfloat16),
                 pltpu.VMEM(virt.shape, jnp.bfloat16),
                 pltpu.VMEM(occ.shape, jnp.bfloat16),
-                pltpu.VMEM((2, OCC, half_rows, LANES), jnp.float32),
-                pltpu.VMEM((2, OCC, half_rows, LANES), jnp.bfloat16),
-                pltpu.VMEM((2, half_rows * OCC, LANES), jnp.bfloat16),
-                pltpu.SemaphoreType.DMA((SLABS + 2,)),
-                pltpu.SemaphoreType.DMA((2 * blocks,)),
+                pltpu.VMEM(sums, jnp.float32),
+                pltpu.VMEM(sums if ends else (OCC, LANES), jnp.bfloat16),
+                pltpu.VMEM((2, half_rows * OCC, LANES) if ends else (OCC, LANES), jnp.bfloat16),
+                pltpu.SemaphoreType.DMA((len(slabs) + 3,)),
+                pltpu.SemaphoreType.DMA((2 * half_rows // SPAN,)),
             ],
         ),
         compiler_params=pltpu.CompilerParams(vmem_limit_bytes=24 << 20),
         cost_estimate=pl.CostEstimate(
-            flops=2 * LANES * (rows * depth + 3 * rows * ROWS),
-            bytes_accessed=2 * LANES * (rows + SLABS * OCC * depth),
+            flops=share * (rows * depth // 2 + 2 * rows * ROWS),
+            bytes_accessed=share * OCC * depth * 2 + rows * LANES * 2,
             transcendentals=0,
         ),
-    )(table, ids, *packs, virt, occ)
+    )(table, ids, *packs, virt, occ, *extra)
 
 
 def assemble_body(*refs):
@@ -268,34 +324,46 @@
     rows = out.shape[0]
     peers = ins[0].shape[0] // rows
     cols = out.shape[2] // peers
-    step = peers // out_sems.shape[0]
-    arrivals = [pltpu.make_async_copy(ref, arrived.at[k], in_sems.at[k]) for k, ref in enumerate(ins)]
-    for copy in arrivals:
-        copy.start()
-
-    def take(k, m):
-        whole[:, :, m * cols + k * LANES:m * cols + (k + 1) * LANES] = arrived[k, m * rows:(m + 1) * rows]
-
-    for k in range(count - 1):
-        arrivals[k].wait()
-        for m in range(peers):
-            take(k, m)
-    arrivals[-1].wait()
-    departures = []
-    for n in range(peers // step):
-        for m in range(n * step, (n + 1) * step):
-            take(count - 1, m)
-        part = pl.ds(n * step * cols, step * cols)
-        copy = pltpu.make_async_copy(whole.at[:, :, part], out.at[:, :, part], out_sems.at[n])
-        copy.start()
-        departures.append(copy)
-    for copy in departures:
-        copy.wait()
-
-
-def assemble(parts, peers):
+    steps = peers // INNER
+
+    def arrivals(n):
+        part = pl.ds(pl.multiple_of(n * INNER * rows, INNER * rows), INNER * rows)
+        return [
+            pltpu.make_async_copy(ref.at[part], arrived.at[k, part], in_sems.at[n, k]) for k, ref in enumerate(ins)
+        ]
+
+    def departure(n):
+        part = pl.ds(pl.multiple_of(n * INNER * cols, INNER * cols), INNER * cols)
+        return pltpu.make_async_copy(whole.at[:, :, part], out.at[:, :, part], out_sems.at[n])
+
+    def fetch(n, carry):
+        for copy in arrivals(n):
+            copy.start()
+        return carry
+
+    def place(n, carry):
+        for copy in arrivals(n):
+            copy.wait()
+        for m in range(INNER):
+            at = pl.multiple_of((n * INNER + m) * rows, rows)
+            for k in range(count):
+                first = pl.multiple_of((n * INNER + m) * cols + k * LANES, LANES)
+                whole[:, :, pl.ds(first, LANES)] = arrived[k, pl.ds(at, rows)]
+        departure(n).start()
+        return carry
+
+    def leave(n, carry):
+        departure(n).wait()
+        return carry
+
+    lax.fori_loop(0, steps, fetch, 0)
+    lax.fori_loop(0, steps, place, 0)
+    lax.fori_loop(0, steps, leave, 0)
+
+
+def assemble(parts, peers, cols):
     rows = parts[0].shape[0] // peers
-    shape = (rows, OCC, peers * len(parts) * LANES)
+    shape = (rows, OCC, peers * cols)
     return pl.pallas_call(
         assemble_body,
         out_shape=jax.ShapeDtypeStruct(shape, jnp.bfloat16),
@@ -304,14 +372,57 @@
         scratch_shapes=[
             pltpu.VMEM((len(parts),) + parts[0].shape, jnp.bfloat16),
             pltpu.VMEM(shape, jnp.bfloat16),
-            pltpu.SemaphoreType.DMA((len(parts),)),
-            pltpu.SemaphoreType.DMA((8,)),
+            pltpu.SemaphoreType.DMA((peers // INNER, len(parts))),
+            pltpu.SemaphoreType.DMA((peers // INNER,)),
         ],
         compiler_params=pltpu.CompilerParams(vmem_limit_bytes=VMEM),
         cost_estimate=pl.CostEstimate(
             flops=0, bytes_accessed=4 * rows * OCC * shape[2], transcendentals=0
         ),
     )(*parts)
+
+
+def place_body(part, _, out, held, in_sems, out_sems):
+    rows = out.shape[0]
+    peers = part.shape[0] // rows
+    cols = out.shape[2] // peers
+    steps = peers // INNER
+    arrivals, departures = [], []
+    for n in range(steps):
+        some = pl.ds(n * INNER * rows, INNER * rows)
+        copy = pltpu.make_async_copy(part.at[some], held.at[some], in_sems.at[n])
+        copy.start()
+        arrivals.append(copy)
+    for n in range(steps):
+        arrivals[n].wait()
+        for m in range(n * INNER, (n + 1) * INNER):
+            copy = pltpu.make_async_copy(
+                held.at[pl.ds(m * rows, rows)],
+                out.at[:, :, pl.ds((m + 1) * cols - LANES, LANES)],
+                out_sems.at[m],
+            )
+            copy.start()
+            departures.append(copy)
+    for copy in departures:
+        copy.wait()
+
+
+def place_last(part, whole):
+    peers = part.shape[0] // whole.shape[0]
+    return pl.pallas_call(
+        place_body,
+        out_shape=jax.ShapeDtypeStruct(whole.shape, whole.dtype),
+        in_specs=[pl.BlockSpec(memory_space=pl.ANY)] * 2,
+        out_specs=pl.BlockSpec(memory_space=pl.ANY),
+        scratch_shapes=[
+            pltpu.VMEM(part.shape, jnp.bfloat16),
+            pltpu.SemaphoreType.DMA((peers // INNER,)),
+            pltpu.SemaphoreType.DMA((peers,)),
+        ],
+        input_output_aliases={1: 0},
+        compiler_params=pltpu.CompilerParams(vmem_limit_bytes=VMEM),
+        cost_estimate=pl.CostEstimate(flops=0, bytes_accessed=4 * part.size, transcendentals=0),
+    )(part, whole)
 
 
 def exchange_groups(peers):
@@ -329,10 +440,10 @@
     peers = lax.axis_size("aux")
     own = lax.axis_index("occ")
     my_half = (lax.axis_index("aux") // INNER) % HALVES
-    ids = jnp.stack([own, my_half]).astype(jnp.int32)
     by_half = virt_density.reshape(peers // (HALVES * INNER), HALVES, -1, virt_count)
 
-    head = first_pack(tile_mask, ids, three_index)
+    head = first_pack(tile_mask, three_index)
+    ids = jnp.stack(lax.optimization_barrier((own, my_half, head))[:2]).astype(jnp.int32)
     others, *weights = rest_pack(tile_mask, ids, three_index, by_half, occ_density)
     virt, occ, table = (pltpu.with_memory_space_constraint(array, pltpu.HBM) for array in weights)
     mine = [head] + others
@@ -341,21 +452,33 @@
     core_pairs = [(s, s ^ 1) for s in range(SLABS)]
     groups = exchange_groups(peers)
     done, acrosses = [], []
+    last = len(mine) - 1
+    besides = [lax.ppermute(part, "occ", core_pairs) for part in mine]
     for k, part in enumerate(mine):
         sent = part
         if k >= 2:
             sent, _ = lax.optimization_barrier((part, acrosses[k - 2]))
         across = lax.ppermute(sent, "occ", chip_pairs)
-        across, _ = lax.optimization_barrier((across, gamma if k else mine[1]))
+        beside = besides[k]
+        partial = None
+        if k in (0, last):
+            own_part = part if k == 0 else lax.optimization_barrier((part, gamma))[0]
+            partial = density(table, ids, (0, 2), (own_part, beside), virt, occ, ends=False)
+        before = (mine[1], partial, *besides[1:]) if k == 0 else (gamma, partial) if k == last else (gamma,)
+        across, *before = lax.optimization_barrier((across,) + before)
+        if k == 0:
+            besides[1:] = before[2:]
         acrosses.append(across)
-        beside = lax.ppermute(part, "occ", core_pairs)
         diagonal = lax.ppermute(across, "occ", core_pairs)
-        gamma = density(table, ids, (part, across, beside, diagonal), virt, occ)
-        gamma = gamma.reshape(virt_count, OCC, -1)
+        if partial is None:
+            gamma = density(table, ids, (0, 1, 2, 3), (part, across, beside, diagonal), virt, occ)
+        else:
+            gamma = density(table, ids, (1, 3), (across, diagonal), virt, occ, partial=before[1])
         done.append(lax.all_to_all(
-            gamma, ("occ", "aux"), split_axis=0, concat_axis=0, axis_index_groups=groups, tiled=True
+            gamma.reshape(virt_count, OCC, -1), ("occ", "aux"),
+            split_axis=0, concat_axis=0, axis_index_groups=groups, tiled=True,
         ))
-    return assemble(done, peers)
+    return place_last(done[-1], assemble(done[:-1], peers, three_index.shape[2]))
 
 
 def solution(mesh):

time: 188 us -> 186 us (0.989)
  blocking collectives: 24.9 us -> 0 us
  Pallas kernels: 47.6 us -> 54.5 us
  local copies, waits for them, and re-layouts: 0.02 us -> 6.85 us
  starting transfers between devices: 36.1 us -> 41.5 us
  waiting for transfers between devices: 76.3 us -> 80.8 us
    all_to_all x1 -> x0, blocking collectives: 24.9 us -> none  [local(): lax.all_to_all(gamma, ('occ', 'aux'), split_axis=0, concat_axis=0, axis_i...]
    all_to_all x4 -> x5, waiting for transfers between devices: 40.6 us -> 50.4 us  [local(): lax.all_to_all(gamma.reshape(virt_count, OCC, -1), ('occ', 'aux'), split_...]
    pallas_call x5 -> x8, Pallas kernels: 30.4 us -> 38 us  [the longest x7 35.5 us: density(): pl.pallas_call(functools.partial(density_body, slabs, begins, ends), out_...]
    unnamed x12 -> x26, local copies, waits for them, and re-layouts: 0.02 us -> 6.85 us
    all_to_all x4 -> x5, starting transfers between devices: 26.1 us -> 31.2 us  [local(): lax.all_to_all(gamma.reshape(virt_count, OCC, -1), ('occ', 'aux'), split_...]
    ppermute x5, waiting for transfers between devices: 26.9 us -> 23.6 us  [local(): across = lax.ppermute(sent, 'occ', chip_pairs)]
    ppermute x5, waiting for transfers between devices: 2.29 us -> 0.01 us  [local(): besides = [lax.ppermute(part, 'occ', core_pairs) for part in mine]]
  transfers between devices with their start and end apart: 19 -> 20, of which waited for: 16 -> 14; matrix products, arithmetic and copies ran while one was open for 0% -> 0% of each run, Pallas kernels for 20% -> 26%
where the time goes in v2:
time: 186 us; the launch traced here: 185 us
  waiting for transfers between devices  80.8 us (43%)
  Pallas kernels  54.5 us (29%)
  starting transfers between devices  41.5 us (22%)
  local copies, waits for them, and re-layouts  6.85 us (4%)
    all_to_all x5, waiting for transfers between devices, local(): lax.all_to_all(gamma.reshape(virt_count, OCC, -1), ('occ', 'aux'), split_...  50.4 us
    pallas_call x7, Pallas kernels, density(): pl.pallas_call(functools.partial(density_body, slabs, begins, ends), out_...  35.5 us
    all_to_all x5, starting transfers between devices, local(): lax.all_to_all(gamma.reshape(virt_count, OCC, -1), ('occ', 'aux'), split_...  31.2 us
    ppermute x5, waiting for transfers between devices, local(): across = lax.ppermute(sent, 'occ', chip_pairs)  23.6 us
    ppermute x5, starting transfers between devices, local(): across = lax.ppermute(sent, 'occ', chip_pairs)  9.08 us
    pallas_call x1, Pallas kernels, rest_pack(): pl.pallas_call(rest_body, out_shape=[jax.ShapeDtypeStruct((2, half_rows,...  7.49 us
    unnamed x26, local copies, waits for them, and re-layouts  6.85 us
    ppermute x5, waiting for transfers between devices, local(): diagonal = lax.ppermute(across, 'occ', core_pairs)  6.81 us
  transfers between devices with their start and end apart: 20, of which 14 were waited for; matrix products, arithmetic and copies ran while one was open for 0% of the time, Pallas kernels for 26%

profile of v2, /device:TPU:2, one launch (start us, length us, event | category | flops | bytes accessed | tf_op | source)
XLA Modules:
  0.0 184.7 jit_solution(3545921147448544631)
XLA Ops:
  0.0 3.4 %shard_map.46.refs_2_ = bf16[8,512,128]{2,1,0:T(8,128)(2,1)} custom-call(s32[4,6]{1,0:T(4,128)} %mask_ref.3, bf16[768,8,640]{2,1,0:T(8,128)(2,1)} %x_ref.3), custom_call_target="tpu_custom_call" | custom-call | flops 536870912 | bytes 2097152 | tf_op jit(solution)/shard_map/pallas_call | solution.py:91
  3.4 0.1 collective-permute-start.1
  3.5 2.0 %collective-permute-start = (bf16[8,512,128]{2,1,0:T(8,128)(2,1)}, bf16[8,512,128]{2,1,0:T(8,128)(2,1)S(1)}, u32[]{:S(2)}, u32[]{:S(2)}) collective-permute-start(bf16[8,512,128]{2,1,0:T(8,128)(2,1)} %shard_map.46.refs_2_), channel_id=1, source_target_pairs={{0,64},{32,96},{64,0},{96,32},{1,65},{33,97},{65,1},{97,33},{2,66}... | collective-permute-start | bytes 3145736 | tf_op jit(solution)/shard_map/ppermute | solution.py:461
  5.5 0.7 pad_add_fusion.ids_ref.refs_1_
  6.1 7.5 %shard_map.47 = (bf16[2,384,512]{2,1,0:T(8,128)(2,1)}, bf16[2,128,512]{2,1,0:T(8,128)(2,1)}, s32[4,6]{1,0:T(4,128)}, bf16[8,512,128]{2,1,0:T(8,128)(2,1)}, bf16[...) custom-call(s32[4,6]{1,0:T(4,128)} %mask_ref.3, ...), custom_call_target="tpu_custom_call" | custom-call | flops 3221225472 | bytes 12582912 | tf_op jit(solution)/shard_map/pallas_call | solution.py:161
  13.6 0.1 collective-permute-start.5
  13.8 0.4 collective-permute-start.3
  14.1 0.1 collective-permute-start.4
  14.3 0.4 collective-permute-start.2
  14.6 3.9 %shard_map.48.refs_6_ = f32[2,8,384,128]{3,2,1,0:T(8,128)S(1)} custom-call(s32[4,6]{1,0:T(4,128)} %get-tuple-element.31.refs_0_, s32[2]{0:T(128)S(1)} %copy-done.2, bf16[8,512,128]{2,1,0:T(8,128)(2,1)S(1)} %copy-done, bf16[8,512,128]{2,1,0:T(8,128)(2,1)} %collective-permute-done.1.refs_3_, bf16[2,384,512]{2,1,0:T(8,128)(2,1)} %get-tuple-element.35.refs_4_.refs_6_, ...), custom_call_target="tpu_custom_call" | custom-call | flops 1207959552 | bytes 3670016 | tf_op jit(solution)/shard_map/pallas_call | solution.py:292
  18.5 10.9 %collective-permute-done.refs_2_ = bf16[8,512,128]{2,1,0:T(8,128)(2,1)S(1)} collective-permute-done((bf16[8,512,128]{2,1,0:T(8,128)(2,1)}, bf16[8,512,128]{2,1,0:T(8,128)(2,1)S(1)}, u32[]{:S(2)}, u32[]{:S(2)}) %collective-permute-start) | collective-permute-done | bytes 1048608 | tf_op jit(solution)/shard_map/ppermute | solution.py:461
  29.4 1.0 copy-done.8
  30.4 1.0 copy-done.5
  31.4 1.8 collective-permute-start.7
  33.2 0.8 collective-permute-done.8.refs_3_
  34.0 4.9 %shard_map.49 = bf16[6144,128]{1,0:T(8,128)(2,1)} custom-call(s32[4,6]{1,0:T(4,128)} %get-tuple-element.31.refs_0_, s32[2]{0:T(128)S(1)} %copy-done.2, bf16[8,512,128]{2,1,0:T(8,128)(2,1)S(1)} %collective-permute-done.refs_2_, bf16[8,512,128]{2,1,0:T(8,128)(2,1)S(1)} %collective-permute-done.8.refs_3_, ...), custom_call_target="tpu_custom_call" | custom-call | flops 1207959552 | bytes 3670016 | tf_op jit(solution)/shard_map/pallas_call | solution.py:292
  38.9 11.1 %all-to-all-start.1 = ((bf16[768,8,128]{2,1,0:T(8,128)(2,1)}), bf16[768,8,128]{2,1,0:T(8,128)(2,1)}, u32[]{:S(2)}, u32[]{:S(2)}) async-start(bf16[768,8,128]{2,1,0:T(8,128)(2,1)} %bitcast.4), calls=%async_computation.1 | async-start | bytes 3145728 | tf_op jit(solution)/shard_map/all_to_all | solution.py:477
  50.1 7.2 %collective-permute-done.7.refs_3_ = bf16[8,512,128]{2,1,0:T(8,128)(2,1)} collective-permute-done((bf16[8,512,128]{2,1,0:T(8,128)(2,1)}, bf16[8,512,128]{2,1,0:T(8,128)(2,1)}, u32[]{:S(2)}, u32[]{:S(2)}) %collective-permute-start.7) | collective-permute-done | bytes 1048608 | tf_op jit(solution)/shard_map/ppermute | solution.py:461
  57.3 1.8 collective-permute-start.6
  59.0 1.1 collective-permute-done.9.refs_5_
  60.2 6.2 %shard_map.50 = bf16[6144,128]{1,0:T(8,128)(2,1)} custom-call(s32[4,6]{1,0:T(4,128)} %get-tuple-element.31.refs_0_, s32[2]{0:T(128)S(1)} %copy-done.2, bf16[8,512,128]{2,1,0:T(8,128)(2,1)} %get-tuple-element.34.refs_2_, bf16[8,512,128]{2,1,0:T(8,128)(2,1)} %collective-permute-done.7.refs_3_, bf16[8,512,128]{2,1,0:T(8,128)(2,1)S(1)} %copy-done.11, ...), custom_call_target="tpu_custom_call" | custom-call | flops 2415919104 | bytes 5767168 | tf_op jit(solution)/shard_map/pallas_call | solution.py:292
  66.3 8.1 %all-to-all-done.1.refs_0_ = bf16[768,8,128]{2,1,0:T(8,128)(2,1)} async-done(((bf16[768,8,128]{2,1,0:T(8,128)(2,1)}), bf16[768,8,128]{2,1,0:T(8,128)(2,1)}, u32[]{:S(2)}, u32[]{:S(2)}) %all-to-all-start.1) | async-done | bytes 1572896 | tf_op jit(solution)/shard_map/all_to_all | solution.py:477
  74.4 4.7 %all-to-all-start.2 = ((bf16[768,8,128]{2,1,0:T(8,128)(2,1)}), bf16[768,8,128]{2,1,0:T(8,128)(2,1)}, u32[]{:S(2)}, u32[]{:S(2)}) async-start(bf16[768,8,128]{2,1,0:T(8,128)(2,1)} %bitcast.5), calls=%async_computation.2 | async-start | bytes 3145728 | tf_op jit(solution)/shard_map/all_to_all | solution.py:477
  79.1 3.9 %collective-permute-done.6.refs_3_ = bf16[8,512,128]{2,1,0:T(8,128)(2,1)} collective-permute-done((bf16[8,512,128]{2,1,0:T(8,128)(2,1)S(1)}, bf16[8,512,128]{2,1,0:T(8,128)(2,1)}, u32[]{:S(2)}, u32[]{:S(2)}) %collective-permute-start.6) | collective-permute-done | bytes 1048608 | tf_op jit(solution)/shard_map/ppermute | solution.py:461
  83.0 1.7 collective-permute-start.11
  84.7 1.1 collective-permute-done.12.refs_5_
  85.9 1.2 copy-done.9
  87.1 5.9 %shard_map.51 = bf16[6144,128]{1,0:T(8,128)(2,1)} custom-call(s32[4,6]{1,0:T(4,128)} %get-tuple-element.31.refs_0_, s32[2]{0:T(128)S(1)} %copy-done.2, bf16[8,512,128]{2,1,0:T(8,128)(2,1)S(1)} %copy-done.7, bf16[8,512,128]{2,1,0:T(8,128)(2,1)} %collective-permute-done.6.refs_3_, bf16[8,512,128]{2,1,0:T(8,128)(2,1)S(1)} %copy-done.9, ...), custom_call_target="tpu_custom_call" | custom-call | flops 2415919104 | bytes 5767168 | tf_op jit(solution)/shard_map/pallas_call | solution.py:292
  93.0 8.4 %all-to-all-done.2.refs_1_ = bf16[768,8,128]{2,1,0:T(8,128)(2,1)} async-done(((bf16[768,8,128]{2,1,0:T(8,128)(2,1)}), bf16[768,8,128]{2,1,0:T(8,128)(2,1)}, u32[]{:S(2)}, u32[]{:S(2)}) %all-to-all-start.2) | async-done | bytes 1572896 | tf_op jit(solution)/shard_map/all_to_all | solution.py:477
  101.4 5.7 %all-to-all-start.3 = ((bf16[768,8,128]{2,1,0:T(8,128)(2,1)}), bf16[768,8,128]{2,1,0:T(8,128)(2,1)}, u32[]{:S(2)}, u32[]{:S(2)}) async-start(bf16[768,8,128]{2,1,0:T(8,128)(2,1)} %bitcast.6), calls=%async_computation.3 | async-start | bytes 3145728 | tf_op jit(solution)/shard_map/all_to_all | solution.py:477
  107.1 1.6 collective-permute-done.11.refs_3_
  108.7 1.7 collective-permute-start.10
  110.4 1.1 collective-permute-done.13.refs_5_
  111.5 1.2 copy-done.4
  112.8 1.2 copy-done.6
  114.0 5.9 %shard_map.52 = bf16[6144,128]{1,0:T(8,128)(2,1)} custom-call(s32[4,6]{1,0:T(4,128)} %get-tuple-element.31.refs_0_, s32[2]{0:T(128)S(1)} %copy-done.2, bf16[8,512,128]{2,1,0:T(8,128)(2,1)S(1)} %copy-done.4, bf16[8,512,128]{2,1,0:T(8,128)(2,1)} %collective-permute-done.11.refs_3_, bf16[8,512,128]{2,1,0:T(8,128)(2,1)S(1)} %copy-done.6, ...), custom_call_target="tpu_custom_call" | custom-call | flops 2415919104 | bytes 5767168 | tf_op jit(solution)/shard_map/pallas_call | solution.py:292
  119.9 8.4 %all-to-all-done.3.refs_2_ = bf16[768,8,128]{2,1,0:T(8,128)(2,1)} async-done(((bf16[768,8,128]{2,1,0:T(8,128)(2,1)}), bf16[768,8,128]{2,1,0:T(8,128)(2,1)}, u32[]{:S(2)}, u32[]{:S(2)}) %all-to-all-start.3) | async-done | bytes 1572896 | tf_op jit(solution)/shard_map/all_to_all | solution.py:477
  128.3 4.7 %all-to-all-start.4 = ((bf16[768,8,128]{2,1,0:T(8,128)(2,1)}), bf16[768,8,128]{2,1,0:T(8,128)(2,1)}, u32[]{:S(2)}, u32[]{:S(2)}) async-start(bf16[768,8,128]{2,1,0:T(8,128)(2,1)} %bitcast.7), calls=%async_computation.4 | async-start | bytes 3145728 | tf_op jit(solution)/shard_map/all_to_all | solution.py:477
  133.1 3.9 %shard_map.53.refs_6_ = f32[2,8,384,128]{3,2,1,0:T(8,128)S(1)} custom-call(s32[4,6]{1,0:T(4,128)} %get-tuple-element.31.refs_0_, s32[2]{0:T(128)S(1)} %copy-done.2, bf16[8,512,128]{2,1,0:T(8,128)(2,1)S(1)} %copy-done.1, bf16[8,512,128]{2,1,0:T(8,128)(2,1)S(1)} %collective-permute-done.5.refs_3_, bf16[2,384,512]{2,1,0:T(8,128)(2,1)} %get-tuple-element.35.refs_4_.refs_6_, ...), custom_call_target="tpu_custom_call" | custom-call | flops 1207959552 | bytes 3670016 | tf_op jit(solution)/shard_map/pallas_call | solution.py:292
  136.9 0.1 collective-permute-start.14
  137.0 2.6 %collective-permute-done.14.refs_3_ = bf16[8,512,128]{2,1,0:T(8,128)(2,1)S(1)} collective-permute-done((bf16[8,512,128]{2,1,0:T(8,128)(2,1)S(1)}, bf16[8,512,128]{2,1,0:T(8,128)(2,1)S(1)}, u32[]{:S(2)}, u32[]{:S(2)}) %collective-permute-start.14) | collective-permute-done | bytes 1048608 | tf_op jit(solution)/shard_map/ppermute | solution.py:472
  139.7 4.9 %shard_map.54 = bf16[6144,128]{1,0:T(8,128)(2,1)} custom-call(s32[4,6]{1,0:T(4,128)} %get-tuple-element.31.refs_0_, s32[2]{0:T(128)S(1)} %copy-done.2, bf16[8,512,128]{2,1,0:T(8,128)(2,1)S(1)} %collective-permute-done.10.refs_2_, bf16[8,512,128]{2,1,0:T(8,128)(2,1)S(1)} %collective-permute-done.14.refs_3_, ...), custom_call_target="tpu_custom_call" | custom-call | flops 1207959552 | bytes 3670016 | tf_op jit(solution)/shard_map/pallas_call | solution.py:292
  144.6 10.0 %all-to-all-done.4.refs_3_ = bf16[768,8,128]{2,1,0:T(8,128)(2,1)} async-done(((bf16[768,8,128]{2,1,0:T(8,128)(2,1)}), bf16[768,8,128]{2,1,0:T(8,128)(2,1)}, u32[]{:S(2)}, u32[]{:S(2)}) %all-to-all-start.4) | async-done | bytes 1572896 | tf_op jit(solution)/shard_map/all_to_all | solution.py:477
  154.6 5.0 %all-to-all-start = ((bf16[768,8,128]{2,1,0:T(8,128)(2,1)}), bf16[768,8,128]{2,1,0:T(8,128)(2,1)S(1)}, u32[]{:S(2)}, u32[]{:S(2)}) async-start(bf16[768,8,128]{2,1,0:T(8,128)(2,1)} %bitcast.3), calls=%async_computation | async-start | bytes 3145728 | tf_op jit(solution)/shard_map/all_to_all | solution.py:477
  159.6 5.7 %shard_map.55._ = bf16[24,8,20480]{2,1,0:T(8,128)(2,1)} custom-call(bf16[768,8,128]{2,1,0:T(8,128)(2,1)} %all-to-all-done.1.refs_0_, bf16[768,8,128]{2,1,0:T(8,128)(2,1)} %all-to-all-done.2.refs_1_, bf16[768,8,128]{2,1,0:T(8,128)(2,1)} %all-to-all-done.3.refs_2_, bf16[768,8,128]{2,1,0:T(8,128)(2,1)} %all-to-all-done.4.refs_3_), custom_call_target="tpu_custom_call" | custom-call | bytes 15728640 | tf_op jit(solution)/shard_map/pallas_call | solution.py:367
  165.3 15.5 %all-to-all-done.part = bf16[768,8,128]{2,1,0:T(8,128)(2,1)S(1)} async-done(((bf16[768,8,128]{2,1,0:T(8,128)(2,1)}), bf16[768,8,128]{2,1,0:T(8,128)(2,1)S(1)}, u32[]{:S(2)}, u32[]{:S(2)}) %all-to-all-start) | async-done | bytes 1572896 | tf_op jit(solution)/shard_map/all_to_all | solution.py:477
  180.8 1.2 copy-done.12
  182.0 2.5 %shard_map.56 = bf16[24,8,20480]{2,1,0:T(8,128)(2,1)} custom-call(bf16[768,8,128]{2,1,0:T(8,128)(2,1)} %copy-done.12, bf16[24,8,20480]{2,1,0:T(8,128)(2,1)} %shard_map.55._), custom_call_target="tpu_custom_call", output_to_operand_aliasing={{}: (1, {})} | custom-call | bytes 3145728 | tf_op jit(solution)/shard_map/pallas_call | solution.py:412
  (30 shorter events, 0.1 us)
Async XLA Ops:
  3.4 10.9 %collective-permute-start.1 = (bf16[8,512,128]{2,1,0:T(8,128)(2,1)}, bf16[8,512,128]{2,1,0:T(8,128)(2,1)}, u32[]{:S(2)}, u32[]{:S(2)}) collective-permute-start(bf16[8,512,128]{2,1,0:T(8,128)(2,1)} %shard_map.46.refs_2_), channel_id=1, source_target_pairs={{0,32},{32,0},{64,96},{96,64},{1,33},{33,1},{65,97},{97,65},{2,34}... | collective-permute-start | bytes 3145736 | tf_op jit(solution)/shard_map/ppermute | solution.py:456
  3.5 25.9 %collective-permute-start = (bf16[8,512,128]{2,1,0:T(8,128)(2,1)}, bf16[8,512,128]{2,1,0:T(8,128)(2,1)S(1)}, u32[]{:S(2)}, u32[]{:S(2)}) collective-permute-start(bf16[8,512,128]{2,1,0:T(8,128)(2,1)} %shard_map.46.refs_2_), channel_id=1, source_target_pairs={{0,64},{32,96},{64,0},{96,32},{1,65},{33,97},{65,1},{97,33},{2,66}... | collective-permute-start | bytes 3145736 | tf_op jit(solution)/shard_map/ppermute | solution.py:461
  6.1 8.5 %copy-start = (bf16[8,512,128]{2,1,0:T(8,128)(2,1)S(1)}, bf16[8,512,128]{2,1,0:T(8,128)(2,1)}, u32[]{:S(2)}) copy-start(bf16[8,512,128]{2,1,0:T(8,128)(2,1)} %shard_map.46.refs_2_) | copy-start | bytes 3145732
  6.1 8.5 %copy-start.2 = (s32[2]{0:T(128)S(1)}, s32[2]{0:T(128)}, u32[]{:S(2)}) copy-start(s32[2]{0:T(128)} %pad_add_fusion.ids_ref.refs_1_) | copy-start | bytes 28
  13.6 15.8 %collective-permute-start.5 = (bf16[8,512,128]{2,1,0:T(8,128)(2,1)}, bf16[8,512,128]{2,1,0:T(8,128)(2,1)S(1)}, u32[]{:S(2)}, u32[]{:S(2)}) collective-permute-start(bf16[8,512,128]{2,1,0:T(8,128)(2,1)} %get-tuple-element.49.refs_2_), channel_id=1, source_target_pairs={{0,32},{32,0},{64,96},{96,64},{1,33},{33,1},{65,97},{97,65},{2,34}... | collective-permute-start | bytes 3145736 | tf_op jit(solution)/shard_map/ppermute | solution.py:456
  13.8 15.7 %collective-permute-start.3 = (bf16[8,512,128]{2,1,0:T(8,128)(2,1)}, bf16[8,512,128]{2,1,0:T(8,128)(2,1)S(1)}, u32[]{:S(2)}, u32[]{:S(2)}) collective-permute-start(bf16[8,512,128]{2,1,0:T(8,128)(2,1)} %get-tuple-element.39.refs_2_), channel_id=1, source_target_pairs={{0,32},{32,0},{64,96},{96,64},{1,33},{33,1},{65,97},{97,65},{2,34}... | collective-permute-start | bytes 3145736 | tf_op jit(solution)/shard_map/ppermute | solution.py:456
  14.1 16.3 %collective-permute-start.4 = (bf16[8,512,128]{2,1,0:T(8,128)(2,1)}, bf16[8,512,128]{2,1,0:T(8,128)(2,1)S(1)}, u32[]{:S(2)}, u32[]{:S(2)}) collective-permute-start(bf16[8,512,128]{2,1,0:T(8,128)(2,1)} %get-tuple-element.45.refs_2_), channel_id=1, source_target_pairs={{0,32},{32,0},{64,96},{96,64},{1,33},{33,1},{65,97},{97,65},{2,34}... | collective-permute-start | bytes 3145736 | tf_op jit(solution)/shard_map/ppermute | solution.py:456
  14.3 17.1 %collective-permute-start.2 = (bf16[8,512,128]{2,1,0:T(8,128)(2,1)}, bf16[8,512,128]{2,1,0:T(8,128)(2,1)S(1)}, u32[]{:S(2)}, u32[]{:S(2)}) collective-permute-start(bf16[8,512,128]{2,1,0:T(8,128)(2,1)} %get-tuple-element.34.refs_2_), channel_id=1, source_target_pairs={{0,32},{32,0},{64,96},{96,64},{1,33},{33,1},{65,97},{97,65},{2,34}... | collective-permute-start | bytes 3145736 | tf_op jit(solution)/shard_map/ppermute | solution.py:456
  29.4 1.0 copy-start.8
  30.4 1.0 copy-start.5
  31.4 7.5 %copy-start.10 = (bf16[8,512,128]{2,1,0:T(8,128)(2,1)}, bf16[8,512,128]{2,1,0:T(8,128)(2,1)S(1)}, u32[]{:S(2)}) copy-start(bf16[8,512,128]{2,1,0:T(8,128)(2,1)S(1)} %collective-permute-done.2.refs_4_) | copy-start | bytes 3145732
  31.4 2.7 %collective-permute-start.8 = (bf16[8,512,128]{2,1,0:T(8,128)(2,1)S(1)}, bf16[8,512,128]{2,1,0:T(8,128)(2,1)S(1)}, u32[]{:S(2)}, u32[]{:S(2)}) collective-permute-start(bf16[8,512,128]{2,1,0:T(8,128)(2,1)S(1)} %collective-permute-done.refs_2_), channel_id=1, source_target_pairs={{0,32},{32,0},{64,96},{96,64},{1,33},{33,1},{65,97},{97,65},{2,34}... | collective-permute-start | bytes 3145736 | tf_op jit(solution)/shard_map/ppermute | solution.py:472
  31.4 25.9 %collective-permute-start.7 = (bf16[8,512,128]{2,1,0:T(8,128)(2,1)}, bf16[8,512,128]{2,1,0:T(8,128)(2,1)}, u32[]{:S(2)}, u32[]{:S(2)}) collective-permute-start(bf16[8,512,128]{2,1,0:T(8,128)(2,1)} %get-tuple-element.34.refs_2_), channel_id=1, source_target_pairs={{0,64},{32,96},{64,0},{96,32},{1,65},{33,97},{65,1},{97,33},{2,66}... | collective-permute-start | bytes 3145736 | tf_op jit(solution)/shard_map/ppermute | solution.py:461
  38.9 18.4 %copy-start.7 = (bf16[8,512,128]{2,1,0:T(8,128)(2,1)S(1)}, bf16[8,512,128]{2,1,0:T(8,128)(2,1)}, u32[]{:S(2)}) copy-start(bf16[8,512,128]{2,1,0:T(8,128)(2,1)} %get-tuple-element.39.refs_2_) | copy-start | bytes 3145732
  38.9 21.2 %copy-start.11 = (bf16[8,512,128]{2,1,0:T(8,128)(2,1)S(1)}, bf16[8,512,128]{2,1,0:T(8,128)(2,1)}, u32[]{:S(2)}) copy-start(bf16[8,512,128]{2,1,0:T(8,128)(2,1)} %copy-done.10) | copy-start | bytes 3145732
  38.9 35.5 %all-to-all-start.1 = ((bf16[768,8,128]{2,1,0:T(8,128)(2,1)}), bf16[768,8,128]{2,1,0:T(8,128)(2,1)}, u32[]{:S(2)}, u32[]{:S(2)}) async-start(bf16[768,8,128]{2,1,0:T(8,128)(2,1)} %bitcast.4), calls=%async_computation.1 | async-start | bytes 3145728 | tf_op jit(solution)/shard_map/all_to_all | solution.py:477
  57.3 2.9 %collective-permute-start.9 = (bf16[8,512,128]{2,1,0:T(8,128)(2,1)}, bf16[8,512,128]{2,1,0:T(8,128)(2,1)S(1)}, u32[]{:S(2)}, u32[]{:S(2)}) collective-permute-start(bf16[8,512,128]{2,1,0:T(8,128)(2,1)} %collective-permute-done.7.refs_3_), channel_id=1, source_target_pairs={{0,32},{32,0},{64,96},{96,64},{1,33},{33,1},{65,97},{97,65},{2,34}... | collective-permute-start | bytes 3145736 | tf_op jit(solution)/shard_map/ppermute | solution.py:472
  57.3 25.7 %collective-permute-start.6 = (bf16[8,512,128]{2,1,0:T(8,128)(2,1)S(1)}, bf16[8,512,128]{2,1,0:T(8,128)(2,1)}, u32[]{:S(2)}, u32[]{:S(2)}) collective-permute-start(bf16[8,512,128]{2,1,0:T(8,128)(2,1)S(1)} %copy-done.7), channel_id=1, source_target_pairs={{0,64},{32,96},{64,0},{96,32},{1,65},{33,97},{65,1},{97,33},{2,66}... | collective-permute-start | bytes 3145736 | tf_op jit(solution)/shard_map/ppermute | solution.py:461
  74.4 8.6 %copy-start.3 = (bf16[8,512,128]{2,1,0:T(8,128)(2,1)S(1)}, bf16[8,512,128]{2,1,0:T(8,128)(2,1)}, u32[]{:S(2)}) copy-start(bf16[8,512,128]{2,1,0:T(8,128)(2,1)} %get-tuple-element.45.refs_2_) | copy-start | bytes 3145732
  74.4 27.0 %all-to-all-start.2 = ((bf16[768,8,128]{2,1,0:T(8,128)(2,1)}), bf16[768,8,128]{2,1,0:T(8,128)(2,1)}, u32[]{:S(2)}, u32[]{:S(2)}) async-start(bf16[768,8,128]{2,1,0:T(8,128)(2,1)} %bitcast.5), calls=%async_computation.2 | async-start | bytes 3145728 | tf_op jit(solution)/shard_map/all_to_all | solution.py:477
  83.0 2.9 %collective-permute-start.12 = (bf16[8,512,128]{2,1,0:T(8,128)(2,1)}, bf16[8,512,128]{2,1,0:T(8,128)(2,1)S(1)}, u32[]{:S(2)}, u32[]{:S(2)}) collective-permute-start(bf16[8,512,128]{2,1,0:T(8,128)(2,1)} %collective-permute-done.6.refs_3_), channel_id=1, source_target_pairs={{0,32},{32,0},{64,96},{96,64},{1,33},{33,1},{65,97},{97,65},{2,34}... | collective-permute-start | bytes 3145736 | tf_op jit(solution)/shard_map/ppermute | solution.py:472
  83.0 25.7 %collective-permute-start.11 = (bf16[8,512,128]{2,1,0:T(8,128)(2,1)S(1)}, bf16[8,512,128]{2,1,0:T(8,128)(2,1)}, u32[]{:S(2)}, u32[]{:S(2)}) collective-permute-start(bf16[8,512,128]{2,1,0:T(8,128)(2,1)S(1)} %copy-done.3), channel_id=1, source_target_pairs={{0,64},{32,96},{64,0},{96,32},{1,65},{33,97},{65,1},{97,33},{2,66}... | collective-permute-start | bytes 3145736 | tf_op jit(solution)/shard_map/ppermute | solution.py:461
  85.9 1.2 copy-start.9
  101.4 7.3 %copy-start.1 = (bf16[8,512,128]{2,1,0:T(8,128)(2,1)S(1)}, bf16[8,512,128]{2,1,0:T(8,128)(2,1)}, u32[]{:S(2)}) copy-start(bf16[8,512,128]{2,1,0:T(8,128)(2,1)} %get-tuple-element.49.refs_2_) | copy-start | bytes 3145732
  101.4 26.9 %all-to-all-start.3 = ((bf16[768,8,128]{2,1,0:T(8,128)(2,1)}), bf16[768,8,128]{2,1,0:T(8,128)(2,1)}, u32[]{:S(2)}, u32[]{:S(2)}) async-start(bf16[768,8,128]{2,1,0:T(8,128)(2,1)} %bitcast.6), calls=%async_computation.3 | async-start | bytes 3145728 | tf_op jit(solution)/shard_map/all_to_all | solution.py:477
  108.7 2.9 %collective-permute-start.13 = (bf16[8,512,128]{2,1,0:T(8,128)(2,1)}, bf16[8,512,128]{2,1,0:T(8,128)(2,1)S(1)}, u32[]{:S(2)}, u32[]{:S(2)}) collective-permute-start(bf16[8,512,128]{2,1,0:T(8,128)(2,1)} %collective-permute-done.11.refs_3_), channel_id=1, source_target_pairs={{0,32},{32,0},{64,96},{96,64},{1,33},{33,1},{65,97},{97,65},{2,34}... | collective-permute-start | bytes 3145736 | tf_op jit(solution)/shard_map/ppermute | solution.py:472
  108.7 28.3 %collective-permute-start.10 = (bf16[8,512,128]{2,1,0:T(8,128)(2,1)S(1)}, bf16[8,512,128]{2,1,0:T(8,128)(2,1)S(1)}, u32[]{:S(2)}, u32[]{:S(2)}) collective-permute-start(bf16[8,512,128]{2,1,0:T(8,128)(2,1)S(1)} %copy-done.1), channel_id=1, source_target_pairs={{0,64},{32,96},{64,0},{96,32},{1,65},{33,97},{65,1},{97,33},{2,66}... | collective-permute-start | bytes 3145736 | tf_op jit(solution)/shard_map/ppermute | solution.py:461
  111.5 1.2 copy-start.4
  112.8 1.2 copy-start.6
  128.3 26.3 %all-to-all-start.4 = ((bf16[768,8,128]{2,1,0:T(8,128)(2,1)}), bf16[768,8,128]{2,1,0:T(8,128)(2,1)}, u32[]{:S(2)}, u32[]{:S(2)}) async-start(bf16[768,8,128]{2,1,0:T(8,128)(2,1)} %bitcast.7), calls=%async_computation.4 | async-start | bytes 3145728 | tf_op jit(solution)/shard_map/all_to_all | solution.py:477
  136.9 2.7 %collective-permute-start.14 = (bf16[8,512,128]{2,1,0:T(8,128)(2,1)S(1)}, bf16[8,512,128]{2,1,0:T(8,128)(2,1)S(1)}, u32[]{:S(2)}, u32[]{:S(2)}) collective-permute-start(bf16[8,512,128]{2,1,0:T(8,128)(2,1)S(1)} %collective-permute-done.10.refs_2_), channel_id=1, source_target_pairs={{0,32},{32,0},{64,96},{96,64},{1,33},{33,1},{65,97},{97,65},{2,34}... | collective-permute-start | bytes 3145736 | tf_op jit(solution)/shard_map/ppermute | solution.py:472
  154.6 26.2 %all-to-all-start = ((bf16[768,8,128]{2,1,0:T(8,128)(2,1)}), bf16[768,8,128]{2,1,0:T(8,128)(2,1)S(1)}, u32[]{:S(2)}, u32[]{:S(2)}) async-start(bf16[768,8,128]{2,1,0:T(8,128)(2,1)} %bitcast.3), calls=%async_computation | async-start | bytes 3145728 | tf_op jit(solution)/shard_map/all_to_all | solution.py:477
  180.8 1.2 copy-start.12

commit v3 on v2

--- a/solution.py
+++ b/solution.py
@@ -382,28 +382,20 @@
     )(*parts)
 
 
-def place_body(part, _, out, held, in_sems, out_sems):
+def place_body(part, _, out, sems):
     rows = out.shape[0]
     peers = part.shape[0] // rows
     cols = out.shape[2] // peers
-    steps = peers // INNER
-    arrivals, departures = [], []
-    for n in range(steps):
-        some = pl.ds(n * INNER * rows, INNER * rows)
-        copy = pltpu.make_async_copy(part.at[some], held.at[some], in_sems.at[n])
+    copies = []
+    for m in range(peers):
+        copy = pltpu.make_async_copy(
+            part.at[pl.ds(m * rows, rows)],
+            out.at[:, :, pl.ds((m + 1) * cols - LANES, LANES)],
+            sems.at[m],
+        )
         copy.start()
-        arrivals.append(copy)
-    for n in range(steps):
-        arrivals[n].wait()
-        for m in range(n * INNER, (n + 1) * INNER):
-            copy = pltpu.make_async_copy(
-                held.at[pl.ds(m * rows, rows)],
-                out.at[:, :, pl.ds((m + 1) * cols - LANES, LANES)],
-                out_sems.at[m],
-            )
-            copy.start()
-            departures.append(copy)
-    for copy in departures:
+        copies.append(copy)
+    for copy in copies:
         copy.wait()
 
 
@@ -412,15 +404,11 @@
     return pl.pallas_call(
         place_body,
         out_shape=jax.ShapeDtypeStruct(whole.shape, whole.dtype),
-        in_specs=[pl.BlockSpec(memory_space=pl.ANY)] * 2,
+        in_specs=[pl.BlockSpec(memory_space=pltpu.VMEM), pl.BlockSpec(memory_space=pl.ANY)],
         out_specs=pl.BlockSpec(memory_space=pl.ANY),
-        scratch_shapes=[
-            pltpu.VMEM(part.shape, jnp.bfloat16),
-            pltpu.SemaphoreType.DMA((peers // INNER,)),
-            pltpu.SemaphoreType.DMA((peers,)),
-        ],
+        scratch_shapes=[pltpu.SemaphoreType.DMA((peers,))],
         input_output_aliases={1: 0},
-        compiler_params=pltpu.CompilerParams(vmem_limit_bytes=VMEM),
+        compiler_params=pltpu.CompilerParams(vmem_limit_bytes=8 << 20),
         cost_estimate=pl.CostEstimate(flops=0, bytes_accessed=4 * part.size, transcendentals=0),
     )(part, whole)
 
@@ -464,10 +452,8 @@
         if k in (0, last):
             own_part = part if k == 0 else lax.optimization_barrier((part, gamma))[0]
             partial = density(table, ids, (0, 2), (own_part, beside), virt, occ, ends=False)
-        before = (mine[1], partial, *besides[1:]) if k == 0 else (gamma, partial) if k == last else (gamma,)
+        before = (mine[1], partial) if k == 0 else (gamma, partial) if k == last else (gamma,)
         across, *before = lax.optimization_barrier((across,) + before)
-        if k == 0:
-            besides[1:] = before[2:]
         acrosses.append(across)
         diagonal = lax.ppermute(across, "occ", core_pairs)
         if partial is None:

time: 186 us -> 181 us (0.973)
  local copies, waits for them, and re-layouts: 6.85 us -> 0.02 us
  waiting for transfers between devices: 80.8 us -> 84.7 us
    unnamed x26 -> x8, local copies, waits for them, and re-layouts: 6.85 us -> 0.02 us
    all_to_all x5, waiting for transfers between devices: 50.4 us -> 52.4 us  [local(): lax.all_to_all(gamma.reshape(virt_count, OCC, -1), ('occ', 'aux'), split_...]
  transfers between devices with their start and end apart: 20 -> 20, of which waited for: 14 -> 14; matrix products, arithmetic and copies ran while one was open for 0% -> 0% of each run, Pallas kernels for 26% -> 27%
where the time goes in v3:
time: 181 us; the launch traced here: 180 us
  waiting for transfers between devices  84.7 us (47%)
  Pallas kernels  53.5 us (30%)
  starting transfers between devices  40.5 us (22%)
    all_to_all x5, waiting for transfers between devices, local(): lax.all_to_all(gamma.reshape(virt_count, OCC, -1), ('occ', 'aux'), split_...  52.4 us
    pallas_call x7, Pallas kernels, density(): pl.pallas_call(functools.partial(density_body, slabs, begins, ends), out_...  35.6 us
    all_to_all x5, starting transfers between devices, local(): lax.all_to_all(gamma.reshape(virt_count, OCC, -1), ('occ', 'aux'), split_...  30.6 us
    ppermute x5, waiting for transfers between devices, local(): across = lax.ppermute(sent, 'occ', chip_pairs)  24.9 us
    ppermute x5, starting transfers between devices, local(): across = lax.ppermute(sent, 'occ', chip_pairs)  8.99 us
    pallas_call x1, Pallas kernels, rest_pack(): pl.pallas_call(rest_body, out_shape=[jax.ShapeDtypeStruct((2, half_rows,...  7.45 us
    ppermute x5, waiting for transfers between devices, local(): diagonal = lax.ppermute(across, 'occ', core_pairs)  7.4 us
    pallas_call x1, Pallas kernels, assemble(): pl.pallas_call(assemble_body, out_shape=jax.ShapeDtypeStruct(shape, jnp.b...  5.71 us
  transfers between devices with their start and end apart: 20, of which 14 were waited for; matrix products, arithmetic and copies ran while one was open for 0% of the time, Pallas kernels for 27%

profile of v3, /device:TPU:2, one launch (start us, length us, event | category | flops | bytes accessed | tf_op | source)
XLA Modules:
  0.0 179.7 jit_solution(2881403705538742227)
XLA Ops:
  0.0 3.4 %shard_map.46.refs_2_ = bf16[8,512,128]{2,1,0:T(8,128)(2,1)} custom-call(s32[4,6]{1,0:T(4,128)} %mask_ref.3, bf16[768,8,640]{2,1,0:T(8,128)(2,1)} %x_ref.3), custom_call_target="tpu_custom_call" | custom-call | flops 536870912 | bytes 2097152 | tf_op jit(solution)/shard_map/pallas_call | solution.py:91
  3.4 0.1 collective-permute-start.1
  3.5 2.0 %collective-permute-start = (bf16[8,512,128]{2,1,0:T(8,128)(2,1)}, bf16[8,512,128]{2,1,0:T(8,128)(2,1)S(1)}, u32[]{:S(2)}, u32[]{:S(2)}) collective-permute-start(bf16[8,512,128]{2,1,0:T(8,128)(2,1)} %shard_map.46.refs_2_), channel_id=1, source_target_pairs={{0,64},{32,96},{64,0},{96,32},{1,65},{33,97},{65,1},{97,33},{2,66}... | collective-permute-start | bytes 3145736 | tf_op jit(solution)/shard_map/ppermute | solution.py:449
  5.5 0.6 pad_add_fusion.ids_ref.refs_1_
  6.1 7.4 %shard_map.47 = (bf16[2,384,512]{2,1,0:T(8,128)(2,1)}, bf16[2,128,512]{2,1,0:T(8,128)(2,1)}, s32[4,6]{1,0:T(4,128)}, bf16[8,512,128]{2,1,0:T(8,128)(2,1)}, bf16[...) custom-call(s32[4,6]{1,0:T(4,128)} %mask_ref.3, ...), custom_call_target="tpu_custom_call" | custom-call | flops 3221225472 | bytes 12582912 | tf_op jit(solution)/shard_map/pallas_call | solution.py:161
  13.5 0.0 collective-permute-done.1.refs_3_
  13.5 3.9 %shard_map.48.refs_6_ = f32[2,8,384,128]{3,2,1,0:T(8,128)S(1)} custom-call(s32[4,6]{1,0:T(4,128)} %get-tuple-element.27.refs_0_, s32[2]{0:T(128)S(1)} %copy-done.2, bf16[8,512,128]{2,1,0:T(8,128)(2,1)S(1)} %copy-done, bf16[8,512,128]{2,1,0:T(8,128)(2,1)S(1)} %collective-permute-done.1.refs_3_, bf16[2,384,512]{2,1,0:T(8,128)(2,1)} %get-tuple-element.31.refs_4_.refs_6_, ...), custom_call_target="tpu_custom_call" | custom-call | flops 1207959552 | bytes 3670016 | tf_op jit(solution)/shard_map/pallas_call | solution.py:292
  17.4 12.0 %collective-permute-done.refs_2_ = bf16[8,512,128]{2,1,0:T(8,128)(2,1)S(1)} collective-permute-done((bf16[8,512,128]{2,1,0:T(8,128)(2,1)}, bf16[8,512,128]{2,1,0:T(8,128)(2,1)S(1)}, u32[]{:S(2)}, u32[]{:S(2)}) %collective-permute-start) | collective-permute-done | bytes 1048608 | tf_op jit(solution)/shard_map/ppermute | solution.py:449
  29.4 0.0 collective-permute-start.4
  29.4 1.8 collective-permute-start.3
  31.2 0.9 collective-permute-done.4.refs_3_
  32.1 4.8 %shard_map.49 = bf16[6144,128]{1,0:T(8,128)(2,1)} custom-call(s32[4,6]{1,0:T(4,128)} %get-tuple-element.27.refs_0_, s32[2]{0:T(128)S(1)} %copy-done.2, bf16[8,512,128]{2,1,0:T(8,128)(2,1)S(1)} %collective-permute-done.refs_2_, bf16[8,512,128]{2,1,0:T(8,128)(2,1)S(1)} %collective-permute-done.4.refs_3_, ...), custom_call_target="tpu_custom_call" | custom-call | flops 1207959552 | bytes 3670016 | tf_op jit(solution)/shard_map/pallas_call | solution.py:292
  36.9 11.1 %all-to-all-start.1 = ((bf16[768,8,128]{2,1,0:T(8,128)(2,1)}), bf16[768,8,128]{2,1,0:T(8,128)(2,1)}, u32[]{:S(2)}, u32[]{:S(2)}) async-start(bf16[768,8,128]{2,1,0:T(8,128)(2,1)} %bitcast.4), calls=%async_computation.1 | async-start | bytes 3145728 | tf_op jit(solution)/shard_map/all_to_all | solution.py:463
  48.1 0.1 collective-permute-start.5
  48.2 7.0 %collective-permute-done.3.refs_3_ = bf16[8,512,128]{2,1,0:T(8,128)(2,1)S(1)} collective-permute-done((bf16[8,512,128]{2,1,0:T(8,128)(2,1)}, bf16[8,512,128]{2,1,0:T(8,128)(2,1)S(1)}, u32[]{:S(2)}, u32[]{:S(2)}) %collective-permute-start.3) | collective-permute-done | bytes 1048608 | tf_op jit(solution)/shard_map/ppermute | solution.py:449
  55.2 0.0 collective-permute-start.6
  55.2 1.7 collective-permute-start.2
  57.0 0.0 collective-permute-done.5.refs_4_
  57.0 0.9 collective-permute-done.6.refs_5_
  57.9 6.1 %shard_map.50 = bf16[6144,128]{1,0:T(8,128)(2,1)} custom-call(s32[4,6]{1,0:T(4,128)} %get-tuple-element.27.refs_0_, s32[2]{0:T(128)S(1)} %copy-done.2, bf16[8,512,128]{2,1,0:T(8,128)(2,1)} %get-tuple-element.30.refs_2_, bf16[8,512,128]{2,1,0:T(8,128)(2,1)S(1)} %collective-permute-done.3.refs_3_, bf16[8,512,128]{2,1,0:T(8,128)(2,1)S(1)} %collective-permute-done.5.refs_4_, ...), custom_call_target="tpu_custom_call" | custom-call | flops 2415919104 | bytes 5767168 | tf_op jit(solution)/shard_map/pallas_call | solution.py:292
  64.0 8.3 %all-to-all-done.1.refs_0_ = bf16[768,8,128]{2,1,0:T(8,128)(2,1)} async-done(((bf16[768,8,128]{2,1,0:T(8,128)(2,1)}), bf16[768,8,128]{2,1,0:T(8,128)(2,1)}, u32[]{:S(2)}, u32[]{:S(2)}) %all-to-all-start.1) | async-done | bytes 1572896 | tf_op jit(solution)/shard_map/all_to_all | solution.py:463
  72.3 4.6 %all-to-all-start.2 = ((bf16[768,8,128]{2,1,0:T(8,128)(2,1)}), bf16[768,8,128]{2,1,0:T(8,128)(2,1)}, u32[]{:S(2)}, u32[]{:S(2)}) async-start(bf16[768,8,128]{2,1,0:T(8,128)(2,1)} %bitcast.5), calls=%async_computation.2 | async-start | bytes 3145728 | tf_op jit(solution)/shard_map/all_to_all | solution.py:463
  76.9 0.1 collective-permute-start.9
  77.0 3.7 %collective-permute-done.2.refs_3_ = bf16[8,512,128]{2,1,0:T(8,128)(2,1)S(1)} collective-permute-done((bf16[8,512,128]{2,1,0:T(8,128)(2,1)S(1)}, bf16[8,512,128]{2,1,0:T(8,128)(2,1)S(1)}, u32[]{:S(2)}, u32[]{:S(2)}) %collective-permute-start.2) | collective-permute-done | bytes 1048608 | tf_op jit(solution)/shard_map/ppermute | solution.py:449
  80.8 0.0 collective-permute-start.10
  80.8 1.7 collective-permute-start.8
  82.5 0.0 collective-permute-done.9.refs_4_
  82.5 0.9 collective-permute-done.10.refs_5_
  83.4 5.9 %shard_map.51 = bf16[6144,128]{1,0:T(8,128)(2,1)} custom-call(s32[4,6]{1,0:T(4,128)} %get-tuple-element.27.refs_0_, s32[2]{0:T(128)S(1)} %copy-done.2, bf16[8,512,128]{2,1,0:T(8,128)(2,1)S(1)} %copy-done.3, bf16[8,512,128]{2,1,0:T(8,128)(2,1)S(1)} %collective-permute-done.2.refs_3_, bf16[8,512,128]{2,1,0:T(8,128)(2,1)S(1)} %collective-permute-done.9.refs_4_, ...), custom_call_target="tpu_custom_call" | custom-call | flops 2415919104 | bytes 5767168 | tf_op jit(solution)/shard_map/pallas_call | solution.py:292
  89.3 9.8 %all-to-all-done.2.refs_1_ = bf16[768,8,128]{2,1,0:T(8,128)(2,1)} async-done(((bf16[768,8,128]{2,1,0:T(8,128)(2,1)}), bf16[768,8,128]{2,1,0:T(8,128)(2,1)}, u32[]{:S(2)}, u32[]{:S(2)}) %all-to-all-start.2) | async-done | bytes 1572896 | tf_op jit(solution)/shard_map/all_to_all | solution.py:463
  99.1 5.4 %all-to-all-start.3 = ((bf16[768,8,128]{2,1,0:T(8,128)(2,1)}), bf16[768,8,128]{2,1,0:T(8,128)(2,1)}, u32[]{:S(2)}, u32[]{:S(2)}) async-start(bf16[768,8,128]{2,1,0:T(8,128)(2,1)} %bitcast.6), calls=%async_computation.3 | async-start | bytes 3145728 | tf_op jit(solution)/shard_map/all_to_all | solution.py:463
  104.5 0.1 collective-permute-start.11
  104.6 2.1 %collective-permute-done.8.refs_3_ = bf16[8,512,128]{2,1,0:T(8,128)(2,1)} collective-permute-done((bf16[8,512,128]{2,1,0:T(8,128)(2,1)}, bf16[8,512,128]{2,1,0:T(8,128)(2,1)}, u32[]{:S(2)}, u32[]{:S(2)}) %collective-permute-start.8) | collective-permute-done | bytes 1048608 | tf_op jit(solution)/shard_map/ppermute | solution.py:449
  106.7 0.5 collective-permute-start.13
  107.2 1.7 collective-permute-start.7
  108.9 2.0 %collective-permute-done.12.refs_5_ = bf16[8,512,128]{2,1,0:T(8,128)(2,1)S(1)} collective-permute-done((bf16[8,512,128]{2,1,0:T(8,128)(2,1)}, bf16[8,512,128]{2,1,0:T(8,128)(2,1)S(1)}, u32[]{:S(2)}, u32[]{:S(2)}) %collective-permute-start.12) | collective-permute-done | bytes 1048608 | tf_op jit(solution)/shard_map/ppermute | solution.py:458
  111.0 6.1 %shard_map.52 = bf16[6144,128]{1,0:T(8,128)(2,1)} custom-call(s32[4,6]{1,0:T(4,128)} %get-tuple-element.27.refs_0_, s32[2]{0:T(128)S(1)} %copy-done.2, bf16[8,512,128]{2,1,0:T(8,128)(2,1)} %get-tuple-element.40.refs_2_, bf16[8,512,128]{2,1,0:T(8,128)(2,1)} %collective-permute-done.8.refs_3_, bf16[8,512,128]{2,1,0:T(8,128)(2,1)S(1)} %collective-permute-done.11.refs_4_, ...), custom_call_target="tpu_custom_call" | custom-call | flops 2415919104 | bytes 5767168 | tf_op jit(solution)/shard_map/pallas_call | solution.py:292
  117.1 8.8 %all-to-all-done.3.refs_2_ = bf16[768,8,128]{2,1,0:T(8,128)(2,1)} async-done(((bf16[768,8,128]{2,1,0:T(8,128)(2,1)}), bf16[768,8,128]{2,1,0:T(8,128)(2,1)}, u32[]{:S(2)}, u32[]{:S(2)}) %all-to-all-start.3) | async-done | bytes 1572896 | tf_op jit(solution)/shard_map/all_to_all | solution.py:463
  125.9 4.8 %all-to-all-start.4 = ((bf16[768,8,128]{2,1,0:T(8,128)(2,1)}), bf16[768,8,128]{2,1,0:T(8,128)(2,1)}, u32[]{:S(2)}, u32[]{:S(2)}) async-start(bf16[768,8,128]{2,1,0:T(8,128)(2,1)} %bitcast.7), calls=%async_computation.4 | async-start | bytes 3145728 | tf_op jit(solution)/shard_map/all_to_all | solution.py:463
  130.7 3.9 %shard_map.53.refs_6_ = f32[2,8,384,128]{3,2,1,0:T(8,128)S(1)} custom-call(s32[4,6]{1,0:T(4,128)} %get-tuple-element.27.refs_0_, s32[2]{0:T(128)S(1)} %copy-done.2, bf16[8,512,128]{2,1,0:T(8,128)(2,1)S(1)} %copy-done.1, bf16[8,512,128]{2,1,0:T(8,128)(2,1)S(1)} %collective-permute-done.13.refs_3_, bf16[2,384,512]{2,1,0:T(8,128)(2,1)} %get-tuple-element.31.refs_4_.refs_6_, ...), custom_call_target="tpu_custom_call" | custom-call | flops 1207959552 | bytes 3670016 | tf_op jit(solution)/shard_map/pallas_call | solution.py:292
  134.6 0.1 collective-permute-start.14
  134.7 2.6 %collective-permute-done.14.refs_3_ = bf16[8,512,128]{2,1,0:T(8,128)(2,1)S(1)} collective-permute-done((bf16[8,512,128]{2,1,0:T(8,128)(2,1)S(1)}, bf16[8,512,128]{2,1,0:T(8,128)(2,1)S(1)}, u32[]{:S(2)}, u32[]{:S(2)}) %collective-permute-start.14) | collective-permute-done | bytes 1048608 | tf_op jit(solution)/shard_map/ppermute | solution.py:458
  137.3 4.9 %shard_map.54 = bf16[6144,128]{1,0:T(8,128)(2,1)} custom-call(s32[4,6]{1,0:T(4,128)} %get-tuple-element.27.refs_0_, s32[2]{0:T(128)S(1)} %copy-done.2, bf16[8,512,128]{2,1,0:T(8,128)(2,1)S(1)} %collective-permute-done.7.refs_2_, bf16[8,512,128]{2,1,0:T(8,128)(2,1)S(1)} %collective-permute-done.14.refs_3_, ...), custom_call_target="tpu_custom_call" | custom-call | flops 1207959552 | bytes 3670016 | tf_op jit(solution)/shard_map/pallas_call | solution.py:292
  142.2 10.0 %all-to-all-done.4.refs_3_ = bf16[768,8,128]{2,1,0:T(8,128)(2,1)} async-done(((bf16[768,8,128]{2,1,0:T(8,128)(2,1)}), bf16[768,8,128]{2,1,0:T(8,128)(2,1)}, u32[]{:S(2)}, u32[]{:S(2)}) %all-to-all-start.4) | async-done | bytes 1572896 | tf_op jit(solution)/shard_map/all_to_all | solution.py:463
  152.2 4.7 %all-to-all-start = ((bf16[768,8,128]{2,1,0:T(8,128)(2,1)}), bf16[768,8,128]{2,1,0:T(8,128)(2,1)S(1)}, u32[]{:S(2)}, u32[]{:S(2)}) async-start(bf16[768,8,128]{2,1,0:T(8,128)(2,1)} %bitcast.3), calls=%async_computation | async-start | bytes 3145728 | tf_op jit(solution)/shard_map/all_to_all | solution.py:463
  157.0 5.7 %shard_map.55._ = bf16[24,8,20480]{2,1,0:T(8,128)(2,1)} custom-call(bf16[768,8,128]{2,1,0:T(8,128)(2,1)} %all-to-all-done.1.refs_0_, bf16[768,8,128]{2,1,0:T(8,128)(2,1)} %all-to-all-done.2.refs_1_, bf16[768,8,128]{2,1,0:T(8,128)(2,1)} %all-to-all-done.3.refs_2_, bf16[768,8,128]{2,1,0:T(8,128)(2,1)} %all-to-all-done.4.refs_3_), custom_call_target="tpu_custom_call" | custom-call | bytes 15728640 | tf_op jit(solution)/shard_map/pallas_call | solution.py:367
  162.7 15.5 %all-to-all-done.part = bf16[768,8,128]{2,1,0:T(8,128)(2,1)S(1)} async-done(((bf16[768,8,128]{2,1,0:T(8,128)(2,1)}), bf16[768,8,128]{2,1,0:T(8,128)(2,1)S(1)}, u32[]{:S(2)}, u32[]{:S(2)}) %all-to-all-start) | async-done | bytes 1572896 | tf_op jit(solution)/shard_map/all_to_all | solution.py:463
  178.2 1.4 shard_map.56
  (12 shorter events, 0.0 us)
Async XLA Ops:
  3.4 10.2 %collective-permute-start.1 = (bf16[8,512,128]{2,1,0:T(8,128)(2,1)}, bf16[8,512,128]{2,1,0:T(8,128)(2,1)S(1)}, u32[]{:S(2)}, u32[]{:S(2)}) collective-permute-start(bf16[8,512,128]{2,1,0:T(8,128)(2,1)} %shard_map.46.refs_2_), channel_id=1, source_target_pairs={{0,32},{32,0},{64,96},{96,64},{1,33},{33,1},{65,97},{97,65},{2,34}... | collective-permute-start | bytes 3145736 | tf_op jit(solution)/shard_map/ppermute | solution.py:444
  3.5 25.9 %collective-permute-start = (bf16[8,512,128]{2,1,0:T(8,128)(2,1)}, bf16[8,512,128]{2,1,0:T(8,128)(2,1)S(1)}, u32[]{:S(2)}, u32[]{:S(2)}) collective-permute-start(bf16[8,512,128]{2,1,0:T(8,128)(2,1)} %shard_map.46.refs_2_), channel_id=1, source_target_pairs={{0,64},{32,96},{64,0},{96,32},{1,65},{33,97},{65,1},{97,33},{2,66}... | collective-permute-start | bytes 3145736 | tf_op jit(solution)/shard_map/ppermute | solution.py:449
  6.1 7.5 %copy-start = (bf16[8,512,128]{2,1,0:T(8,128)(2,1)S(1)}, bf16[8,512,128]{2,1,0:T(8,128)(2,1)}, u32[]{:S(2)}) copy-start(bf16[8,512,128]{2,1,0:T(8,128)(2,1)} %shard_map.46.refs_2_) | copy-start | bytes 3145732
  6.1 7.5 %copy-start.2 = (s32[2]{0:T(128)S(1)}, s32[2]{0:T(128)}, u32[]{:S(2)}) copy-start(s32[2]{0:T(128)} %pad_add_fusion.ids_ref.refs_1_) | copy-start | bytes 28
  29.4 2.7 %collective-permute-start.4 = (bf16[8,512,128]{2,1,0:T(8,128)(2,1)S(1)}, bf16[8,512,128]{2,1,0:T(8,128)(2,1)S(1)}, u32[]{:S(2)}, u32[]{:S(2)}) collective-permute-start(bf16[8,512,128]{2,1,0:T(8,128)(2,1)S(1)} %collective-permute-done.refs_2_), channel_id=1, source_target_pairs={{0,32},{32,0},{64,96},{96,64},{1,33},{33,1},{65,97},{97,65},{2,34}... | collective-permute-start | bytes 3145736 | tf_op jit(solution)/shard_map/ppermute | solution.py:458
  29.4 25.8 %collective-permute-start.3 = (bf16[8,512,128]{2,1,0:T(8,128)(2,1)}, bf16[8,512,128]{2,1,0:T(8,128)(2,1)S(1)}, u32[]{:S(2)}, u32[]{:S(2)}) collective-permute-start(bf16[8,512,128]{2,1,0:T(8,128)(2,1)} %get-tuple-element.30.refs_2_), channel_id=1, source_target_pairs={{0,64},{32,96},{64,0},{96,32},{1,65},{33,97},{65,1},{97,33},{2,66}... | collective-permute-start | bytes 3145736 | tf_op jit(solution)/shard_map/ppermute | solution.py:449
  36.9 18.3 %copy-start.3 = (bf16[8,512,128]{2,1,0:T(8,128)(2,1)S(1)}, bf16[8,512,128]{2,1,0:T(8,128)(2,1)}, u32[]{:S(2)}) copy-start(bf16[8,512,128]{2,1,0:T(8,128)(2,1)} %get-tuple-element.34.refs_2_) | copy-start | bytes 3145732
  36.9 35.4 %all-to-all-start.1 = ((bf16[768,8,128]{2,1,0:T(8,128)(2,1)}), bf16[768,8,128]{2,1,0:T(8,128)(2,1)}, u32[]{:S(2)}, u32[]{:S(2)}) async-start(bf16[768,8,128]{2,1,0:T(8,128)(2,1)} %bitcast.4), calls=%async_computation.1 | async-start | bytes 3145728 | tf_op jit(solution)/shard_map/all_to_all | solution.py:463
  48.1 8.9 %collective-permute-start.5 = (bf16[8,512,128]{2,1,0:T(8,128)(2,1)}, bf16[8,512,128]{2,1,0:T(8,128)(2,1)S(1)}, u32[]{:S(2)}, u32[]{:S(2)}) collective-permute-start(bf16[8,512,128]{2,1,0:T(8,128)(2,1)} %get-tuple-element.30.refs_2_), channel_id=1, source_target_pairs={{0,32},{32,0},{64,96},{96,64},{1,33},{33,1},{65,97},{97,65},{2,34}... | collective-permute-start | bytes 3145736 | tf_op jit(solution)/shard_map/ppermute | solution.py:444
  55.2 2.7 %collective-permute-start.6 = (bf16[8,512,128]{2,1,0:T(8,128)(2,1)S(1)}, bf16[8,512,128]{2,1,0:T(8,128)(2,1)S(1)}, u32[]{:S(2)}, u32[]{:S(2)}) collective-permute-start(bf16[8,512,128]{2,1,0:T(8,128)(2,1)S(1)} %collective-permute-done.3.refs_3_), channel_id=1, source_target_pairs={{0,32},{32,0},{64,96},{96,64},{1,33},{33,1},{65,97},{97,65},{2,34}... | collective-permute-start | bytes 3145736 | tf_op jit(solution)/shard_map/ppermute | solution.py:458
  55.2 25.6 %collective-permute-start.2 = (bf16[8,512,128]{2,1,0:T(8,128)(2,1)S(1)}, bf16[8,512,128]{2,1,0:T(8,128)(2,1)S(1)}, u32[]{:S(2)}, u32[]{:S(2)}) collective-permute-start(bf16[8,512,128]{2,1,0:T(8,128)(2,1)S(1)} %copy-done.3), channel_id=1, source_target_pairs={{0,64},{32,96},{64,0},{96,32},{1,65},{33,97},{65,1},{97,33},{2,66}... | collective-permute-start | bytes 3145736 | tf_op jit(solution)/shard_map/ppermute | solution.py:449
  72.3 26.7 %all-to-all-start.2 = ((bf16[768,8,128]{2,1,0:T(8,128)(2,1)}), bf16[768,8,128]{2,1,0:T(8,128)(2,1)}, u32[]{:S(2)}, u32[]{:S(2)}) async-start(bf16[768,8,128]{2,1,0:T(8,128)(2,1)} %bitcast.5), calls=%async_computation.2 | async-start | bytes 3145728 | tf_op jit(solution)/shard_map/all_to_all | solution.py:463
  76.9 5.6 %collective-permute-start.9 = (bf16[8,512,128]{2,1,0:T(8,128)(2,1)S(1)}, bf16[8,512,128]{2,1,0:T(8,128)(2,1)S(1)}, u32[]{:S(2)}, u32[]{:S(2)}) collective-permute-start(bf16[8,512,128]{2,1,0:T(8,128)(2,1)S(1)} %copy-done.3), channel_id=1, source_target_pairs={{0,32},{32,0},{64,96},{96,64},{1,33},{33,1},{65,97},{97,65},{2,34}... | collective-permute-start | bytes 3145736 | tf_op jit(solution)/shard_map/ppermute | solution.py:444
  80.8 2.7 %collective-permute-start.10 = (bf16[8,512,128]{2,1,0:T(8,128)(2,1)S(1)}, bf16[8,512,128]{2,1,0:T(8,128)(2,1)S(1)}, u32[]{:S(2)}, u32[]{:S(2)}) collective-permute-start(bf16[8,512,128]{2,1,0:T(8,128)(2,1)S(1)} %collective-permute-done.2.refs_3_), channel_id=1, source_target_pairs={{0,32},{32,0},{64,96},{96,64},{1,33},{33,1},{65,97},{97,65},{2,34}... | collective-permute-start | bytes 3145736 | tf_op jit(solution)/shard_map/ppermute | solution.py:458
  80.8 25.9 %collective-permute-start.8 = (bf16[8,512,128]{2,1,0:T(8,128)(2,1)}, bf16[8,512,128]{2,1,0:T(8,128)(2,1)}, u32[]{:S(2)}, u32[]{:S(2)}) collective-permute-start(bf16[8,512,128]{2,1,0:T(8,128)(2,1)} %get-tuple-element.40.refs_2_), channel_id=1, source_target_pairs={{0,64},{32,96},{64,0},{96,32},{1,65},{33,97},{65,1},{97,33},{2,66}... | collective-permute-start | bytes 3145736 | tf_op jit(solution)/shard_map/ppermute | solution.py:449
  99.1 7.6 %copy-start.1 = (bf16[8,512,128]{2,1,0:T(8,128)(2,1)S(1)}, bf16[8,512,128]{2,1,0:T(8,128)(2,1)}, u32[]{:S(2)}) copy-start(bf16[8,512,128]{2,1,0:T(8,128)(2,1)} %get-tuple-element.42.refs_2_) | copy-start | bytes 3145732
  99.1 26.8 %all-to-all-start.3 = ((bf16[768,8,128]{2,1,0:T(8,128)(2,1)}), bf16[768,8,128]{2,1,0:T(8,128)(2,1)}, u32[]{:S(2)}, u32[]{:S(2)}) async-start(bf16[768,8,128]{2,1,0:T(8,128)(2,1)} %bitcast.6), calls=%async_computation.3 | async-start | bytes 3145728 | tf_op jit(solution)/shard_map/all_to_all | solution.py:463
  104.5 4.5 %collective-permute-start.11 = (bf16[8,512,128]{2,1,0:T(8,128)(2,1)}, bf16[8,512,128]{2,1,0:T(8,128)(2,1)S(1)}, u32[]{:S(2)}, u32[]{:S(2)}) collective-permute-start(bf16[8,512,128]{2,1,0:T(8,128)(2,1)} %get-tuple-element.40.refs_2_), channel_id=1, source_target_pairs={{0,32},{32,0},{64,96},{96,64},{1,33},{33,1},{65,97},{97,65},{2,34}... | collective-permute-start | bytes 3145736 | tf_op jit(solution)/shard_map/ppermute | solution.py:444
  106.7 4.3 %collective-permute-start.12 = (bf16[8,512,128]{2,1,0:T(8,128)(2,1)}, bf16[8,512,128]{2,1,0:T(8,128)(2,1)S(1)}, u32[]{:S(2)}, u32[]{:S(2)}) collective-permute-start(bf16[8,512,128]{2,1,0:T(8,128)(2,1)} %collective-permute-done.8.refs_3_), channel_id=1, source_target_pairs={{0,32},{32,0},{64,96},{96,64},{1,33},{33,1},{65,97},{97,65},{2,34}... | collective-permute-start | bytes 3145736 | tf_op jit(solution)/shard_map/ppermute | solution.py:458
  106.7 24.0 %collective-permute-start.13 = (bf16[8,512,128]{2,1,0:T(8,128)(2,1)S(1)}, bf16[8,512,128]{2,1,0:T(8,128)(2,1)S(1)}, u32[]{:S(2)}, u32[]{:S(2)}) collective-permute-start(bf16[8,512,128]{2,1,0:T(8,128)(2,1)S(1)} %copy-done.1), channel_id=1, source_target_pairs={{0,32},{32,0},{64,96},{96,64},{1,33},{33,1},{65,97},{97,65},{2,34}... | collective-permute-start | bytes 3145736 | tf_op jit(solution)/shard_map/ppermute | solution.py:444
  107.2 27.4 %collective-permute-start.7 = (bf16[8,512,128]{2,1,0:T(8,128)(2,1)S(1)}, bf16[8,512,128]{2,1,0:T(8,128)(2,1)S(1)}, u32[]{:S(2)}, u32[]{:S(2)}) collective-permute-start(bf16[8,512,128]{2,1,0:T(8,128)(2,1)S(1)} %copy-done.1), channel_id=1, source_target_pairs={{0,64},{32,96},{64,0},{96,32},{1,65},{33,97},{65,1},{97,33},{2,66}... | collective-permute-start | bytes 3145736 | tf_op jit(solution)/shard_map/ppermute | solution.py:449
  125.9 26.3 %all-to-all-start.4 = ((bf16[768,8,128]{2,1,0:T(8,128)(2,1)}), bf16[768,8,128]{2,1,0:T(8,128)(2,1)}, u32[]{:S(2)}, u32[]{:S(2)}) async-start(bf16[768,8,128]{2,1,0:T(8,128)(2,1)} %bitcast.7), calls=%async_computation.4 | async-start | bytes 3145728 | tf_op jit(solution)/shard_map/all_to_all | solution.py:463
  134.6 2.7 %collective-permute-start.14 = (bf16[8,512,128]{2,1,0:T(8,128)(2,1)S(1)}, bf16[8,512,128]{2,1,0:T(8,128)(2,1)S(1)}, u32[]{:S(2)}, u32[]{:S(2)}) collective-permute-start(bf16[8,512,128]{2,1,0:T(8,128)(2,1)S(1)} %collective-permute-done.7.refs_2_), channel_id=1, source_target_pairs={{0,32},{32,0},{64,96},{96,64},{1,33},{33,1},{65,97},{97,65},{2,34}... | collective-permute-start | bytes 3145736 | tf_op jit(solution)/shard_map/ppermute | solution.py:458
  152.2 25.9 %all-to-all-start = ((bf16[768,8,128]{2,1,0:T(8,128)(2,1)}), bf16[768,8,128]{2,1,0:T(8,128)(2,1)S(1)}, u32[]{:S(2)}, u32[]{:S(2)}) async-start(bf16[768,8,128]{2,1,0:T(8,128)(2,1)} %bitcast.3), calls=%async_computation | async-start | bytes 3145728 | tf_op jit(solution)/shard_map/all_to_all | solution.py:463

commit v4 on v3

--- a/solution.py
+++ b/solution.py
@@ -70,14 +70,20 @@
     tile = tiles.shape[1]
     own = lax.axis_index("occ")
     arrivals, departures = [], []
+    half = tile // 2
     for q in range(CAP):
-        at = pl.multiple_of(tile_of(mask_ref, own, q) * tile, tile)
-        copy = pltpu.make_async_copy(x_ref.at[pl.ds(at, tile), :, pl.ds(0, LANES)], tiles.at[q], in_sems.at[q])
-        copy.start()
-        arrivals.append(copy)
+        at = tile_of(mask_ref, own, q) * tile
+        for n in range(2):
+            rows = pl.ds(pl.multiple_of(at + n * half, half), half)
+            copy = pltpu.make_async_copy(
+                x_ref.at[rows, :, pl.ds(0, LANES)], tiles.at[q, pl.ds(n * half, half)], in_sems.at[2 * q + n]
+            )
+            copy.start()
+            arrivals.append(copy)
     perm = permutation(False)
     for q in range(CAP):
-        arrivals[q].wait()
+        arrivals[2 * q].wait()
+        arrivals[2 * q + 1].wait()
         pack_rows(perm, tiles.at[q], [packed.at[q]], 0)
         copy = pltpu.make_async_copy(packed.at[q], out.at[:, pl.ds(q * tile, tile), :], out_sems.at[q])
         copy.start()
@@ -99,7 +105,7 @@
             scratch_shapes=[
                 pltpu.VMEM((CAP, tile, OCC, LANES), jnp.bfloat16),
                 pltpu.VMEM((CAP, OCC, tile, LANES), jnp.bfloat16),
-                pltpu.SemaphoreType.DMA((CAP,)),
+                pltpu.SemaphoreType.DMA((2 * CAP,)),
                 pltpu.SemaphoreType.DMA((CAP,)),
             ],
         ),
@@ -186,13 +192,21 @@
     return packs, virt, occ, table
 
 
-def density_body(slabs, begins, ends, *refs):
+def density_body(slabs, begins, ends, only, *refs):
+    if only is None:
+        density_terms(slabs, begins, ends, *refs)
+    else:
+        @pl.when(refs[1][0] % 2 == only)
+        def _():
+            density_terms(slabs, begins, ends, *refs)
+
+
+def density_terms(slabs, begins, ends, *refs):
     table_ref, ids_ref, *refs = refs
     count = len(slabs)
     sources, (virt_in, occ_in), refs = refs[:count], refs[count:count + 2], refs[count + 2:]
-    if not begins:
-        partial, *refs = refs
-    out, packs, virt_ref, occ_ref, total, mixed, result, in_sems, out_sems = refs
+    partial = refs[0]
+    out, packs, virt_ref, occ_ref, total, mixed, result, in_sems, out_sems = refs[-9:]
     depth = sources[0].shape[1]
     half_rows = virt_ref.shape[1]
     blocks = half_rows // SPAN
@@ -281,16 +295,17 @@
         copy.wait()
 
 
-def density(table, ids, slabs, packs, virt, occ, partial=None, ends=True):
+def density(table, ids, slabs, packs, virt, occ, partial=None, ends=True, only=None, into=None):
     depth = packs[0].shape[1]
     half_rows = virt.shape[1]
     rows = 2 * half_rows * OCC
     sums = (2, OCC, half_rows, LANES)
     begins = partial is None
     share = len(slabs) * LANES
-    extra = [] if begins else [partial]
+    extra = [array for array in (partial, into) if array is not None]
+    aliases = {} if into is None else {2 + len(slabs) + 2: 0}
     return pl.pallas_call(
-        functools.partial(density_body, slabs, begins, ends),
+        functools.partial(density_body, slabs, begins, ends, only),
         out_shape=jax.ShapeDtypeStruct((rows, LANES), jnp.bfloat16) if ends else jax.ShapeDtypeStruct(sums, jnp.float32),
         grid_spec=pltpu.PrefetchScalarGridSpec(
             num_scalar_prefetch=2,
@@ -308,6 +323,7 @@
                 pltpu.SemaphoreType.DMA((2 * half_rows // SPAN,)),
             ],
         ),
+        input_output_aliases=aliases,
         compiler_params=pltpu.CompilerParams(vmem_limit_bytes=24 << 20),
         cost_estimate=pl.CostEstimate(
             flops=share * (rows * depth // 2 + 2 * rows * ROWS),
@@ -439,7 +455,7 @@
     chip_pairs = [(s, s ^ 2) for s in range(SLABS)]
     core_pairs = [(s, s ^ 1) for s in range(SLABS)]
     groups = exchange_groups(peers)
-    done, acrosses = [], []
+    done, acrosses, early = [], [], None
     last = len(mine) - 1
     besides = [lax.ppermute(part, "occ", core_pairs) for part in mine]
     for k, part in enumerate(mine):
@@ -451,7 +467,9 @@
         partial = None
         if k in (0, last):
             own_part = part if k == 0 else lax.optimization_barrier((part, gamma))[0]
-            partial = density(table, ids, (0, 2), (own_part, beside), virt, occ, ends=False)
+            partial = density(
+                table, ids, (0, 2), (own_part, beside), virt, occ, ends=False, only=1 if k else None, into=early
+            )
         before = (mine[1], partial) if k == 0 else (gamma, partial) if k == last else (gamma,)
         across, *before = lax.optimization_barrier((across,) + before)
         acrosses.append(across)
@@ -460,6 +478,11 @@
             gamma = density(table, ids, (0, 1, 2, 3), (part, across, beside, diagonal), virt, occ)
         else:
             gamma = density(table, ids, (1, 3), (across, diagonal), virt, occ, partial=before[1])
+        if k == 0:
+            own_part, _ = lax.optimization_barrier((mine[last], gamma))
+            beside = lax.ppermute(mine[last], "occ", core_pairs)
+            early = density(table, ids, (0, 2), (own_part, beside), virt, occ, ends=False, only=0)
+            gamma, early = lax.optimization_barrier((gamma, early))
         done.append(lax.all_to_all(
             gamma.reshape(virt_count, OCC, -1), ("occ", "aux"),
             split_axis=0, concat_axis=0, axis_index_groups=groups, tiled=True,

time: 181 us -> 184 us (1.017)
  waiting for transfers between devices: 84.7 us -> 69.7 us
  local copies, waits for them, and re-layouts: 0.02 us -> 9.56 us
  Pallas kernels: 53.5 us -> 61.4 us
    unnamed x8 -> x26, local copies, waits for them, and re-layouts: 0.02 us -> 9.56 us
    ppermute x5, waiting for transfers between devices: 24.9 us -> 15.5 us  [local(): across = lax.ppermute(sent, 'occ', chip_pairs)]
    pallas_call x7 -> x8, Pallas kernels: 35.6 us -> 43.4 us  [density(): pl.pallas_call(functools.partial(density_body, slabs, begins, ends, only)...]
    all_to_all x5, waiting for transfers between devices: 52.4 us -> 46.5 us  [local(): lax.all_to_all(gamma.reshape(virt_count, OCC, -1), ('occ', 'aux'), split_...]
  transfers between devices with their start and end apart: 20 -> 20, of which waited for: 14 -> 15; matrix products, arithmetic and copies ran while one was open for 0% -> 0% of each run, Pallas kernels for 27% -> 31%
where the time goes in v4:
time: 184 us; the launch traced here: 182 us
  waiting for transfers between devices  69.7 us (38%)
  Pallas kernels  61.4 us (33%)
  starting transfers between devices  40.6 us (22%)
  local copies, waits for them, and re-layouts  9.56 us (5%)
    all_to_all x5, waiting for transfers between devices, local(): lax.all_to_all(gamma.reshape(virt_count, OCC, -1), ('occ', 'aux'), split_...  46.5 us
    pallas_call x8, Pallas kernels, density(): pl.pallas_call(functools.partial(density_body, slabs, begins, ends, only)...  43.4 us
    all_to_all x5, starting transfers between devices, local(): lax.all_to_all(gamma.reshape(virt_count, OCC, -1), ('occ', 'aux'), split_...  30.7 us
    ppermute x5, waiting for transfers between devices, local(): across = lax.ppermute(sent, 'occ', chip_pairs)  15.5 us
    unnamed x26, local copies, waits for them, and re-layouts  9.56 us
    ppermute x5, starting transfers between devices, local(): across = lax.ppermute(sent, 'occ', chip_pairs)  8.92 us
    pallas_call x1, Pallas kernels, rest_pack(): pl.pallas_call(rest_body, out_shape=[jax.ShapeDtypeStruct((2, half_rows,...  7.56 us
    ppermute x5, waiting for transfers between devices, local(): diagonal = lax.ppermute(across, 'occ', core_pairs)  7.01 us
  transfers between devices with their start and end apart: 20, of which 15 were waited for; matrix products, arithmetic and copies ran while one was open for 0% of the time, Pallas kernels for 31%

profile of v4, /device:TPU:2, one launch (start us, length us, event | category | flops | bytes accessed | tf_op | source)
XLA Modules:
  0.0 182.5 jit_solution(10859134101888889346)
XLA Ops:
  0.0 3.4 %shard_map.46.refs_2_ = bf16[8,512,128]{2,1,0:T(8,128)(2,1)} custom-call(s32[4,6]{1,0:T(4,128)} %mask_ref.3, bf16[768,8,640]{2,1,0:T(8,128)(2,1)} %x_ref.3), custom_call_target="tpu_custom_call" | custom-call | flops 536870912 | bytes 2097152 | tf_op jit(solution)/shard_map/pallas_call | solution.py:97
  3.4 0.1 collective-permute-start.1
  3.5 2.0 %collective-permute-start = (bf16[8,512,128]{2,1,0:T(8,128)(2,1)}, bf16[8,512,128]{2,1,0:T(8,128)(2,1)S(1)}, u32[]{:S(2)}, u32[]{:S(2)}) collective-permute-start(bf16[8,512,128]{2,1,0:T(8,128)(2,1)} %shard_map.46.refs_2_), channel_id=1, source_target_pairs={{0,64},{32,96},{64,0},{96,32},{1,65},{33,97},{65,1},{97,33},{2,66}... | collective-permute-start | bytes 3145736 | tf_op jit(solution)/shard_map/ppermute | solution.py:465
  5.5 0.7 pad_add_fusion.ids_ref.refs_1_
  6.2 7.6 %shard_map.47 = (bf16[2,384,512]{2,1,0:T(8,128)(2,1)}, bf16[2,128,512]{2,1,0:T(8,128)(2,1)}, s32[4,6]{1,0:T(4,128)}, bf16[8,512,128]{2,1,0:T(8,128)(2,1)}, bf16[...) custom-call(s32[4,6]{1,0:T(4,128)} %mask_ref.3, ...), custom_call_target="tpu_custom_call" | custom-call | flops 3221225472 | bytes 12582912 | tf_op jit(solution)/shard_map/pallas_call | solution.py:167
  13.8 4.0 %shard_map.48.refs_6_ = f32[2,8,384,128]{3,2,1,0:T(8,128)S(1)} custom-call(s32[4,6]{1,0:T(4,128)} %get-tuple-element.30.refs_0_, s32[2]{0:T(128)S(1)} %copy-done.10, bf16[8,512,128]{2,1,0:T(8,128)(2,1)S(1)} %copy-done.2, bf16[8,512,128]{2,1,0:T(8,128)(2,1)S(1)} %collective-permute-done.1.refs_3_, bf16[2,384,512]{2,1,0:T(8,128)(2,1)} %get-tuple-element.34.refs_4_.refs_6_, ...), custom_call_target="tpu_custom_call" | custom-call | flops 1207959552 | bytes 3670016 | tf_op jit(solution)/shard_map/pallas_call | solution.py:307
  17.8 11.7 %collective-permute-done.refs_2_ = bf16[8,512,128]{2,1,0:T(8,128)(2,1)S(1)} collective-permute-done((bf16[8,512,128]{2,1,0:T(8,128)(2,1)}, bf16[8,512,128]{2,1,0:T(8,128)(2,1)S(1)}, u32[]{:S(2)}, u32[]{:S(2)}) %collective-permute-start) | collective-permute-done | bytes 1048608 | tf_op jit(solution)/shard_map/ppermute | solution.py:465
  29.5 0.5 collective-permute-start.5
  30.0 1.8 collective-permute-start.3
  31.7 0.4 collective-permute-done.4.refs_3_
  32.1 6.2 %shard_map.49 = bf16[6144,128]{1,0:T(8,128)(2,1)S(1)} custom-call(s32[4,6]{1,0:T(4,128)} %get-tuple-element.30.refs_0_, s32[2]{0:T(128)S(1)} %copy-done.10, bf16[8,512,128]{2,1,0:T(8,128)(2,1)S(1)} %collective-permute-done.refs_2_, bf16[8,512,128]{2,1,0:T(8,128)(2,1)S(1)} %collective-permute-done.4.refs_3_, ...), custom_call_target="tpu_custom_call" | custom-call | flops 1207959552 | bytes 3670016 | tf_op jit(solution)/shard_map/pallas_call | solution.py:307
  38.3 4.0 %shard_map.50.refs_6_ = f32[2,8,384,128]{3,2,1,0:T(8,128)S(1)} custom-call(s32[4,6]{1,0:T(4,128)} %get-tuple-element.30.refs_0_, s32[2]{0:T(128)S(1)} %copy-done.10, bf16[8,512,128]{2,1,0:T(8,128)(2,1)S(1)} %copy-done.3, bf16[8,512,128]{2,1,0:T(8,128)(2,1)S(1)} %collective-permute-done.5.refs_3_, bf16[2,384,512]{2,1,0:T(8,128)(2,1)} %get-tuple-element.34.refs_4_.refs_6_, ...), custom_call_target="tpu_custom_call" | custom-call | flops 1207959552 | bytes 3670016 | tf_op jit(solution)/shard_map/pallas_call | solution.py:307
  42.3 11.0 %all-to-all-start.1 = ((bf16[768,8,128]{2,1,0:T(8,128)(2,1)}), bf16[768,8,128]{2,1,0:T(8,128)(2,1)}, u32[]{:S(2)}, u32[]{:S(2)}) async-start(bf16[768,8,128]{2,1,0:T(8,128)(2,1)} %bitcast.8), calls=%async_computation.1 | async-start | bytes 3145728 | tf_op jit(solution)/shard_map/all_to_all | solution.py:486
  53.4 1.9 %collective-permute-done.3.refs_3_ = bf16[8,512,128]{2,1,0:T(8,128)(2,1)} collective-permute-done((bf16[8,512,128]{2,1,0:T(8,128)(2,1)}, bf16[8,512,128]{2,1,0:T(8,128)(2,1)}, u32[]{:S(2)}, u32[]{:S(2)}) %collective-permute-start.3) | collective-permute-done | bytes 1048608 | tf_op jit(solution)/shard_map/ppermute | solution.py:465
  55.4 1.7 collective-permute-start.2
  57.1 1.1 collective-permute-done.7.refs_5_
  58.2 7.5 %shard_map.51 = bf16[6144,128]{1,0:T(8,128)(2,1)S(1)} custom-call(s32[4,6]{1,0:T(4,128)} %get-tuple-element.30.refs_0_, s32[2]{0:T(128)S(1)} %copy-done.10, bf16[8,512,128]{2,1,0:T(8,128)(2,1)} %get-tuple-element.33.refs_2_, bf16[8,512,128]{2,1,0:T(8,128)(2,1)} %collective-permute-done.3.refs_3_, bf16[8,512,128]{2,1,0:T(8,128)(2,1)S(1)} %collective-permute-done.6.refs_4_, ...), custom_call_target="tpu_custom_call" | custom-call | flops 2415919104 | bytes 5767168 | tf_op jit(solution)/shard_map/pallas_call | solution.py:307
  65.8 1.1 copy-done.7
  66.9 8.0 %all-to-all-done.1.refs_0_ = bf16[768,8,128]{2,1,0:T(8,128)(2,1)} async-done(((bf16[768,8,128]{2,1,0:T(8,128)(2,1)}), bf16[768,8,128]{2,1,0:T(8,128)(2,1)}, u32[]{:S(2)}, u32[]{:S(2)}) %all-to-all-start.1) | async-done | bytes 1572896 | tf_op jit(solution)/shard_map/all_to_all | solution.py:486
  74.9 4.8 %all-to-all-start.2 = ((bf16[768,8,128]{2,1,0:T(8,128)(2,1)}), bf16[768,8,128]{2,1,0:T(8,128)(2,1)}, u32[]{:S(2)}, u32[]{:S(2)}) async-start(bf16[768,8,128]{2,1,0:T(8,128)(2,1)} %bitcast.10), calls=%async_computation.2 | async-start | bytes 3145728 | tf_op jit(solution)/shard_map/all_to_all | solution.py:486
  79.8 1.5 collective-permute-done.2.refs_3_
  81.3 1.7 collective-permute-start.9
  83.0 1.1 collective-permute-done.11.refs_5_
  84.2 1.2 copy-done.12
  85.4 7.2 %shard_map.52 = bf16[6144,128]{1,0:T(8,128)(2,1)S(1)} custom-call(s32[4,6]{1,0:T(4,128)} %get-tuple-element.30.refs_0_, s32[2]{0:T(128)S(1)} %copy-done.10, bf16[8,512,128]{2,1,0:T(8,128)(2,1)S(1)} %copy-done.12, bf16[8,512,128]{2,1,0:T(8,128)(2,1)} %collective-permute-done.2.refs_3_, bf16[8,512,128]{2,1,0:T(8,128)(2,1)S(1)} %collective-permute-done.10.refs_4_, ...), custom_call_target="tpu_custom_call" | custom-call | flops 2415919104 | bytes 5767168 | tf_op jit(solution)/shard_map/pallas_call | solution.py:307
  92.6 1.1 copy-done.8
  93.8 7.8 %all-to-all-done.2.refs_1_ = bf16[768,8,128]{2,1,0:T(8,128)(2,1)} async-done(((bf16[768,8,128]{2,1,0:T(8,128)(2,1)}), bf16[768,8,128]{2,1,0:T(8,128)(2,1)}, u32[]{:S(2)}, u32[]{:S(2)}) %all-to-all-start.2) | async-done | bytes 1572896 | tf_op jit(solution)/shard_map/all_to_all | solution.py:486
  101.6 5.0 %all-to-all-start.3 = ((bf16[768,8,128]{2,1,0:T(8,128)(2,1)}), bf16[768,8,128]{2,1,0:T(8,128)(2,1)}, u32[]{:S(2)}, u32[]{:S(2)}) async-start(bf16[768,8,128]{2,1,0:T(8,128)(2,1)} %bitcast.11), calls=%async_computation.3 | async-start | bytes 3145728 | tf_op jit(solution)/shard_map/all_to_all | solution.py:486
  106.7 0.4 collective-permute-done.9.refs_3_
  107.2 1.7 collective-permute-start.8
  108.9 0.7 collective-permute-done.12.refs_4_
  109.6 1.5 collective-permute-done.13.refs_5_
  111.1 1.2 copy-done.11
  112.3 7.2 %shard_map.53 = bf16[6144,128]{1,0:T(8,128)(2,1)S(1)} custom-call(s32[4,6]{1,0:T(4,128)} %get-tuple-element.30.refs_0_, s32[2]{0:T(128)S(1)} %copy-done.10, bf16[8,512,128]{2,1,0:T(8,128)(2,1)S(1)} %copy-done.11, bf16[8,512,128]{2,1,0:T(8,128)(2,1)} %collective-permute-done.9.refs_3_, bf16[8,512,128]{2,1,0:T(8,128)(2,1)S(1)} %collective-permute-done.12.refs_4_, ...), custom_call_target="tpu_custom_call" | custom-call | flops 2415919104 | bytes 5767168 | tf_op jit(solution)/shard_map/pallas_call | solution.py:307
  119.6 1.2 copy-done.9
  120.7 7.7 %all-to-all-done.3.refs_2_ = bf16[768,8,128]{2,1,0:T(8,128)(2,1)} async-done(((bf16[768,8,128]{2,1,0:T(8,128)(2,1)}), bf16[768,8,128]{2,1,0:T(8,128)(2,1)}, u32[]{:S(2)}, u32[]{:S(2)}) %all-to-all-start.3) | async-done | bytes 1572896 | tf_op jit(solution)/shard_map/all_to_all | solution.py:486
  128.4 5.1 %all-to-all-start.4 = ((bf16[768,8,128]{2,1,0:T(8,128)(2,1)}), bf16[768,8,128]{2,1,0:T(8,128)(2,1)}, u32[]{:S(2)}, u32[]{:S(2)}) async-start(bf16[768,8,128]{2,1,0:T(8,128)(2,1)} %bitcast.12), calls=%async_computation.4 | async-start | bytes 3145728 | tf_op jit(solution)/shard_map/all_to_all | solution.py:486
  133.5 1.2 copy-done.4
  134.7 1.2 copy-done.6
  136.0 0.8 shard_map.54.refs_6_
  136.9 2.9 %collective-permute-done.14.refs_3_ = bf16[8,512,128]{2,1,0:T(8,128)(2,1)S(1)} collective-permute-done((bf16[8,512,128]{2,1,0:T(8,128)(2,1)}, bf16[8,512,128]{2,1,0:T(8,128)(2,1)S(1)}, u32[]{:S(2)}, u32[]{:S(2)}) %collective-permute-start.14) | collective-permute-done | bytes 1048608 | tf_op jit(solution)/shard_map/ppermute | solution.py:476
  139.8 6.4 %shard_map.55 = bf16[6144,128]{1,0:T(8,128)(2,1)S(1)} custom-call(s32[4,6]{1,0:T(4,128)} %get-tuple-element.30.refs_0_, s32[2]{0:T(128)S(1)} %copy-done.10, bf16[8,512,128]{2,1,0:T(8,128)(2,1)} %collective-permute-done.8.refs_2_, bf16[8,512,128]{2,1,0:T(8,128)(2,1)S(1)} %collective-permute-done.14.refs_3_, ...), custom_call_target="tpu_custom_call" | custom-call | flops 1207959552 | bytes 3670016 | tf_op jit(solution)/shard_map/pallas_call | solution.py:307
  146.2 1.2 copy-done.1
  147.4 7.4 %all-to-all-done.4.refs_3_ = bf16[768,8,128]{2,1,0:T(8,128)(2,1)} async-done(((bf16[768,8,128]{2,1,0:T(8,128)(2,1)}), bf16[768,8,128]{2,1,0:T(8,128)(2,1)}, u32[]{:S(2)}, u32[]{:S(2)}) %all-to-all-start.4) | async-done | bytes 1572896 | tf_op jit(solution)/shard_map/all_to_all | solution.py:486
  154.8 4.7 %all-to-all-start = ((bf16[768,8,128]{2,1,0:T(8,128)(2,1)}), bf16[768,8,128]{2,1,0:T(8,128)(2,1)S(1)}, u32[]{:S(2)}, u32[]{:S(2)}) async-start(bf16[768,8,128]{2,1,0:T(8,128)(2,1)} %bitcast.9), calls=%async_computation | async-start | bytes 3145728 | tf_op jit(solution)/shard_map/all_to_all | solution.py:486
  159.5 5.7 %shard_map.56._ = bf16[24,8,20480]{2,1,0:T(8,128)(2,1)} custom-call(bf16[768,8,128]{2,1,0:T(8,128)(2,1)} %all-to-all-done.1.refs_0_, bf16[768,8,128]{2,1,0:T(8,128)(2,1)} %all-to-all-done.2.refs_1_, bf16[768,8,128]{2,1,0:T(8,128)(2,1)} %all-to-all-done.3.refs_2_, bf16[768,8,128]{2,1,0:T(8,128)(2,1)} %all-to-all-done.4.refs_3_), custom_call_target="tpu_custom_call" | custom-call | bytes 15728640 | tf_op jit(solution)/shard_map/pallas_call | solution.py:383
  165.2 15.7 %all-to-all-done.part = bf16[768,8,128]{2,1,0:T(8,128)(2,1)S(1)} async-done(((bf16[768,8,128]{2,1,0:T(8,128)(2,1)}), bf16[768,8,128]{2,1,0:T(8,128)(2,1)S(1)}, u32[]{:S(2)}, u32[]{:S(2)}) %all-to-all-start) | async-done | bytes 1572896 | tf_op jit(solution)/shard_map/all_to_all | solution.py:486
  180.9 1.4 shard_map.57
  (31 shorter events, 0.5 us)
Async XLA Ops:
  3.4 10.3 %collective-permute-start.1 = (bf16[8,512,128]{2,1,0:T(8,128)(2,1)}, bf16[8,512,128]{2,1,0:T(8,128)(2,1)S(1)}, u32[]{:S(2)}, u32[]{:S(2)}) collective-permute-start(bf16[8,512,128]{2,1,0:T(8,128)(2,1)} %shard_map.46.refs_2_), channel_id=1, source_target_pairs={{0,32},{32,0},{64,96},{96,64},{1,33},{33,1},{65,97},{97,65},{2,34}... | collective-permute-start | bytes 3145736 | tf_op jit(solution)/shard_map/ppermute | solution.py:460
  3.5 25.9 %collective-permute-start = (bf16[8,512,128]{2,1,0:T(8,128)(2,1)}, bf16[8,512,128]{2,1,0:T(8,128)(2,1)S(1)}, u32[]{:S(2)}, u32[]{:S(2)}) collective-permute-start(bf16[8,512,128]{2,1,0:T(8,128)(2,1)} %shard_map.46.refs_2_), channel_id=1, source_target_pairs={{0,64},{32,96},{64,0},{96,32},{1,65},{33,97},{65,1},{97,33},{2,66}... | collective-permute-start | bytes 3145736 | tf_op jit(solution)/shard_map/ppermute | solution.py:465
  6.2 7.6 %copy-start.2 = (bf16[8,512,128]{2,1,0:T(8,128)(2,1)S(1)}, bf16[8,512,128]{2,1,0:T(8,128)(2,1)}, u32[]{:S(2)}) copy-start(bf16[8,512,128]{2,1,0:T(8,128)(2,1)} %shard_map.46.refs_2_) | copy-start | bytes 3145732
  6.2 7.6 %copy-start.10 = (s32[2]{0:T(128)S(1)}, s32[2]{0:T(128)}, u32[]{:S(2)}) copy-start(s32[2]{0:T(128)} %pad_add_fusion.ids_ref.refs_1_) | copy-start | bytes 28
  13.8 15.7 %copy-start.3 = (bf16[8,512,128]{2,1,0:T(8,128)(2,1)S(1)}, bf16[8,512,128]{2,1,0:T(8,128)(2,1)}, u32[]{:S(2)}) copy-start(bf16[8,512,128]{2,1,0:T(8,128)(2,1)} %get-tuple-element.47.refs_2_) | copy-start | bytes 3145732
  29.5 2.7 %collective-permute-start.4 = (bf16[8,512,128]{2,1,0:T(8,128)(2,1)S(1)}, bf16[8,512,128]{2,1,0:T(8,128)(2,1)S(1)}, u32[]{:S(2)}, u32[]{:S(2)}) collective-permute-start(bf16[8,512,128]{2,1,0:T(8,128)(2,1)S(1)} %collective-permute-done.refs_2_), channel_id=1, source_target_pairs={{0,32},{32,0},{64,96},{96,64},{1,33},{33,1},{65,97},{97,65},{2,34}... | collective-permute-start | bytes 3145736 | tf_op jit(solution)/shard_map/ppermute | solution.py:476
  29.5 8.9 %collective-permute-start.5 = (bf16[8,512,128]{2,1,0:T(8,128)(2,1)S(1)}, bf16[8,512,128]{2,1,0:T(8,128)(2,1)S(1)}, u32[]{:S(2)}, u32[]{:S(2)}) collective-permute-start(bf16[8,512,128]{2,1,0:T(8,128)(2,1)S(1)} %copy-done.3), channel_id=1, source_target_pairs={{0,32},{32,0},{64,96},{96,64},{1,33},{33,1},{65,97},{97,65},{2,34}... | collective-permute-start | bytes 3145736 | tf_op jit(solution)/shard_map/ppermute | solution.py:483
  30.0 25.4 %collective-permute-start.3 = (bf16[8,512,128]{2,1,0:T(8,128)(2,1)}, bf16[8,512,128]{2,1,0:T(8,128)(2,1)}, u32[]{:S(2)}, u32[]{:S(2)}) collective-permute-start(bf16[8,512,128]{2,1,0:T(8,128)(2,1)} %get-tuple-element.33.refs_2_), channel_id=1, source_target_pairs={{0,64},{32,96},{64,0},{96,32},{1,65},{33,97},{65,1},{97,33},{2,66}... | collective-permute-start | bytes 3145736 | tf_op jit(solution)/shard_map/ppermute | solution.py:465
  38.3 4.0 %copy-start = (bf16[6144,128]{1,0:T(8,128)(2,1)}, bf16[6144,128]{1,0:T(8,128)(2,1)S(1)}, u32[]{:S(2)}) copy-start(bf16[6144,128]{1,0:T(8,128)(2,1)S(1)} %shard_map.49) | copy-start | bytes 4718596
  38.3 4.0 %copy-start.5 = (bf16[8,512,128]{2,1,0:T(8,128)(2,1)}, bf16[8,512,128]{2,1,0:T(8,128)(2,1)S(1)}, u32[]{:S(2)}) copy-start(bf16[8,512,128]{2,1,0:T(8,128)(2,1)S(1)} %collective-permute-done.5.refs_3_) | copy-start | bytes 3145732
  42.3 32.5 %all-to-all-start.1 = ((bf16[768,8,128]{2,1,0:T(8,128)(2,1)}), bf16[768,8,128]{2,1,0:T(8,128)(2,1)}, u32[]{:S(2)}, u32[]{:S(2)}) async-start(bf16[768,8,128]{2,1,0:T(8,128)(2,1)} %bitcast.8), calls=%async_computation.1 | async-start | bytes 3145728 | tf_op jit(solution)/shard_map/all_to_all | solution.py:486
  53.4 3.8 %collective-permute-start.6 = (bf16[8,512,128]{2,1,0:T(8,128)(2,1)}, bf16[8,512,128]{2,1,0:T(8,128)(2,1)S(1)}, u32[]{:S(2)}, u32[]{:S(2)}) collective-permute-start(bf16[8,512,128]{2,1,0:T(8,128)(2,1)} %get-tuple-element.33.refs_2_), channel_id=1, source_target_pairs={{0,32},{32,0},{64,96},{96,64},{1,33},{33,1},{65,97},{97,65},{2,34}... | collective-permute-start | bytes 3145736 | tf_op jit(solution)/shard_map/ppermute | solution.py:460
  55.4 2.9 %collective-permute-start.7 = (bf16[8,512,128]{2,1,0:T(8,128)(2,1)}, bf16[8,512,128]{2,1,0:T(8,128)(2,1)S(1)}, u32[]{:S(2)}, u32[]{:S(2)}) collective-permute-start(bf16[8,512,128]{2,1,0:T(8,128)(2,1)} %collective-permute-done.3.refs_3_), channel_id=1, source_target_pairs={{0,32},{32,0},{64,96},{96,64},{1,33},{33,1},{65,97},{97,65},{2,34}... | collective-permute-start | bytes 3145736 | tf_op jit(solution)/shard_map/ppermute | solution.py:476
  55.4 25.9 %collective-permute-start.2 = (bf16[8,512,128]{2,1,0:T(8,128)(2,1)}, bf16[8,512,128]{2,1,0:T(8,128)(2,1)}, u32[]{:S(2)}, u32[]{:S(2)}) collective-permute-start(bf16[8,512,128]{2,1,0:T(8,128)(2,1)} %get-tuple-element.37.refs_2_), channel_id=1, source_target_pairs={{0,64},{32,96},{64,0},{96,32},{1,65},{33,97},{65,1},{97,33},{2,66}... | collective-permute-start | bytes 3145736 | tf_op jit(solution)/shard_map/ppermute | solution.py:465
  65.7 1.1 copy-start.7
  74.9 26.7 %all-to-all-start.2 = ((bf16[768,8,128]{2,1,0:T(8,128)(2,1)}), bf16[768,8,128]{2,1,0:T(8,128)(2,1)}, u32[]{:S(2)}, u32[]{:S(2)}) async-start(bf16[768,8,128]{2,1,0:T(8,128)(2,1)} %bitcast.10), calls=%async_computation.2 | async-start | bytes 3145728 | tf_op jit(solution)/shard_map/all_to_all | solution.py:486
  79.7 3.3 %collective-permute-start.10 = (bf16[8,512,128]{2,1,0:T(8,128)(2,1)}, bf16[8,512,128]{2,1,0:T(8,128)(2,1)S(1)}, u32[]{:S(2)}, u32[]{:S(2)}) collective-permute-start(bf16[8,512,128]{2,1,0:T(8,128)(2,1)} %get-tuple-element.37.refs_2_), channel_id=1, source_target_pairs={{0,32},{32,0},{64,96},{96,64},{1,33},{33,1},{65,97},{97,65},{2,34}... | collective-permute-start | bytes 3145736 | tf_op jit(solution)/shard_map/ppermute | solution.py:460
  81.3 2.9 %collective-permute-start.11 = (bf16[8,512,128]{2,1,0:T(8,128)(2,1)}, bf16[8,512,128]{2,1,0:T(8,128)(2,1)S(1)}, u32[]{:S(2)}, u32[]{:S(2)}) collective-permute-start(bf16[8,512,128]{2,1,0:T(8,128)(2,1)} %collective-permute-done.2.refs_3_), channel_id=1, source_target_pairs={{0,32},{32,0},{64,96},{96,64},{1,33},{33,1},{65,97},{97,65},{2,34}... | collective-permute-start | bytes 3145736 | tf_op jit(solution)/shard_map/ppermute | solution.py:476
  81.3 25.9 %collective-permute-start.9 = (bf16[8,512,128]{2,1,0:T(8,128)(2,1)}, bf16[8,512,128]{2,1,0:T(8,128)(2,1)}, u32[]{:S(2)}, u32[]{:S(2)}) collective-permute-start(bf16[8,512,128]{2,1,0:T(8,128)(2,1)} %get-tuple-element.45.refs_2_), channel_id=1, source_target_pairs={{0,64},{32,96},{64,0},{96,32},{1,65},{33,97},{65,1},{97,33},{2,66}... | collective-permute-start | bytes 3145736 | tf_op jit(solution)/shard_map/ppermute | solution.py:465
  84.2 1.2 copy-start.12
  92.6 1.1 copy-start.8
  101.6 26.8 %all-to-all-start.3 = ((bf16[768,8,128]{2,1,0:T(8,128)(2,1)}), bf16[768,8,128]{2,1,0:T(8,128)(2,1)}, u32[]{:S(2)}, u32[]{:S(2)}) async-start(bf16[768,8,128]{2,1,0:T(8,128)(2,1)} %bitcast.11), calls=%async_computation.3 | async-start | bytes 3145728 | tf_op jit(solution)/shard_map/all_to_all | solution.py:486
  106.6 3.0 %collective-permute-start.12 = (bf16[8,512,128]{2,1,0:T(8,128)(2,1)}, bf16[8,512,128]{2,1,0:T(8,128)(2,1)S(1)}, u32[]{:S(2)}, u32[]{:S(2)}) collective-permute-start(bf16[8,512,128]{2,1,0:T(8,128)(2,1)} %get-tuple-element.45.refs_2_), channel_id=1, source_target_pairs={{0,32},{32,0},{64,96},{96,64},{1,33},{33,1},{65,97},{97,65},{2,34}... | collective-permute-start | bytes 3145736 | tf_op jit(solution)/shard_map/ppermute | solution.py:460
  107.2 3.9 %collective-permute-start.13 = (bf16[8,512,128]{2,1,0:T(8,128)(2,1)}, bf16[8,512,128]{2,1,0:T(8,128)(2,1)S(1)}, u32[]{:S(2)}, u32[]{:S(2)}) collective-permute-start(bf16[8,512,128]{2,1,0:T(8,128)(2,1)} %collective-permute-done.9.refs_3_), channel_id=1, source_target_pairs={{0,32},{32,0},{64,96},{96,64},{1,33},{33,1},{65,97},{97,65},{2,34}... | collective-permute-start | bytes 3145736 | tf_op jit(solution)/shard_map/ppermute | solution.py:476
  107.2 29.6 %collective-permute-start.8 = (bf16[8,512,128]{2,1,0:T(8,128)(2,1)}, bf16[8,512,128]{2,1,0:T(8,128)(2,1)}, u32[]{:S(2)}, u32[]{:S(2)}) collective-permute-start(bf16[8,512,128]{2,1,0:T(8,128)(2,1)} %get-tuple-element.47.refs_2_), channel_id=1, source_target_pairs={{0,64},{32,96},{64,0},{96,32},{1,65},{33,97},{65,1},{97,33},{2,66}... | collective-permute-start | bytes 3145736 | tf_op jit(solution)/shard_map/ppermute | solution.py:465
  111.1 1.2 copy-start.11
  119.5 1.2 copy-start.9
  128.4 26.4 %all-to-all-start.4 = ((bf16[768,8,128]{2,1,0:T(8,128)(2,1)}), bf16[768,8,128]{2,1,0:T(8,128)(2,1)}, u32[]{:S(2)}, u32[]{:S(2)}) async-start(bf16[768,8,128]{2,1,0:T(8,128)(2,1)} %bitcast.12), calls=%async_computation.4 | async-start | bytes 3145728 | tf_op jit(solution)/shard_map/all_to_all | solution.py:486
  133.5 1.2 copy-start.4
  134.7 1.2 copy-start.6
  136.8 3.0 %collective-permute-start.14 = (bf16[8,512,128]{2,1,0:T(8,128)(2,1)}, bf16[8,512,128]{2,1,0:T(8,128)(2,1)S(1)}, u32[]{:S(2)}, u32[]{:S(2)}) collective-permute-start(bf16[8,512,128]{2,1,0:T(8,128)(2,1)} %collective-permute-done.8.refs_2_), channel_id=1, source_target_pairs={{0,32},{32,0},{64,96},{96,64},{1,33},{33,1},{65,97},{97,65},{2,34}... | collective-permute-start | bytes 3145736 | tf_op jit(solution)/shard_map/ppermute | solution.py:476
  146.2 1.2 copy-start.1
  154.8 26.2 %all-to-all-start = ((bf16[768,8,128]{2,1,0:T(8,128)(2,1)}), bf16[768,8,128]{2,1,0:T(8,128)(2,1)S(1)}, u32[]{:S(2)}, u32[]{:S(2)}) async-start(bf16[768,8,128]{2,1,0:T(8,128)(2,1)} %bitcast.9), calls=%async_computation | async-start | bytes 3145728 | tf_op jit(solution)/shard_map/all_to_all | solution.py:486

commit v5 on v3

--- a/solution.py
+++ b/solution.py
@@ -190,51 +190,48 @@
     table_ref, ids_ref, *refs = refs
     count = len(slabs)
     sources, (virt_in, occ_in), refs = refs[:count], refs[count:count + 2], refs[count + 2:]
-    if not begins:
-        partial, *refs = refs
+    partial = None if begins else refs.pop(0)
     out, packs, virt_ref, occ_ref, total, mixed, result, in_sems, out_sems = refs
+    if not ends:
+        total = out
     depth = sources[0].shape[1]
-    half_rows = virt_ref.shape[1]
+    half_rows = virt_in.shape[1]
     blocks = half_rows // SPAN
     tile = depth // CAP
-    targets = [packs.at[n, :, pl.ds(0, depth), :] for n in range(count)] + [virt_ref, occ_ref]
     arrivals = [
-        pltpu.make_async_copy(ref, target, in_sems.at[n])
-        for n, (ref, target) in enumerate(zip(list(sources) + [virt_in, occ_in], targets))
+        pltpu.make_async_copy(ref, packs.at[n, :, pl.ds(0, depth), :], in_sems.at[n])
+        for n, ref in enumerate(sources)
     ]
-    if not begins:
-        arrivals.append(pltpu.make_async_copy(partial, total, in_sems.at[count + 2]))
-    for n in [0, count] + list(range(1, count)) + list(range(count + 1, len(arrivals))):
-        arrivals[n].start()
+    direct = [(n, slab) for n, slab in enumerate(slabs) if slab < 2]
+    virt_copy = pltpu.make_async_copy(virt_in, virt_ref, in_sems.at[count])
+    occ_copy = pltpu.make_async_copy(occ_in, occ_ref, in_sems.at[count + 1])
+    arrivals[0].start()
+    if direct:
+        virt_copy.start()
+    for copy in arrivals[1:]:
+        copy.start()
+    occ_copy.start()
     for n in range(count):
         packs[n, :, depth:depth + FINE, :] = jnp.zeros((OCC, FINE, LANES), jnp.bfloat16)
     perm = permutation(True) if ends else None
-    waited = set()
-
-    def arrived(n):
-        if n not in waited:
-            waited.add(n)
-            arrivals[n].wait()
-
-    arrived(count)
-    if not begins:
-        arrived(count + 2)
-    for n, slab in enumerate(slabs):
-        if slab >= 2:
-            continue
-        arrived(n)
+    if direct:
+        virt_copy.wait()
+    for n, slab in direct:
+        arrivals[n].wait()
         for i in range(0, OCC, 2):
             both = jnp.concatenate([packs[n, i, :depth], packs[n, i + 1, :depth]], axis=1)
             y = dot(virt_ref[slab], both)
             for j in range(2):
                 part = y[:, j * LANES:(j + 1) * LANES]
-                total[slab, i + j] = part if begins else part + total[slab, i + j]
-    for n in range(len(arrivals)):
-        arrived(n)
-    fresh = [which for which in range(2) if begins and which not in slabs]
+                total[slab, i + j] = part if begins else part + partial[slab, i + j]
+    for n, slab in enumerate(slabs):
+        if slab >= 2:
+            arrivals[n].wait()
+    occ_copy.wait()
     departures = []
     for which in range(2):
         half = ids_ref[1] if which == 0 else 1 - ids_ref[1]
+        base = total if which in slabs else partial
         weights = jnp.concatenate([occ_ref[which][:, s * FROWS:(s + 1) * FROWS] for s in slabs], axis=1)
         for first in range(0, half_rows, 2 * FINE):
             columns = []
@@ -242,24 +239,21 @@
                 start = row // SPAN * (HALVES * SPAN) + row % SPAN + half * SPAN
                 parts = []
                 for n, s in enumerate(slabs):
-                    base = table_ref[s, start // tile]
-                    at = pl.multiple_of(jnp.where(base < 0, depth, base + start % tile), FINE)
+                    at = table_ref[s, start // tile]
+                    at = pl.multiple_of(jnp.where(at < 0, depth, at + start % tile), FINE)
                     parts.append(packs[n, :, pl.ds(at, FINE), :].reshape(FROWS, LANES))
                 columns.append(jnp.concatenate(parts, axis=0))
             y = dot(weights, jnp.concatenate(columns, axis=1))
             for n in range(2):
                 row = first + n * FINE
                 part = y[:, n * LANES:(n + 1) * LANES].reshape(OCC, FINE, LANES)
-                if which not in fresh:
-                    part = part + total[which, :, row:row + FINE, :]
+                if base is not None:
+                    part = part + base[which, :, row:row + FINE, :]
                 if ends:
                     mixed[which, :, row:row + FINE, :] = part.astype(jnp.bfloat16)
                 else:
                     total[which, :, row:row + FINE, :] = part
         if not ends:
-            copy = pltpu.make_async_copy(total.at[which], out.at[which], out_sems.at[which])
-            copy.start()
-            departures.append(copy)
             continue
         for first in range(0, half_rows, 2 * GROUP):
             pair = transpose_rows(perm, [
@@ -289,22 +283,24 @@
     begins = partial is None
     share = len(slabs) * LANES
     extra = [] if begins else [partial]
+    held = pl.BlockSpec(memory_space=pltpu.VMEM)
+    unused = (OCC, LANES)
     return pl.pallas_call(
         functools.partial(density_body, slabs, begins, ends),
         out_shape=jax.ShapeDtypeStruct((rows, LANES), jnp.bfloat16) if ends else jax.ShapeDtypeStruct(sums, jnp.float32),
         grid_spec=pltpu.PrefetchScalarGridSpec(
             num_scalar_prefetch=2,
             grid=(1,),
-            in_specs=[pl.BlockSpec(memory_space=pl.ANY)] * (len(slabs) + 2 + len(extra)),
-            out_specs=pl.BlockSpec(memory_space=pl.ANY),
+            in_specs=[pl.BlockSpec(memory_space=pl.ANY)] * (len(slabs) + 2) + [held] * len(extra),
+            out_specs=pl.BlockSpec(memory_space=pl.ANY) if ends else held,
             scratch_shapes=[
                 pltpu.VMEM((len(slabs), OCC, depth + FINE, LANES), jnp.bfloat16),
-                pltpu.VMEM(virt.shape, jnp.bfloat16),
+                pltpu.VMEM(virt.shape if min(slabs) < 2 else unused, jnp.bfloat16),
                 pltpu.VMEM(occ.shape, jnp.bfloat16),
-                pltpu.VMEM(sums, jnp.float32),
-                pltpu.VMEM(sums if ends else (OCC, LANES), jnp.bfloat16),
-                pltpu.VMEM((2, half_rows * OCC, LANES) if ends else (OCC, LANES), jnp.bfloat16),
-                pltpu.SemaphoreType.DMA((len(slabs) + 3,)),
+                pltpu.VMEM(sums if ends and min(slabs) < 2 else unused, jnp.float32),
+                pltpu.VMEM(sums if ends else unused, jnp.bfloat16),
+                pltpu.VMEM((2, half_rows * OCC, LANES) if ends else unused, jnp.bfloat16),
+                pltpu.SemaphoreType.DMA((len(slabs) + 2,)),
                 pltpu.SemaphoreType.DMA((2 * half_rows // SPAN,)),
             ],
         ),
@@ -459,7 +455,8 @@
         if partial is None:
             gamma = density(table, ids, (0, 1, 2, 3), (part, across, beside, diagonal), virt, occ)
         else:
-            gamma = density(table, ids, (1, 3), (across, diagonal), virt, occ, partial=before[1])
+            partial = density(table, ids, (1,), (across,), virt, occ, partial=before[1], ends=False)
+            gamma = density(table, ids, (3,), (diagonal,), virt, occ, partial=partial)
         done.append(lax.all_to_all(
             gamma.reshape(virt_count, OCC, -1), ("occ", "aux"),
             split_axis=0, concat_axis=0, axis_index_groups=groups, tiled=True,

time: 181 us -> 181 us (level)
  Pallas kernels: 53.5 us -> 57 us
  waiting for transfers between devices: 84.7 us -> 82.8 us
    ppermute x5, waiting for transfers between devices: 7.4 us -> 3.86 us  [local(): diagonal = lax.ppermute(across, 'occ', core_pairs)]
    pallas_call x7 -> x9, Pallas kernels: 35.6 us -> 39.1 us  [density(): pl.pallas_call(functools.partial(density_body, slabs, begins, ends), out_...]
  transfers between devices with their start and end apart: 20 -> 20, of which waited for: 14 -> 12; matrix products, arithmetic and copies ran while one was open for 0% -> 0% of each run, Pallas kernels for 27% -> 29%
where the time goes in v5:
time: 181 us; the launch traced here: 180 us
  waiting for transfers between devices  82.8 us (46%)
  Pallas kernels  57 us (31%)
  starting transfers between devices  39 us (22%)
    all_to_all x5, waiting for transfers between devices, local(): lax.all_to_all(gamma.reshape(virt_count, OCC, -1), ('occ', 'aux'), split_...  54 us
    pallas_call x9, Pallas kernels, density(): pl.pallas_call(functools.partial(density_body, slabs, begins, ends), out_...  39.1 us
    all_to_all x5, starting transfers between devices, local(): lax.all_to_all(gamma.reshape(virt_count, OCC, -1), ('occ', 'aux'), split_...  29.1 us
    ppermute x5, waiting for transfers between devices, local(): across = lax.ppermute(sent, 'occ', chip_pairs)  24.9 us
    ppermute x5, starting transfers between devices, local(): across = lax.ppermute(sent, 'occ', chip_pairs)  8.99 us
    pallas_call x1, Pallas kernels, rest_pack(): pl.pallas_call(rest_body, out_shape=[jax.ShapeDtypeStruct((2, half_rows,...  7.45 us
    pallas_call x1, Pallas kernels, assemble(): pl.pallas_call(assemble_body, out_shape=jax.ShapeDtypeStruct(shape, jnp.b...  5.71 us
    ppermute x5, waiting for transfers between devices, local(): diagonal = lax.ppermute(across, 'occ', core_pairs)  3.86 us
  transfers between devices with their start and end apart: 20, of which 12 were waited for; matrix products, arithmetic and copies ran while one was open for 0% of the time, Pallas kernels for 29%

profile of v5, /device:TPU:2, one launch (start us, length us, event | category | flops | bytes accessed | tf_op | source)
XLA Modules:
  0.0 179.8 jit_solution(11039001106346638392)
XLA Ops:
  0.0 3.4 %shard_map.46.refs_2_ = bf16[8,512,128]{2,1,0:T(8,128)(2,1)} custom-call(s32[4,6]{1,0:T(4,128)} %mask_ref.3, bf16[768,8,640]{2,1,0:T(8,128)(2,1)} %x_ref.3), custom_call_target="tpu_custom_call" | custom-call | flops 536870912 | bytes 2097152 | tf_op jit(solution)/shard_map/pallas_call | solution.py:91
  3.4 0.1 collective-permute-start.1
  3.5 2.0 %collective-permute-start = (bf16[8,512,128]{2,1,0:T(8,128)(2,1)}, bf16[8,512,128]{2,1,0:T(8,128)(2,1)S(1)}, u32[]{:S(2)}, u32[]{:S(2)}) collective-permute-start(bf16[8,512,128]{2,1,0:T(8,128)(2,1)} %shard_map.46.refs_2_), channel_id=1, source_target_pairs={{0,64},{32,96},{64,0},{96,32},{1,65},{33,97},{65,1},{97,33},{2,66}... | collective-permute-start | bytes 3145736 | tf_op jit(solution)/shard_map/ppermute | solution.py:445
  5.5 0.6 pad_add_fusion.ids_ref.refs_1_
  6.1 7.4 %shard_map.47 = (bf16[2,384,512]{2,1,0:T(8,128)(2,1)}, bf16[2,128,512]{2,1,0:T(8,128)(2,1)}, s32[4,6]{1,0:T(4,128)}, bf16[8,512,128]{2,1,0:T(8,128)(2,1)}, bf16[...) custom-call(s32[4,6]{1,0:T(4,128)} %mask_ref.3, ...), custom_call_target="tpu_custom_call" | custom-call | flops 3221225472 | bytes 12582912 | tf_op jit(solution)/shard_map/pallas_call | solution.py:161
  13.5 0.0 collective-permute-done.1.refs_3_
  13.5 3.4 %shard_map.48.refs_5_ = f32[2,8,384,128]{3,2,1,0:T(8,128)S(1)} custom-call(s32[4,6]{1,0:T(4,128)} %get-tuple-element.27.refs_0_, s32[2]{0:T(128)S(1)} %copy-done.2, bf16[8,512,128]{2,1,0:T(8,128)(2,1)S(1)} %copy-done, bf16[8,512,128]{2,1,0:T(8,128)(2,1)S(1)} %collective-permute-done.1.refs_3_, ...), custom_call_target="tpu_custom_call" | custom-call | flops 1207959552 | bytes 3670016 | tf_op jit(solution)/shard_map/pallas_call | solution.py:288
  17.0 12.4 %collective-permute-done.refs_2_ = bf16[8,512,128]{2,1,0:T(8,128)(2,1)S(1)} collective-permute-done((bf16[8,512,128]{2,1,0:T(8,128)(2,1)}, bf16[8,512,128]{2,1,0:T(8,128)(2,1)S(1)}, u32[]{:S(2)}, u32[]{:S(2)}) %collective-permute-start) | collective-permute-done | bytes 1048608 | tf_op jit(solution)/shard_map/ppermute | solution.py:445
  29.4 0.0 collective-permute-start.4
  29.4 1.8 collective-permute-start.3
  31.2 3.2 %shard_map.49.refs_5_ = f32[2,8,384,128]{3,2,1,0:T(8,128)S(1)} custom-call(s32[4,6]{1,0:T(4,128)} %get-tuple-element.27.refs_0_, s32[2]{0:T(128)S(1)} %copy-done.2, bf16[8,512,128]{2,1,0:T(8,128)(2,1)S(1)} %collective-permute-done.refs_2_, bf16[2,384,512]{2,1,0:T(8,128)(2,1)} %get-tuple-element.31.refs_4_.refs_3_.refs_6_, ...), custom_call_target="tpu_custom_call" | custom-call | flops 603979776 | bytes 2621440 | tf_op jit(solution)/shard_map/pallas_call | solution.py:288
  34.4 0.0 collective-permute-done.4.refs_2_
  34.4 3.8 %shard_map.50 = bf16[6144,128]{1,0:T(8,128)(2,1)} custom-call(s32[4,6]{1,0:T(4,128)} %get-tuple-element.27.refs_0_, s32[2]{0:T(128)S(1)} %copy-done.2, bf16[8,512,128]{2,1,0:T(8,128)(2,1)S(1)} %collective-permute-done.4.refs_2_, bf16[2,384,512]{2,1,0:T(8,128)(2,1)} %get-tuple-element.31.refs_4_.refs_3_.refs_6_, ...), custom_call_target="tpu_custom_call" | custom-call | flops 603979776 | bytes 2621440 | tf_op jit(solution)/shard_map/pallas_call | solution.py:288
  38.2 9.8 %all-to-all-start.1 = ((bf16[768,8,128]{2,1,0:T(8,128)(2,1)}), bf16[768,8,128]{2,1,0:T(8,128)(2,1)}, u32[]{:S(2)}, u32[]{:S(2)}) async-start(bf16[768,8,128]{2,1,0:T(8,128)(2,1)} %bitcast.4), calls=%async_computation.1 | async-start | bytes 3145728 | tf_op jit(solution)/shard_map/all_to_all | solution.py:460
  48.0 0.1 collective-permute-start.5
  48.1 7.1 %collective-permute-done.3.refs_3_ = bf16[8,512,128]{2,1,0:T(8,128)(2,1)S(1)} collective-permute-done((bf16[8,512,128]{2,1,0:T(8,128)(2,1)}, bf16[8,512,128]{2,1,0:T(8,128)(2,1)S(1)}, u32[]{:S(2)}, u32[]{:S(2)}) %collective-permute-start.3) | collective-permute-done | bytes 1048608 | tf_op jit(solution)/shard_map/ppermute | solution.py:445
  55.2 0.0 collective-permute-start.6
  55.2 1.7 collective-permute-start.2
  57.0 0.0 collective-permute-done.5.refs_4_
  57.0 0.9 collective-permute-done.6.refs_5_
  57.9 6.2 %shard_map.51 = bf16[6144,128]{1,0:T(8,128)(2,1)} custom-call(s32[4,6]{1,0:T(4,128)} %get-tuple-element.27.refs_0_, s32[2]{0:T(128)S(1)} %copy-done.2, bf16[8,512,128]{2,1,0:T(8,128)(2,1)} %get-tuple-element.30.refs_2_, bf16[8,512,128]{2,1,0:T(8,128)(2,1)S(1)} %collective-permute-done.3.refs_3_, bf16[8,512,128]{2,1,0:T(8,128)(2,1)S(1)} %collective-permute-done.5.refs_4_, ...), custom_call_target="tpu_custom_call" | custom-call | flops 2415919104 | bytes 5767168 | tf_op jit(solution)/shard_map/pallas_call | solution.py:288
  64.0 8.5 %all-to-all-done.1.refs_0_ = bf16[768,8,128]{2,1,0:T(8,128)(2,1)} async-done(((bf16[768,8,128]{2,1,0:T(8,128)(2,1)}), bf16[768,8,128]{2,1,0:T(8,128)(2,1)}, u32[]{:S(2)}, u32[]{:S(2)}) %all-to-all-start.1) | async-done | bytes 1572896 | tf_op jit(solution)/shard_map/all_to_all | solution.py:460
  72.5 4.5 %all-to-all-start.2 = ((bf16[768,8,128]{2,1,0:T(8,128)(2,1)}), bf16[768,8,128]{2,1,0:T(8,128)(2,1)}, u32[]{:S(2)}, u32[]{:S(2)}) async-start(bf16[768,8,128]{2,1,0:T(8,128)(2,1)} %bitcast.5), calls=%async_computation.2 | async-start | bytes 3145728 | tf_op jit(solution)/shard_map/all_to_all | solution.py:460
  77.0 0.1 collective-permute-start.9
  77.1 3.7 %collective-permute-done.2.refs_3_ = bf16[8,512,128]{2,1,0:T(8,128)(2,1)S(1)} collective-permute-done((bf16[8,512,128]{2,1,0:T(8,128)(2,1)S(1)}, bf16[8,512,128]{2,1,0:T(8,128)(2,1)S(1)}, u32[]{:S(2)}, u32[]{:S(2)}) %collective-permute-start.2) | collective-permute-done | bytes 1048608 | tf_op jit(solution)/shard_map/ppermute | solution.py:445
  80.8 0.0 collective-permute-start.10
  80.8 1.7 collective-permute-start.8
  82.5 0.9 collective-permute-done.10.refs_5_
  83.4 5.9 %shard_map.52 = bf16[6144,128]{1,0:T(8,128)(2,1)} custom-call(s32[4,6]{1,0:T(4,128)} %get-tuple-element.27.refs_0_, s32[2]{0:T(128)S(1)} %copy-done.2, bf16[8,512,128]{2,1,0:T(8,128)(2,1)S(1)} %copy-done.3, bf16[8,512,128]{2,1,0:T(8,128)(2,1)S(1)} %collective-permute-done.2.refs_3_, bf16[8,512,128]{2,1,0:T(8,128)(2,1)S(1)} %collective-permute-done.9.refs_4_, ...), custom_call_target="tpu_custom_call" | custom-call | flops 2415919104 | bytes 5767168 | tf_op jit(solution)/shard_map/pallas_call | solution.py:288
  89.3 10.6 %all-to-all-done.2.refs_1_ = bf16[768,8,128]{2,1,0:T(8,128)(2,1)} async-done(((bf16[768,8,128]{2,1,0:T(8,128)(2,1)}), bf16[768,8,128]{2,1,0:T(8,128)(2,1)}, u32[]{:S(2)}, u32[]{:S(2)}) %all-to-all-start.2) | async-done | bytes 1572896 | tf_op jit(solution)/shard_map/all_to_all | solution.py:460
  99.9 5.0 %all-to-all-start.3 = ((bf16[768,8,128]{2,1,0:T(8,128)(2,1)}), bf16[768,8,128]{2,1,0:T(8,128)(2,1)}, u32[]{:S(2)}, u32[]{:S(2)}) async-start(bf16[768,8,128]{2,1,0:T(8,128)(2,1)} %bitcast.6), calls=%async_computation.3 | async-start | bytes 3145728 | tf_op jit(solution)/shard_map/all_to_all | solution.py:460
  104.9 0.1 collective-permute-start.11
  105.0 1.6 collective-permute-done.8.refs_3_
  106.7 0.5 collective-permute-start.13
  107.2 1.7 collective-permute-start.7
  108.9 2.0 %collective-permute-done.12.refs_5_ = bf16[8,512,128]{2,1,0:T(8,128)(2,1)S(1)} collective-permute-done((bf16[8,512,128]{2,1,0:T(8,128)(2,1)}, bf16[8,512,128]{2,1,0:T(8,128)(2,1)S(1)}, u32[]{:S(2)}, u32[]{:S(2)}) %collective-permute-start.12) | collective-permute-done | bytes 1048608 | tf_op jit(solution)/shard_map/ppermute | solution.py:454
  111.0 6.2 %shard_map.53 = bf16[6144,128]{1,0:T(8,128)(2,1)} custom-call(s32[4,6]{1,0:T(4,128)} %get-tuple-element.27.refs_0_, s32[2]{0:T(128)S(1)} %copy-done.2, bf16[8,512,128]{2,1,0:T(8,128)(2,1)} %get-tuple-element.40.refs_2_, bf16[8,512,128]{2,1,0:T(8,128)(2,1)} %collective-permute-done.8.refs_3_, bf16[8,512,128]{2,1,0:T(8,128)(2,1)S(1)} %collective-permute-done.11.refs_4_, ...), custom_call_target="tpu_custom_call" | custom-call | flops 2415919104 | bytes 5767168 | tf_op jit(solution)/shard_map/pallas_call | solution.py:288
  117.1 9.3 %all-to-all-done.3.refs_2_ = bf16[768,8,128]{2,1,0:T(8,128)(2,1)} async-done(((bf16[768,8,128]{2,1,0:T(8,128)(2,1)}), bf16[768,8,128]{2,1,0:T(8,128)(2,1)}, u32[]{:S(2)}, u32[]{:S(2)}) %all-to-all-start.3) | async-done | bytes 1572896 | tf_op jit(solution)/shard_map/all_to_all | solution.py:460
  126.4 4.9 %all-to-all-start.4 = ((bf16[768,8,128]{2,1,0:T(8,128)(2,1)}), bf16[768,8,128]{2,1,0:T(8,128)(2,1)}, u32[]{:S(2)}, u32[]{:S(2)}) async-start(bf16[768,8,128]{2,1,0:T(8,128)(2,1)} %bitcast.7), calls=%async_computation.4 | async-start | bytes 3145728 | tf_op jit(solution)/shard_map/all_to_all | solution.py:460
  131.4 3.4 %shard_map.54.refs_5_ = f32[2,8,384,128]{3,2,1,0:T(8,128)S(1)} custom-call(s32[4,6]{1,0:T(4,128)} %get-tuple-element.27.refs_0_, s32[2]{0:T(128)S(1)} %copy-done.2, bf16[8,512,128]{2,1,0:T(8,128)(2,1)S(1)} %copy-done.1, bf16[8,512,128]{2,1,0:T(8,128)(2,1)S(1)} %collective-permute-done.13.refs_3_, ...), custom_call_target="tpu_custom_call" | custom-call | flops 1207959552 | bytes 3670016 | tf_op jit(solution)/shard_map/pallas_call | solution.py:288
  134.8 0.1 collective-permute-start.14
  134.9 3.2 %shard_map.55.refs_5_ = f32[2,8,384,128]{3,2,1,0:T(8,128)S(1)} custom-call(s32[4,6]{1,0:T(4,128)} %get-tuple-element.27.refs_0_, s32[2]{0:T(128)S(1)} %copy-done.2, bf16[8,512,128]{2,1,0:T(8,128)(2,1)S(1)} %collective-permute-done.7.refs_2_, bf16[2,384,512]{2,1,0:T(8,128)(2,1)} %get-tuple-element.31.refs_4_.refs_3_.refs_6_, ...), custom_call_target="tpu_custom_call" | custom-call | flops 603979776 | bytes 2621440 | tf_op jit(solution)/shard_map/pallas_call | solution.py:288
  138.1 3.8 %shard_map.56 = bf16[6144,128]{1,0:T(8,128)(2,1)} custom-call(s32[4,6]{1,0:T(4,128)} %get-tuple-element.27.refs_0_, s32[2]{0:T(128)S(1)} %copy-done.2, bf16[8,512,128]{2,1,0:T(8,128)(2,1)S(1)} %collective-permute-done.14.refs_2_, bf16[2,384,512]{2,1,0:T(8,128)(2,1)} %get-tuple-element.31.refs_4_.refs_3_.refs_6_, ...), custom_call_target="tpu_custom_call" | custom-call | flops 603979776 | bytes 2621440 | tf_op jit(solution)/shard_map/pallas_call | solution.py:288
  141.9 10.5 %all-to-all-done.4.refs_3_ = bf16[768,8,128]{2,1,0:T(8,128)(2,1)} async-done(((bf16[768,8,128]{2,1,0:T(8,128)(2,1)}), bf16[768,8,128]{2,1,0:T(8,128)(2,1)}, u32[]{:S(2)}, u32[]{:S(2)}) %all-to-all-start.4) | async-done | bytes 1572896 | tf_op jit(solution)/shard_map/all_to_all | solution.py:460
  152.5 4.9 %all-to-all-start = ((bf16[768,8,128]{2,1,0:T(8,128)(2,1)}), bf16[768,8,128]{2,1,0:T(8,128)(2,1)S(1)}, u32[]{:S(2)}, u32[]{:S(2)}) async-start(bf16[768,8,128]{2,1,0:T(8,128)(2,1)} %bitcast.3), calls=%async_computation | async-start | bytes 3145728 | tf_op jit(solution)/shard_map/all_to_all | solution.py:460
  157.4 5.7 %shard_map.57._ = bf16[24,8,20480]{2,1,0:T(8,128)(2,1)} custom-call(bf16[768,8,128]{2,1,0:T(8,128)(2,1)} %all-to-all-done.1.refs_0_, bf16[768,8,128]{2,1,0:T(8,128)(2,1)} %all-to-all-done.2.refs_1_, bf16[768,8,128]{2,1,0:T(8,128)(2,1)} %all-to-all-done.3.refs_2_, bf16[768,8,128]{2,1,0:T(8,128)(2,1)} %all-to-all-done.4.refs_3_), custom_call_target="tpu_custom_call" | custom-call | bytes 15728640 | tf_op jit(solution)/shard_map/pallas_call | solution.py:363
  163.1 15.2 %all-to-all-done.part = bf16[768,8,128]{2,1,0:T(8,128)(2,1)S(1)} async-done(((bf16[768,8,128]{2,1,0:T(8,128)(2,1)}), bf16[768,8,128]{2,1,0:T(8,128)(2,1)S(1)}, u32[]{:S(2)}, u32[]{:S(2)}) %all-to-all-start) | async-done | bytes 1572896 | tf_op jit(solution)/shard_map/all_to_all | solution.py:460
  178.3 1.4 shard_map.58
  (14 shorter events, 0.0 us)
Async XLA Ops:
  3.4 10.2 %collective-permute-start.1 = (bf16[8,512,128]{2,1,0:T(8,128)(2,1)}, bf16[8,512,128]{2,1,0:T(8,128)(2,1)S(1)}, u32[]{:S(2)}, u32[]{:S(2)}) collective-permute-start(bf16[8,512,128]{2,1,0:T(8,128)(2,1)} %shard_map.46.refs_2_), channel_id=1, source_target_pairs={{0,32},{32,0},{64,96},{96,64},{1,33},{33,1},{65,97},{97,65},{2,34}... | collective-permute-start | bytes 3145736 | tf_op jit(solution)/shard_map/ppermute | solution.py:440
  3.5 25.9 %collective-permute-start = (bf16[8,512,128]{2,1,0:T(8,128)(2,1)}, bf16[8,512,128]{2,1,0:T(8,128)(2,1)S(1)}, u32[]{:S(2)}, u32[]{:S(2)}) collective-permute-start(bf16[8,512,128]{2,1,0:T(8,128)(2,1)} %shard_map.46.refs_2_), channel_id=1, source_target_pairs={{0,64},{32,96},{64,0},{96,32},{1,65},{33,97},{65,1},{97,33},{2,66}... | collective-permute-start | bytes 3145736 | tf_op jit(solution)/shard_map/ppermute | solution.py:445
  6.1 7.5 %copy-start = (bf16[8,512,128]{2,1,0:T(8,128)(2,1)S(1)}, bf16[8,512,128]{2,1,0:T(8,128)(2,1)}, u32[]{:S(2)}) copy-start(bf16[8,512,128]{2,1,0:T(8,128)(2,1)} %shard_map.46.refs_2_) | copy-start | bytes 3145732
  6.1 7.5 %copy-start.2 = (s32[2]{0:T(128)S(1)}, s32[2]{0:T(128)}, u32[]{:S(2)}) copy-start(s32[2]{0:T(128)} %pad_add_fusion.ids_ref.refs_1_) | copy-start | bytes 28
  29.4 5.0 %collective-permute-start.4 = (bf16[8,512,128]{2,1,0:T(8,128)(2,1)S(1)}, bf16[8,512,128]{2,1,0:T(8,128)(2,1)S(1)}, u32[]{:S(2)}, u32[]{:S(2)}) collective-permute-start(bf16[8,512,128]{2,1,0:T(8,128)(2,1)S(1)} %collective-permute-done.refs_2_), channel_id=1, source_target_pairs={{0,32},{32,0},{64,96},{96,64},{1,33},{33,1},{65,97},{97,65},{2,34}... | collective-permute-start | bytes 3145736 | tf_op jit(solution)/shard_map/ppermute | solution.py:454
  29.4 25.8 %collective-permute-start.3 = (bf16[8,512,128]{2,1,0:T(8,128)(2,1)}, bf16[8,512,128]{2,1,0:T(8,128)(2,1)S(1)}, u32[]{:S(2)}, u32[]{:S(2)}) collective-permute-start(bf16[8,512,128]{2,1,0:T(8,128)(2,1)} %get-tuple-element.30.refs_2_), channel_id=1, source_target_pairs={{0,64},{32,96},{64,0},{96,32},{1,65},{33,97},{65,1},{97,33},{2,66}... | collective-permute-start | bytes 3145736 | tf_op jit(solution)/shard_map/ppermute | solution.py:445
  38.2 17.0 %copy-start.3 = (bf16[8,512,128]{2,1,0:T(8,128)(2,1)S(1)}, bf16[8,512,128]{2,1,0:T(8,128)(2,1)}, u32[]{:S(2)}) copy-start(bf16[8,512,128]{2,1,0:T(8,128)(2,1)} %get-tuple-element.34.refs_2_) | copy-start | bytes 3145732
  38.2 34.3 %all-to-all-start.1 = ((bf16[768,8,128]{2,1,0:T(8,128)(2,1)}), bf16[768,8,128]{2,1,0:T(8,128)(2,1)}, u32[]{:S(2)}, u32[]{:S(2)}) async-start(bf16[768,8,128]{2,1,0:T(8,128)(2,1)} %bitcast.4), calls=%async_computation.1 | async-start | bytes 3145728 | tf_op jit(solution)/shard_map/all_to_all | solution.py:460
  48.0 9.0 %collective-permute-start.5 = (bf16[8,512,128]{2,1,0:T(8,128)(2,1)}, bf16[8,512,128]{2,1,0:T(8,128)(2,1)S(1)}, u32[]{:S(2)}, u32[]{:S(2)}) collective-permute-start(bf16[8,512,128]{2,1,0:T(8,128)(2,1)} %get-tuple-element.30.refs_2_), channel_id=1, source_target_pairs={{0,32},{32,0},{64,96},{96,64},{1,33},{33,1},{65,97},{97,65},{2,34}... | collective-permute-start | bytes 3145736 | tf_op jit(solution)/shard_map/ppermute | solution.py:440
  55.2 2.7 %collective-permute-start.6 = (bf16[8,512,128]{2,1,0:T(8,128)(2,1)S(1)}, bf16[8,512,128]{2,1,0:T(8,128)(2,1)S(1)}, u32[]{:S(2)}, u32[]{:S(2)}) collective-permute-start(bf16[8,512,128]{2,1,0:T(8,128)(2,1)S(1)} %collective-permute-done.3.refs_3_), channel_id=1, source_target_pairs={{0,32},{32,0},{64,96},{96,64},{1,33},{33,1},{65,97},{97,65},{2,34}... | collective-permute-start | bytes 3145736 | tf_op jit(solution)/shard_map/ppermute | solution.py:454
  55.2 25.6 %collective-permute-start.2 = (bf16[8,512,128]{2,1,0:T(8,128)(2,1)S(1)}, bf16[8,512,128]{2,1,0:T(8,128)(2,1)S(1)}, u32[]{:S(2)}, u32[]{:S(2)}) collective-permute-start(bf16[8,512,128]{2,1,0:T(8,128)(2,1)S(1)} %copy-done.3), channel_id=1, source_target_pairs={{0,64},{32,96},{64,0},{96,32},{1,65},{33,97},{65,1},{97,33},{2,66}... | collective-permute-start | bytes 3145736 | tf_op jit(solution)/shard_map/ppermute | solution.py:445
  72.5 27.4 %all-to-all-start.2 = ((bf16[768,8,128]{2,1,0:T(8,128)(2,1)}), bf16[768,8,128]{2,1,0:T(8,128)(2,1)}, u32[]{:S(2)}, u32[]{:S(2)}) async-start(bf16[768,8,128]{2,1,0:T(8,128)(2,1)} %bitcast.5), calls=%async_computation.2 | async-start | bytes 3145728 | tf_op jit(solution)/shard_map/all_to_all | solution.py:460
  77.0 5.5 %collective-permute-start.9 = (bf16[8,512,128]{2,1,0:T(8,128)(2,1)S(1)}, bf16[8,512,128]{2,1,0:T(8,128)(2,1)S(1)}, u32[]{:S(2)}, u32[]{:S(2)}) collective-permute-start(bf16[8,512,128]{2,1,0:T(8,128)(2,1)S(1)} %copy-done.3), channel_id=1, source_target_pairs={{0,32},{32,0},{64,96},{96,64},{1,33},{33,1},{65,97},{97,65},{2,34}... | collective-permute-start | bytes 3145736 | tf_op jit(solution)/shard_map/ppermute | solution.py:440
  80.8 2.7 %collective-permute-start.10 = (bf16[8,512,128]{2,1,0:T(8,128)(2,1)S(1)}, bf16[8,512,128]{2,1,0:T(8,128)(2,1)S(1)}, u32[]{:S(2)}, u32[]{:S(2)}) collective-permute-start(bf16[8,512,128]{2,1,0:T(8,128)(2,1)S(1)} %collective-permute-done.2.refs_3_), channel_id=1, source_target_pairs={{0,32},{32,0},{64,96},{96,64},{1,33},{33,1},{65,97},{97,65},{2,34}... | collective-permute-start | bytes 3145736 | tf_op jit(solution)/shard_map/ppermute | solution.py:454
  80.8 25.9 %collective-permute-start.8 = (bf16[8,512,128]{2,1,0:T(8,128)(2,1)}, bf16[8,512,128]{2,1,0:T(8,128)(2,1)}, u32[]{:S(2)}, u32[]{:S(2)}) collective-permute-start(bf16[8,512,128]{2,1,0:T(8,128)(2,1)} %get-tuple-element.40.refs_2_), channel_id=1, source_target_pairs={{0,64},{32,96},{64,0},{96,32},{1,65},{33,97},{65,1},{97,33},{2,66}... | collective-permute-start | bytes 3145736 | tf_op jit(solution)/shard_map/ppermute | solution.py:445
  99.9 6.8 %copy-start.1 = (bf16[8,512,128]{2,1,0:T(8,128)(2,1)S(1)}, bf16[8,512,128]{2,1,0:T(8,128)(2,1)}, u32[]{:S(2)}) copy-start(bf16[8,512,128]{2,1,0:T(8,128)(2,1)} %get-tuple-element.42.refs_2_) | copy-start | bytes 3145732
  99.9 26.5 %all-to-all-start.3 = ((bf16[768,8,128]{2,1,0:T(8,128)(2,1)}), bf16[768,8,128]{2,1,0:T(8,128)(2,1)}, u32[]{:S(2)}, u32[]{:S(2)}) async-start(bf16[768,8,128]{2,1,0:T(8,128)(2,1)} %bitcast.6), calls=%async_computation.3 | async-start | bytes 3145728 | tf_op jit(solution)/shard_map/all_to_all | solution.py:460
  104.9 4.0 %collective-permute-start.11 = (bf16[8,512,128]{2,1,0:T(8,128)(2,1)}, bf16[8,512,128]{2,1,0:T(8,128)(2,1)S(1)}, u32[]{:S(2)}, u32[]{:S(2)}) collective-permute-start(bf16[8,512,128]{2,1,0:T(8,128)(2,1)} %get-tuple-element.40.refs_2_), channel_id=1, source_target_pairs={{0,32},{32,0},{64,96},{96,64},{1,33},{33,1},{65,97},{97,65},{2,34}... | collective-permute-start | bytes 3145736 | tf_op jit(solution)/shard_map/ppermute | solution.py:440
  106.7 4.3 %collective-permute-start.12 = (bf16[8,512,128]{2,1,0:T(8,128)(2,1)}, bf16[8,512,128]{2,1,0:T(8,128)(2,1)S(1)}, u32[]{:S(2)}, u32[]{:S(2)}) collective-permute-start(bf16[8,512,128]{2,1,0:T(8,128)(2,1)} %collective-permute-done.8.refs_3_), channel_id=1, source_target_pairs={{0,32},{32,0},{64,96},{96,64},{1,33},{33,1},{65,97},{97,65},{2,34}... | collective-permute-start | bytes 3145736 | tf_op jit(solution)/shard_map/ppermute | solution.py:454
  106.7 24.7 %collective-permute-start.13 = (bf16[8,512,128]{2,1,0:T(8,128)(2,1)S(1)}, bf16[8,512,128]{2,1,0:T(8,128)(2,1)S(1)}, u32[]{:S(2)}, u32[]{:S(2)}) collective-permute-start(bf16[8,512,128]{2,1,0:T(8,128)(2,1)S(1)} %copy-done.1), channel_id=1, source_target_pairs={{0,32},{32,0},{64,96},{96,64},{1,33},{33,1},{65,97},{97,65},{2,34}... | collective-permute-start | bytes 3145736 | tf_op jit(solution)/shard_map/ppermute | solution.py:440
  107.2 27.6 %collective-permute-start.7 = (bf16[8,512,128]{2,1,0:T(8,128)(2,1)S(1)}, bf16[8,512,128]{2,1,0:T(8,128)(2,1)S(1)}, u32[]{:S(2)}, u32[]{:S(2)}) collective-permute-start(bf16[8,512,128]{2,1,0:T(8,128)(2,1)S(1)} %copy-done.1), channel_id=1, source_target_pairs={{0,64},{32,96},{64,0},{96,32},{1,65},{33,97},{65,1},{97,33},{2,66}... | collective-permute-start | bytes 3145736 | tf_op jit(solution)/shard_map/ppermute | solution.py:445
  126.4 26.1 %all-to-all-start.4 = ((bf16[768,8,128]{2,1,0:T(8,128)(2,1)}), bf16[768,8,128]{2,1,0:T(8,128)(2,1)}, u32[]{:S(2)}, u32[]{:S(2)}) async-start(bf16[768,8,128]{2,1,0:T(8,128)(2,1)} %bitcast.7), calls=%async_computation.4 | async-start | bytes 3145728 | tf_op jit(solution)/shard_map/all_to_all | solution.py:460
  134.8 3.3 %collective-permute-start.14 = (bf16[8,512,128]{2,1,0:T(8,128)(2,1)S(1)}, bf16[8,512,128]{2,1,0:T(8,128)(2,1)S(1)}, u32[]{:S(2)}, u32[]{:S(2)}) collective-permute-start(bf16[8,512,128]{2,1,0:T(8,128)(2,1)S(1)} %collective-permute-done.7.refs_2_), channel_id=1, source_target_pairs={{0,32},{32,0},{64,96},{96,64},{1,33},{33,1},{65,97},{97,65},{2,34}... | collective-permute-start | bytes 3145736 | tf_op jit(solution)/shard_map/ppermute | solution.py:454
  152.5 25.8 %all-to-all-start = ((bf16[768,8,128]{2,1,0:T(8,128)(2,1)}), bf16[768,8,128]{2,1,0:T(8,128)(2,1)S(1)}, u32[]{:S(2)}, u32[]{:S(2)}) async-start(bf16[768,8,128]{2,1,0:T(8,128)(2,1)} %bitcast.3), calls=%async_computation | async-start | bytes 3145728 | tf_op jit(solution)/shard_map/all_to_all | solution.py:460

commit v6 on v3

--- a/solution.py
+++ b/solution.py
@@ -439,14 +439,12 @@
     chip_pairs = [(s, s ^ 2) for s in range(SLABS)]
     core_pairs = [(s, s ^ 1) for s in range(SLABS)]
     groups = exchange_groups(peers)
-    done, acrosses = [], []
+    done = []
+    arrivals = [lax.ppermute(part, "occ", chip_pairs) for part in mine]
     last = len(mine) - 1
     besides = [lax.ppermute(part, "occ", core_pairs) for part in mine]
     for k, part in enumerate(mine):
-        sent = part
-        if k >= 2:
-            sent, _ = lax.optimization_barrier((part, acrosses[k - 2]))
-        across = lax.ppermute(sent, "occ", chip_pairs)
+        across = arrivals[k]
         beside = besides[k]
         partial = None
         if k in (0, last):
@@ -454,7 +452,6 @@
             partial = density(table, ids, (0, 2), (own_part, beside), virt, occ, ends=False)
         before = (mine[1], partial) if k == 0 else (gamma, partial) if k == last else (gamma,)
         across, *before = lax.optimization_barrier((across,) + before)
-        acrosses.append(across)
         diagonal = lax.ppermute(across, "occ", core_pairs)
         if partial is None:
             gamma = density(table, ids, (0, 1, 2, 3), (part, across, beside, diagonal), virt, occ)

time: 181 us -> 181 us (level)
  no operation moved by 1% of the time
where the time goes in v6:
time: 181 us; the launch traced here: 180 us
  waiting for transfers between devices  84.4 us (47%)
  Pallas kernels  53.7 us (30%)
  starting transfers between devices  40.7 us (22%)
    all_to_all x5, waiting for transfers between devices, local(): lax.all_to_all(gamma.reshape(virt_count, OCC, -1), ('occ', 'aux'), split_...  52.1 us
    pallas_call x7, Pallas kernels, density(): pl.pallas_call(functools.partial(density_body, slabs, begins, ends), out_...  35.7 us
    all_to_all x5, starting transfers between devices, local(): lax.all_to_all(gamma.reshape(virt_count, OCC, -1), ('occ', 'aux'), split_...  30.7 us
    ppermute x5, waiting for transfers between devices, local(): arrivals = [lax.ppermute(part, 'occ', chip_pairs) for part in mine]  24.9 us
    ppermute x5, starting transfers between devices, local(): arrivals = [lax.ppermute(part, 'occ', chip_pairs) for part in mine]  8.99 us
    pallas_call x1, Pallas kernels, rest_pack(): pl.pallas_call(rest_body, out_shape=[jax.ShapeDtypeStruct((2, half_rows,...  7.45 us
    ppermute x5, waiting for transfers between devices, local(): diagonal = lax.ppermute(across, 'occ', core_pairs)  7.4 us
    pallas_call x1, Pallas kernels, assemble(): pl.pallas_call(assemble_body, out_shape=jax.ShapeDtypeStruct(shape, jnp.b...  5.71 us
  transfers between devices with their start and end apart: 20, of which 14 were waited for; matrix products, arithmetic and copies ran while one was open for 0% of the time, Pallas kernels for 27%

profile of v6, /device:TPU:2, one launch (start us, length us, event | category | flops | bytes accessed | tf_op | source)
XLA Modules:
  0.0 179.7 jit_solution(9845773163519706318)
XLA Ops:
  0.0 3.4 %shard_map.46.refs_2_ = bf16[8,512,128]{2,1,0:T(8,128)(2,1)} custom-call(s32[4,6]{1,0:T(4,128)} %mask_ref.3, bf16[768,8,640]{2,1,0:T(8,128)(2,1)} %x_ref.3), custom_call_target="tpu_custom_call" | custom-call | flops 536870912 | bytes 2097152 | tf_op jit(solution)/shard_map/pallas_call | solution.py:91
  3.4 0.1 collective-permute-start.5
  3.5 2.0 %collective-permute-start.4 = (bf16[8,512,128]{2,1,0:T(8,128)(2,1)}, bf16[8,512,128]{2,1,0:T(8,128)(2,1)S(1)}, u32[]{:S(2)}, u32[]{:S(2)}) collective-permute-start(bf16[8,512,128]{2,1,0:T(8,128)(2,1)} %shard_map.46.refs_2_), channel_id=1, source_target_pairs={{0,64},{32,96},{64,0},{96,32},{1,65},{33,97},{65,1},{97,33},{2,66}... | collective-permute-start | bytes 3145736 | tf_op jit(solution)/shard_map/ppermute | solution.py:443
  5.5 0.6 pad_add_fusion.ids_ref.refs_1_
  6.1 7.4 %shard_map.47 = (bf16[2,384,512]{2,1,0:T(8,128)(2,1)}, bf16[2,128,512]{2,1,0:T(8,128)(2,1)}, s32[4,6]{1,0:T(4,128)}, bf16[8,512,128]{2,1,0:T(8,128)(2,1)}, bf16[...) custom-call(s32[4,6]{1,0:T(4,128)} %mask_ref.3, ...), custom_call_target="tpu_custom_call" | custom-call | flops 3221225472 | bytes 12582912 | tf_op jit(solution)/shard_map/pallas_call | solution.py:161
  13.5 0.0 collective-permute-done.5.refs_3_
  13.5 3.9 %shard_map.48.refs_6_ = f32[2,8,384,128]{3,2,1,0:T(8,128)S(1)} custom-call(s32[4,6]{1,0:T(4,128)} %get-tuple-element.24.refs_0_, s32[2]{0:T(128)S(1)} %copy-done.2, bf16[8,512,128]{2,1,0:T(8,128)(2,1)S(1)} %copy-done, bf16[8,512,128]{2,1,0:T(8,128)(2,1)S(1)} %collective-permute-done.5.refs_3_, bf16[2,384,512]{2,1,0:T(8,128)(2,1)} %get-tuple-element.29.refs_4_.refs_6_, ...), custom_call_target="tpu_custom_call" | custom-call | flops 1207959552 | bytes 3670016 | tf_op jit(solution)/shard_map/pallas_call | solution.py:292
  17.4 12.0 %collective-permute-done.4.refs_2_ = bf16[8,512,128]{2,1,0:T(8,128)(2,1)S(1)} collective-permute-done((bf16[8,512,128]{2,1,0:T(8,128)(2,1)}, bf16[8,512,128]{2,1,0:T(8,128)(2,1)S(1)}, u32[]{:S(2)}, u32[]{:S(2)}) %collective-permute-start.4) | collective-permute-done | bytes 1048608 | tf_op jit(solution)/shard_map/ppermute | solution.py:443
  29.4 0.0 collective-permute-start.6
  29.4 1.8 collective-permute-start.3
  31.2 0.9 collective-permute-done.6.refs_3_
  32.1 4.8 %shard_map.49 = bf16[6144,128]{1,0:T(8,128)(2,1)} custom-call(s32[4,6]{1,0:T(4,128)} %get-tuple-element.24.refs_0_, s32[2]{0:T(128)S(1)} %copy-done.2, bf16[8,512,128]{2,1,0:T(8,128)(2,1)S(1)} %collective-permute-done.4.refs_2_, bf16[8,512,128]{2,1,0:T(8,128)(2,1)S(1)} %collective-permute-done.6.refs_3_, ...), custom_call_target="tpu_custom_call" | custom-call | flops 1207959552 | bytes 3670016 | tf_op jit(solution)/shard_map/pallas_call | solution.py:292
  36.9 11.1 %all-to-all-start.1 = ((bf16[768,8,128]{2,1,0:T(8,128)(2,1)}), bf16[768,8,128]{2,1,0:T(8,128)(2,1)}, u32[]{:S(2)}, u32[]{:S(2)}) async-start(bf16[768,8,128]{2,1,0:T(8,128)(2,1)} %bitcast.4), calls=%async_computation.1 | async-start | bytes 3145728 | tf_op jit(solution)/shard_map/all_to_all | solution.py:460
  48.1 0.1 collective-permute-start.7
  48.2 7.0 %collective-permute-done.3.refs_3_ = bf16[8,512,128]{2,1,0:T(8,128)(2,1)S(1)} collective-permute-done((bf16[8,512,128]{2,1,0:T(8,128)(2,1)}, bf16[8,512,128]{2,1,0:T(8,128)(2,1)S(1)}, u32[]{:S(2)}, u32[]{:S(2)}) %collective-permute-start.3) | collective-permute-done | bytes 1048608 | tf_op jit(solution)/shard_map/ppermute | solution.py:443
  55.2 0.0 collective-permute-start.8
  55.2 1.7 collective-permute-start.2
  57.0 0.0 collective-permute-done.7.refs_4_
  57.0 0.9 collective-permute-done.8.refs_5_
  57.9 6.2 %shard_map.50 = bf16[6144,128]{1,0:T(8,128)(2,1)} custom-call(s32[4,6]{1,0:T(4,128)} %get-tuple-element.24.refs_0_, s32[2]{0:T(128)S(1)} %copy-done.2, bf16[8,512,128]{2,1,0:T(8,128)(2,1)} %get-tuple-element.28.refs_2_, bf16[8,512,128]{2,1,0:T(8,128)(2,1)S(1)} %collective-permute-done.3.refs_3_, bf16[8,512,128]{2,1,0:T(8,128)(2,1)S(1)} %collective-permute-done.7.refs_4_, ...), custom_call_target="tpu_custom_call" | custom-call | flops 2415919104 | bytes 5767168 | tf_op jit(solution)/shard_map/pallas_call | solution.py:292
  64.1 8.3 %all-to-all-done.1.refs_0_ = bf16[768,8,128]{2,1,0:T(8,128)(2,1)} async-done(((bf16[768,8,128]{2,1,0:T(8,128)(2,1)}), bf16[768,8,128]{2,1,0:T(8,128)(2,1)}, u32[]{:S(2)}, u32[]{:S(2)}) %all-to-all-start.1) | async-done | bytes 1572896 | tf_op jit(solution)/shard_map/all_to_all | solution.py:460
  72.3 4.6 %all-to-all-start.2 = ((bf16[768,8,128]{2,1,0:T(8,128)(2,1)}), bf16[768,8,128]{2,1,0:T(8,128)(2,1)}, u32[]{:S(2)}, u32[]{:S(2)}) async-start(bf16[768,8,128]{2,1,0:T(8,128)(2,1)} %bitcast.5), calls=%async_computation.2 | async-start | bytes 3145728 | tf_op jit(solution)/shard_map/all_to_all | solution.py:460
  76.9 0.1 collective-permute-start.9
  77.0 3.8 %collective-permute-done.2.refs_3_ = bf16[8,512,128]{2,1,0:T(8,128)(2,1)S(1)} collective-permute-done((bf16[8,512,128]{2,1,0:T(8,128)(2,1)S(1)}, bf16[8,512,128]{2,1,0:T(8,128)(2,1)S(1)}, u32[]{:S(2)}, u32[]{:S(2)}) %collective-permute-start.2) | collective-permute-done | bytes 1048608 | tf_op jit(solution)/shard_map/ppermute | solution.py:443
  80.8 0.0 collective-permute-start.10
  80.8 1.7 collective-permute-start.1
  82.5 0.0 collective-permute-done.9.refs_4_
  82.5 0.9 collective-permute-done.10.refs_5_
  83.4 5.9 %shard_map.51 = bf16[6144,128]{1,0:T(8,128)(2,1)} custom-call(s32[4,6]{1,0:T(4,128)} %get-tuple-element.24.refs_0_, s32[2]{0:T(128)S(1)} %copy-done.2, bf16[8,512,128]{2,1,0:T(8,128)(2,1)S(1)} %copy-done.3, bf16[8,512,128]{2,1,0:T(8,128)(2,1)S(1)} %collective-permute-done.2.refs_3_, bf16[8,512,128]{2,1,0:T(8,128)(2,1)S(1)} %collective-permute-done.9.refs_4_, ...), custom_call_target="tpu_custom_call" | custom-call | flops 2415919104 | bytes 5767168 | tf_op jit(solution)/shard_map/pallas_call | solution.py:292
  89.4 9.7 %all-to-all-done.2.refs_1_ = bf16[768,8,128]{2,1,0:T(8,128)(2,1)} async-done(((bf16[768,8,128]{2,1,0:T(8,128)(2,1)}), bf16[768,8,128]{2,1,0:T(8,128)(2,1)}, u32[]{:S(2)}, u32[]{:S(2)}) %all-to-all-start.2) | async-done | bytes 1572896 | tf_op jit(solution)/shard_map/all_to_all | solution.py:460
  99.1 5.4 %all-to-all-start.3 = ((bf16[768,8,128]{2,1,0:T(8,128)(2,1)}), bf16[768,8,128]{2,1,0:T(8,128)(2,1)}, u32[]{:S(2)}, u32[]{:S(2)}) async-start(bf16[768,8,128]{2,1,0:T(8,128)(2,1)} %bitcast.6), calls=%async_computation.3 | async-start | bytes 3145728 | tf_op jit(solution)/shard_map/all_to_all | solution.py:460
  104.5 0.1 collective-permute-start.11
  104.6 2.1 %collective-permute-done.1.refs_3_ = bf16[8,512,128]{2,1,0:T(8,128)(2,1)} collective-permute-done((bf16[8,512,128]{2,1,0:T(8,128)(2,1)}, bf16[8,512,128]{2,1,0:T(8,128)(2,1)}, u32[]{:S(2)}, u32[]{:S(2)}) %collective-permute-start.1) | collective-permute-done | bytes 1048608 | tf_op jit(solution)/shard_map/ppermute | solution.py:443
  106.7 0.5 collective-permute-start.13
  107.2 1.7 collective-permute-start
  108.9 2.0 %collective-permute-done.12.refs_5_ = bf16[8,512,128]{2,1,0:T(8,128)(2,1)S(1)} collective-permute-done((bf16[8,512,128]{2,1,0:T(8,128)(2,1)}, bf16[8,512,128]{2,1,0:T(8,128)(2,1)S(1)}, u32[]{:S(2)}, u32[]{:S(2)}) %collective-permute-start.12) | collective-permute-done | bytes 1048608 | tf_op jit(solution)/shard_map/ppermute | solution.py:455
  111.0 6.2 %shard_map.52 = bf16[6144,128]{1,0:T(8,128)(2,1)} custom-call(s32[4,6]{1,0:T(4,128)} %get-tuple-element.24.refs_0_, s32[2]{0:T(128)S(1)} %copy-done.2, bf16[8,512,128]{2,1,0:T(8,128)(2,1)} %get-tuple-element.26.refs_2_, bf16[8,512,128]{2,1,0:T(8,128)(2,1)} %collective-permute-done.1.refs_3_, bf16[8,512,128]{2,1,0:T(8,128)(2,1)S(1)} %collective-permute-done.11.refs_4_, ...), custom_call_target="tpu_custom_call" | custom-call | flops 2415919104 | bytes 5767168 | tf_op jit(solution)/shard_map/pallas_call | solution.py:292
  117.2 8.7 %all-to-all-done.3.refs_2_ = bf16[768,8,128]{2,1,0:T(8,128)(2,1)} async-done(((bf16[768,8,128]{2,1,0:T(8,128)(2,1)}), bf16[768,8,128]{2,1,0:T(8,128)(2,1)}, u32[]{:S(2)}, u32[]{:S(2)}) %all-to-all-start.3) | async-done | bytes 1572896 | tf_op jit(solution)/shard_map/all_to_all | solution.py:460
  125.9 4.7 %all-to-all-start.4 = ((bf16[768,8,128]{2,1,0:T(8,128)(2,1)}), bf16[768,8,128]{2,1,0:T(8,128)(2,1)}, u32[]{:S(2)}, u32[]{:S(2)}) async-start(bf16[768,8,128]{2,1,0:T(8,128)(2,1)} %bitcast.7), calls=%async_computation.4 | async-start | bytes 3145728 | tf_op jit(solution)/shard_map/all_to_all | solution.py:460
  130.6 3.9 %shard_map.53.refs_6_ = f32[2,8,384,128]{3,2,1,0:T(8,128)S(1)} custom-call(s32[4,6]{1,0:T(4,128)} %get-tuple-element.24.refs_0_, s32[2]{0:T(128)S(1)} %copy-done.2, bf16[8,512,128]{2,1,0:T(8,128)(2,1)S(1)} %copy-done.1, bf16[8,512,128]{2,1,0:T(8,128)(2,1)S(1)} %collective-permute-done.13.refs_3_, bf16[2,384,512]{2,1,0:T(8,128)(2,1)} %get-tuple-element.29.refs_4_.refs_6_, ...), custom_call_target="tpu_custom_call" | custom-call | flops 1207959552 | bytes 3670016 | tf_op jit(solution)/shard_map/pallas_call | solution.py:292
  134.5 0.1 collective-permute-start.14
  134.6 2.6 %collective-permute-done.14.refs_3_ = bf16[8,512,128]{2,1,0:T(8,128)(2,1)S(1)} collective-permute-done((bf16[8,512,128]{2,1,0:T(8,128)(2,1)S(1)}, bf16[8,512,128]{2,1,0:T(8,128)(2,1)S(1)}, u32[]{:S(2)}, u32[]{:S(2)}) %collective-permute-start.14) | collective-permute-done | bytes 1048608 | tf_op jit(solution)/shard_map/ppermute | solution.py:455
  137.3 4.9 %shard_map.54 = bf16[6144,128]{1,0:T(8,128)(2,1)} custom-call(s32[4,6]{1,0:T(4,128)} %get-tuple-element.24.refs_0_, s32[2]{0:T(128)S(1)} %copy-done.2, bf16[8,512,128]{2,1,0:T(8,128)(2,1)S(1)} %collective-permute-done.refs_2_, bf16[8,512,128]{2,1,0:T(8,128)(2,1)S(1)} %collective-permute-done.14.refs_3_, ...), custom_call_target="tpu_custom_call" | custom-call | flops 1207959552 | bytes 3670016 | tf_op jit(solution)/shard_map/pallas_call | solution.py:292
  142.2 9.9 %all-to-all-done.4.refs_3_ = bf16[768,8,128]{2,1,0:T(8,128)(2,1)} async-done(((bf16[768,8,128]{2,1,0:T(8,128)(2,1)}), bf16[768,8,128]{2,1,0:T(8,128)(2,1)}, u32[]{:S(2)}, u32[]{:S(2)}) %all-to-all-start.4) | async-done | bytes 1572896 | tf_op jit(solution)/shard_map/all_to_all | solution.py:460
  152.1 4.9 %all-to-all-start = ((bf16[768,8,128]{2,1,0:T(8,128)(2,1)}), bf16[768,8,128]{2,1,0:T(8,128)(2,1)S(1)}, u32[]{:S(2)}, u32[]{:S(2)}) async-start(bf16[768,8,128]{2,1,0:T(8,128)(2,1)} %bitcast.3), calls=%async_computation | async-start | bytes 3145728 | tf_op jit(solution)/shard_map/all_to_all | solution.py:460
  157.0 5.7 %shard_map.55._ = bf16[24,8,20480]{2,1,0:T(8,128)(2,1)} custom-call(bf16[768,8,128]{2,1,0:T(8,128)(2,1)} %all-to-all-done.1.refs_0_, bf16[768,8,128]{2,1,0:T(8,128)(2,1)} %all-to-all-done.2.refs_1_, bf16[768,8,128]{2,1,0:T(8,128)(2,1)} %all-to-all-done.3.refs_2_, bf16[768,8,128]{2,1,0:T(8,128)(2,1)} %all-to-all-done.4.refs_3_), custom_call_target="tpu_custom_call" | custom-call | bytes 15728640 | tf_op jit(solution)/shard_map/pallas_call | solution.py:367
  162.7 15.5 %all-to-all-done.part = bf16[768,8,128]{2,1,0:T(8,128)(2,1)S(1)} async-done(((bf16[768,8,128]{2,1,0:T(8,128)(2,1)}), bf16[768,8,128]{2,1,0:T(8,128)(2,1)S(1)}, u32[]{:S(2)}, u32[]{:S(2)}) %all-to-all-start) | async-done | bytes 1572896 | tf_op jit(solution)/shard_map/all_to_all | solution.py:460
  178.2 1.4 shard_map.56
  (12 shorter events, 0.0 us)
Async XLA Ops:
  3.4 10.2 %collective-permute-start.5 = (bf16[8,512,128]{2,1,0:T(8,128)(2,1)}, bf16[8,512,128]{2,1,0:T(8,128)(2,1)S(1)}, u32[]{:S(2)}, u32[]{:S(2)}) collective-permute-start(bf16[8,512,128]{2,1,0:T(8,128)(2,1)} %shard_map.46.refs_2_), channel_id=1, source_target_pairs={{0,32},{32,0},{64,96},{96,64},{1,33},{33,1},{65,97},{97,65},{2,34}... | collective-permute-start | bytes 3145736 | tf_op jit(solution)/shard_map/ppermute | solution.py:445
  3.5 25.9 %collective-permute-start.4 = (bf16[8,512,128]{2,1,0:T(8,128)(2,1)}, bf16[8,512,128]{2,1,0:T(8,128)(2,1)S(1)}, u32[]{:S(2)}, u32[]{:S(2)}) collective-permute-start(bf16[8,512,128]{2,1,0:T(8,128)(2,1)} %shard_map.46.refs_2_), channel_id=1, source_target_pairs={{0,64},{32,96},{64,0},{96,32},{1,65},{33,97},{65,1},{97,33},{2,66}... | collective-permute-start | bytes 3145736 | tf_op jit(solution)/shard_map/ppermute | solution.py:443
  6.1 7.5 %copy-start = (bf16[8,512,128]{2,1,0:T(8,128)(2,1)S(1)}, bf16[8,512,128]{2,1,0:T(8,128)(2,1)}, u32[]{:S(2)}) copy-start(bf16[8,512,128]{2,1,0:T(8,128)(2,1)} %shard_map.46.refs_2_) | copy-start | bytes 3145732
  6.1 7.5 %copy-start.2 = (s32[2]{0:T(128)S(1)}, s32[2]{0:T(128)}, u32[]{:S(2)}) copy-start(s32[2]{0:T(128)} %pad_add_fusion.ids_ref.refs_1_) | copy-start | bytes 28
  29.4 2.7 %collective-permute-start.6 = (bf16[8,512,128]{2,1,0:T(8,128)(2,1)S(1)}, bf16[8,512,128]{2,1,0:T(8,128)(2,1)S(1)}, u32[]{:S(2)}, u32[]{:S(2)}) collective-permute-start(bf16[8,512,128]{2,1,0:T(8,128)(2,1)S(1)} %collective-permute-done.4.refs_2_), channel_id=1, source_target_pairs={{0,32},{32,0},{64,96},{96,64},{1,33},{33,1},{65,97},{97,65},{2,34}... | collective-permute-start | bytes 3145736 | tf_op jit(solution)/shard_map/ppermute | solution.py:455
  29.4 25.8 %collective-permute-start.3 = (bf16[8,512,128]{2,1,0:T(8,128)(2,1)}, bf16[8,512,128]{2,1,0:T(8,128)(2,1)S(1)}, u32[]{:S(2)}, u32[]{:S(2)}) collective-permute-start(bf16[8,512,128]{2,1,0:T(8,128)(2,1)} %get-tuple-element.28.refs_2_), channel_id=1, source_target_pairs={{0,64},{32,96},{64,0},{96,32},{1,65},{33,97},{65,1},{97,33},{2,66}... | collective-permute-start | bytes 3145736 | tf_op jit(solution)/shard_map/ppermute | solution.py:443
  36.9 18.3 %copy-start.3 = (bf16[8,512,128]{2,1,0:T(8,128)(2,1)S(1)}, bf16[8,512,128]{2,1,0:T(8,128)(2,1)}, u32[]{:S(2)}) copy-start(bf16[8,512,128]{2,1,0:T(8,128)(2,1)} %get-tuple-element.27.refs_2_) | copy-start | bytes 3145732
  36.9 35.4 %all-to-all-start.1 = ((bf16[768,8,128]{2,1,0:T(8,128)(2,1)}), bf16[768,8,128]{2,1,0:T(8,128)(2,1)}, u32[]{:S(2)}, u32[]{:S(2)}) async-start(bf16[768,8,128]{2,1,0:T(8,128)(2,1)} %bitcast.4), calls=%async_computation.1 | async-start | bytes 3145728 | tf_op jit(solution)/shard_map/all_to_all | solution.py:460
  48.1 8.9 %collective-permute-start.7 = (bf16[8,512,128]{2,1,0:T(8,128)(2,1)}, bf16[8,512,128]{2,1,0:T(8,128)(2,1)S(1)}, u32[]{:S(2)}, u32[]{:S(2)}) collective-permute-start(bf16[8,512,128]{2,1,0:T(8,128)(2,1)} %get-tuple-element.28.refs_2_), channel_id=1, source_target_pairs={{0,32},{32,0},{64,96},{96,64},{1,33},{33,1},{65,97},{97,65},{2,34}... | collective-permute-start | bytes 3145736 | tf_op jit(solution)/shard_map/ppermute | solution.py:445
  55.2 2.7 %collective-permute-start.8 = (bf16[8,512,128]{2,1,0:T(8,128)(2,1)S(1)}, bf16[8,512,128]{2,1,0:T(8,128)(2,1)S(1)}, u32[]{:S(2)}, u32[]{:S(2)}) collective-permute-start(bf16[8,512,128]{2,1,0:T(8,128)(2,1)S(1)} %collective-permute-done.3.refs_3_), channel_id=1, source_target_pairs={{0,32},{32,0},{64,96},{96,64},{1,33},{33,1},{65,97},{97,65},{2,34}... | collective-permute-start | bytes 3145736 | tf_op jit(solution)/shard_map/ppermute | solution.py:455
  55.2 25.6 %collective-permute-start.2 = (bf16[8,512,128]{2,1,0:T(8,128)(2,1)S(1)}, bf16[8,512,128]{2,1,0:T(8,128)(2,1)S(1)}, u32[]{:S(2)}, u32[]{:S(2)}) collective-permute-start(bf16[8,512,128]{2,1,0:T(8,128)(2,1)S(1)} %copy-done.3), channel_id=1, source_target_pairs={{0,64},{32,96},{64,0},{96,32},{1,65},{33,97},{65,1},{97,33},{2,66}... | collective-permute-start | bytes 3145736 | tf_op jit(solution)/shard_map/ppermute | solution.py:443
  72.3 26.7 %all-to-all-start.2 = ((bf16[768,8,128]{2,1,0:T(8,128)(2,1)}), bf16[768,8,128]{2,1,0:T(8,128)(2,1)}, u32[]{:S(2)}, u32[]{:S(2)}) async-start(bf16[768,8,128]{2,1,0:T(8,128)(2,1)} %bitcast.5), calls=%async_computation.2 | async-start | bytes 3145728 | tf_op jit(solution)/shard_map/all_to_all | solution.py:460
  76.9 5.6 %collective-permute-start.9 = (bf16[8,512,128]{2,1,0:T(8,128)(2,1)S(1)}, bf16[8,512,128]{2,1,0:T(8,128)(2,1)S(1)}, u32[]{:S(2)}, u32[]{:S(2)}) collective-permute-start(bf16[8,512,128]{2,1,0:T(8,128)(2,1)S(1)} %copy-done.3), channel_id=1, source_target_pairs={{0,32},{32,0},{64,96},{96,64},{1,33},{33,1},{65,97},{97,65},{2,34}... | collective-permute-start | bytes 3145736 | tf_op jit(solution)/shard_map/ppermute | solution.py:445
  80.8 2.7 %collective-permute-start.10 = (bf16[8,512,128]{2,1,0:T(8,128)(2,1)S(1)}, bf16[8,512,128]{2,1,0:T(8,128)(2,1)S(1)}, u32[]{:S(2)}, u32[]{:S(2)}) collective-permute-start(bf16[8,512,128]{2,1,0:T(8,128)(2,1)S(1)} %collective-permute-done.2.refs_3_), channel_id=1, source_target_pairs={{0,32},{32,0},{64,96},{96,64},{1,33},{33,1},{65,97},{97,65},{2,34}... | collective-permute-start | bytes 3145736 | tf_op jit(solution)/shard_map/ppermute | solution.py:455
  80.8 25.9 %collective-permute-start.1 = (bf16[8,512,128]{2,1,0:T(8,128)(2,1)}, bf16[8,512,128]{2,1,0:T(8,128)(2,1)}, u32[]{:S(2)}, u32[]{:S(2)}) collective-permute-start(bf16[8,512,128]{2,1,0:T(8,128)(2,1)} %get-tuple-element.26.refs_2_), channel_id=1, source_target_pairs={{0,64},{32,96},{64,0},{96,32},{1,65},{33,97},{65,1},{97,33},{2,66}... | collective-permute-start | bytes 3145736 | tf_op jit(solution)/shard_map/ppermute | solution.py:443
  99.1 7.6 %copy-start.1 = (bf16[8,512,128]{2,1,0:T(8,128)(2,1)S(1)}, bf16[8,512,128]{2,1,0:T(8,128)(2,1)}, u32[]{:S(2)}) copy-start(bf16[8,512,128]{2,1,0:T(8,128)(2,1)} %get-tuple-element.36.refs_2_) | copy-start | bytes 3145732
  99.1 26.8 %all-to-all-start.3 = ((bf16[768,8,128]{2,1,0:T(8,128)(2,1)}), bf16[768,8,128]{2,1,0:T(8,128)(2,1)}, u32[]{:S(2)}, u32[]{:S(2)}) async-start(bf16[768,8,128]{2,1,0:T(8,128)(2,1)} %bitcast.6), calls=%async_computation.3 | async-start | bytes 3145728 | tf_op jit(solution)/shard_map/all_to_all | solution.py:460
  104.5 4.5 %collective-permute-start.11 = (bf16[8,512,128]{2,1,0:T(8,128)(2,1)}, bf16[8,512,128]{2,1,0:T(8,128)(2,1)S(1)}, u32[]{:S(2)}, u32[]{:S(2)}) collective-permute-start(bf16[8,512,128]{2,1,0:T(8,128)(2,1)} %get-tuple-element.26.refs_2_), channel_id=1, source_target_pairs={{0,32},{32,0},{64,96},{96,64},{1,33},{33,1},{65,97},{97,65},{2,34}... | collective-permute-start | bytes 3145736 | tf_op jit(solution)/shard_map/ppermute | solution.py:445
  106.7 4.3 %collective-permute-start.12 = (bf16[8,512,128]{2,1,0:T(8,128)(2,1)}, bf16[8,512,128]{2,1,0:T(8,128)(2,1)S(1)}, u32[]{:S(2)}, u32[]{:S(2)}) collective-permute-start(bf16[8,512,128]{2,1,0:T(8,128)(2,1)} %collective-permute-done.1.refs_3_), channel_id=1, source_target_pairs={{0,32},{32,0},{64,96},{96,64},{1,33},{33,1},{65,97},{97,65},{2,34}... | collective-permute-start | bytes 3145736 | tf_op jit(solution)/shard_map/ppermute | solution.py:455
  106.7 24.0 %collective-permute-start.13 = (bf16[8,512,128]{2,1,0:T(8,128)(2,1)S(1)}, bf16[8,512,128]{2,1,0:T(8,128)(2,1)S(1)}, u32[]{:S(2)}, u32[]{:S(2)}) collective-permute-start(bf16[8,512,128]{2,1,0:T(8,128)(2,1)S(1)} %copy-done.1), channel_id=1, source_target_pairs={{0,32},{32,0},{64,96},{96,64},{1,33},{33,1},{65,97},{97,65},{2,34}... | collective-permute-start | bytes 3145736 | tf_op jit(solution)/shard_map/ppermute | solution.py:445
  107.2 27.4 %collective-permute-start = (bf16[8,512,128]{2,1,0:T(8,128)(2,1)S(1)}, bf16[8,512,128]{2,1,0:T(8,128)(2,1)S(1)}, u32[]{:S(2)}, u32[]{:S(2)}) collective-permute-start(bf16[8,512,128]{2,1,0:T(8,128)(2,1)S(1)} %copy-done.1), channel_id=1, source_target_pairs={{0,64},{32,96},{64,0},{96,32},{1,65},{33,97},{65,1},{97,33},{2,66}... | collective-permute-start | bytes 3145736 | tf_op jit(solution)/shard_map/ppermute | solution.py:443
  125.9 26.2 %all-to-all-start.4 = ((bf16[768,8,128]{2,1,0:T(8,128)(2,1)}), bf16[768,8,128]{2,1,0:T(8,128)(2,1)}, u32[]{:S(2)}, u32[]{:S(2)}) async-start(bf16[768,8,128]{2,1,0:T(8,128)(2,1)} %bitcast.7), calls=%async_computation.4 | async-start | bytes 3145728 | tf_op jit(solution)/shard_map/all_to_all | solution.py:460
  134.5 2.7 %collective-permute-start.14 = (bf16[8,512,128]{2,1,0:T(8,128)(2,1)S(1)}, bf16[8,512,128]{2,1,0:T(8,128)(2,1)S(1)}, u32[]{:S(2)}, u32[]{:S(2)}) collective-permute-start(bf16[8,512,128]{2,1,0:T(8,128)(2,1)S(1)} %collective-permute-done.refs_2_), channel_id=1, source_target_pairs={{0,32},{32,0},{64,96},{96,64},{1,33},{33,1},{65,97},{97,65},{2,34}... | collective-permute-start | bytes 3145736 | tf_op jit(solution)/shard_map/ppermute | solution.py:455
  152.1 26.0 %all-to-all-start = ((bf16[768,8,128]{2,1,0:T(8,128)(2,1)}), bf16[768,8,128]{2,1,0:T(8,128)(2,1)S(1)}, u32[]{:S(2)}, u32[]{:S(2)}) async-start(bf16[768,8,128]{2,1,0:T(8,128)(2,1)} %bitcast.3), calls=%async_computation | async-start | bytes 3145728 | tf_op jit(solution)/shard_map/all_to_all | solution.py:460

commit v7 on v6

--- a/solution.py
+++ b/solution.py
@@ -186,26 +186,34 @@
     return packs, virt, occ, table
 
 
-def density_body(slabs, begins, ends, *refs):
+def density_body(slabs, shape_of, begins, ends, *refs):
     table_ref, ids_ref, *refs = refs
     count = len(slabs)
-    sources, (virt_in, occ_in), refs = refs[:count], refs[count:count + 2], refs[count + 2:]
+    sources = [[refs.pop(0) for _ in range(pieces)] for pieces in shape_of]
+    virt_in, occ_in, *refs = refs
     if not begins:
         partial, *refs = refs
     out, packs, virt_ref, occ_ref, total, mixed, result, in_sems, out_sems = refs
-    depth = sources[0].shape[1]
+    depth = sources[0][0].shape[1]
     half_rows = virt_ref.shape[1]
     blocks = half_rows // SPAN
     tile = depth // CAP
-    targets = [packs.at[n, :, pl.ds(0, depth), :] for n in range(count)] + [virt_ref, occ_ref]
-    arrivals = [
-        pltpu.make_async_copy(ref, target, in_sems.at[n])
-        for n, (ref, target) in enumerate(zip(list(sources) + [virt_in, occ_in], targets))
-    ]
+    arrivals = []
+    for n, parts in enumerate(sources):
+        step = OCC // len(parts)
+        arrivals.append([
+            pltpu.make_async_copy(
+                ref, packs.at[n, pl.ds(m * step, step), pl.ds(0, depth), :], in_sems.at[2 * n + m]
+            )
+            for m, ref in enumerate(parts)
+        ])
+    arrivals.append([pltpu.make_async_copy(virt_in, virt_ref, in_sems.at[2 * count])])
+    arrivals.append([pltpu.make_async_copy(occ_in, occ_ref, in_sems.at[2 * count + 1])])
     if not begins:
-        arrivals.append(pltpu.make_async_copy(partial, total, in_sems.at[count + 2]))
+        arrivals.append([pltpu.make_async_copy(partial, total, in_sems.at[2 * count + 2])])
     for n in [0, count] + list(range(1, count)) + list(range(count + 1, len(arrivals))):
-        arrivals[n].start()
+        for copy in arrivals[n]:
+            copy.start()
     for n in range(count):
         packs[n, :, depth:depth + FINE, :] = jnp.zeros((OCC, FINE, LANES), jnp.bfloat16)
     perm = permutation(True) if ends else None
@@ -214,7 +222,8 @@
     def arrived(n):
         if n not in waited:
             waited.add(n)
-            arrivals[n].wait()
+            for copy in arrivals[n]:
+                copy.wait()
 
     arrived(count)
     if not begins:
@@ -282,7 +291,9 @@
 
 
 def density(table, ids, slabs, packs, virt, occ, partial=None, ends=True):
-    depth = packs[0].shape[1]
+    packs = [pack if isinstance(pack, list) else [pack] for pack in packs]
+    shape_of = [len(pack) for pack in packs]
+    depth = packs[0][0].shape[1]
     half_rows = virt.shape[1]
     rows = 2 * half_rows * OCC
     sums = (2, OCC, half_rows, LANES)
@@ -290,12 +301,12 @@
     share = len(slabs) * LANES
     extra = [] if begins else [partial]
     return pl.pallas_call(
-        functools.partial(density_body, slabs, begins, ends),
+        functools.partial(density_body, slabs, shape_of, begins, ends),
         out_shape=jax.ShapeDtypeStruct((rows, LANES), jnp.bfloat16) if ends else jax.ShapeDtypeStruct(sums, jnp.float32),
         grid_spec=pltpu.PrefetchScalarGridSpec(
             num_scalar_prefetch=2,
             grid=(1,),
-            in_specs=[pl.BlockSpec(memory_space=pl.ANY)] * (len(slabs) + 2 + len(extra)),
+            in_specs=[pl.BlockSpec(memory_space=pl.ANY)] * (sum(shape_of) + 2 + len(extra)),
             out_specs=pl.BlockSpec(memory_space=pl.ANY),
             scratch_shapes=[
                 pltpu.VMEM((len(slabs), OCC, depth + FINE, LANES), jnp.bfloat16),
@@ -304,17 +315,17 @@
                 pltpu.VMEM(sums, jnp.float32),
                 pltpu.VMEM(sums if ends else (OCC, LANES), jnp.bfloat16),
                 pltpu.VMEM((2, half_rows * OCC, LANES) if ends else (OCC, LANES), jnp.bfloat16),
-                pltpu.SemaphoreType.DMA((len(slabs) + 3,)),
+                pltpu.SemaphoreType.DMA((2 * len(slabs) + 3,)),
                 pltpu.SemaphoreType.DMA((2 * half_rows // SPAN,)),
             ],
         ),
         compiler_params=pltpu.CompilerParams(vmem_limit_bytes=24 << 20),
         cost_estimate=pl.CostEstimate(
-            flops=share * (rows * depth // 2 + 2 * rows * ROWS),
-            bytes_accessed=share * OCC * depth * 2 + rows * LANES * 2,
+            flops=1 if ends else share * (rows * depth // 2 + 2 * rows * ROWS),
+            bytes_accessed=1 if ends else share * OCC * depth * 2 + rows * LANES * 2,
             transcendentals=0,
         ),
-    )(table, ids, *packs, virt, occ, *extra)
+    )(table, ids, *(piece for pack in packs for piece in pack), virt, occ, *extra)
 
 
 def assemble_body(*refs):
@@ -452,7 +463,7 @@
             partial = density(table, ids, (0, 2), (own_part, beside), virt, occ, ends=False)
         before = (mine[1], partial) if k == 0 else (gamma, partial) if k == last else (gamma,)
         across, *before = lax.optimization_barrier((across,) + before)
-        diagonal = lax.ppermute(across, "occ", core_pairs)
+        diagonal = [lax.ppermute(half, "occ", core_pairs) for half in jnp.split(across, 2, axis=0)]
         if partial is None:
             gamma = density(table, ids, (0, 1, 2, 3), (part, across, beside, diagonal), virt, occ)
         else:

time: 181 us -> 180 us (level)
  waiting for transfers between devices: 84.4 us -> 81.2 us
  starting transfers between devices: 40.7 us -> 42.6 us
    ppermute x5 -> x10, waiting for transfers between devices: 7.4 us -> 4.4 us  [local(): lax.ppermute(half, 'occ', core_pairs)]
    ppermute x5 -> x10, starting transfers between devices: 0.1 us -> 2.91 us  [local(): lax.ppermute(half, 'occ', core_pairs)]
  transfers between devices with their start and end apart: 20 -> 25, of which waited for: 14 -> 15; matrix products, arithmetic and copies ran while one was open for 0% -> 0% of each run, Pallas kernels for 27% -> 28%
where the time goes in v7:
time: 180 us; the launch traced here: 179 us
  waiting for transfers between devices  81.2 us (45%)
  Pallas kernels  54.1 us (30%)
  starting transfers between devices  42.6 us (24%)
    all_to_all x5, waiting for transfers between devices, local(): lax.all_to_all(gamma.reshape(virt_count, OCC, -1), ('occ', 'aux'), split_...  50.4 us
    pallas_call x7, Pallas kernels, density(): pl.pallas_call(functools.partial(density_body, slabs, shape_of, begins, e...  36.2 us
    all_to_all x5, starting transfers between devices, local(): lax.all_to_all(gamma.reshape(virt_count, OCC, -1), ('occ', 'aux'), split_...  30.3 us
    ppermute x5, waiting for transfers between devices, local(): arrivals = [lax.ppermute(part, 'occ', chip_pairs) for part in mine]  26.4 us
    ppermute x5, starting transfers between devices, local(): arrivals = [lax.ppermute(part, 'occ', chip_pairs) for part in mine]  8.98 us
    pallas_call x1, Pallas kernels, rest_pack(): pl.pallas_call(rest_body, out_shape=[jax.ShapeDtypeStruct((2, half_rows,...  7.53 us
    pallas_call x1, Pallas kernels, assemble(): pl.pallas_call(assemble_body, out_shape=jax.ShapeDtypeStruct(shape, jnp.b...  5.71 us
    ppermute x10, waiting for transfers between devices, local(): lax.ppermute(half, 'occ', core_pairs)  4.4 us
  transfers between devices with their start and end apart: 25, of which 15 were waited for; matrix products, arithmetic and copies ran while one was open for 0% of the time, Pallas kernels for 28%

profile of v7, /device:TPU:2, one launch (start us, length us, event | category | flops | bytes accessed | tf_op | source)
XLA Modules:
  0.0 179.3 jit_solution(13922690836520336895)
XLA Ops:
  0.0 3.4 %shard_map.46.refs_2_ = bf16[8,512,128]{2,1,0:T(8,128)(2,1)} custom-call(s32[4,6]{1,0:T(4,128)} %mask_ref.3, bf16[768,8,640]{2,1,0:T(8,128)(2,1)} %x_ref.3), custom_call_target="tpu_custom_call" | custom-call | flops 536870912 | bytes 2097152 | tf_op jit(solution)/shard_map/pallas_call | solution.py:91
  3.5 2.0 %collective-permute-start.4 = (bf16[8,512,128]{2,1,0:T(8,128)(2,1)}, bf16[8,512,128]{2,1,0:T(8,128)(2,1)S(1)}, u32[]{:S(2)}, u32[]{:S(2)}) collective-permute-start(bf16[8,512,128]{2,1,0:T(8,128)(2,1)} %shard_map.46.refs_2_), channel_id=1, source_target_pairs={{0,64},{32,96},{64,0},{96,32},{1,65},{33,97},{65,1},{97,33},{2,66}... | collective-permute-start | bytes 3145736 | tf_op jit(solution)/shard_map/ppermute | solution.py:454
  5.5 0.6 pad_add_fusion.ids_ref.refs_1_
  6.1 7.5 %shard_map.47 = (bf16[2,384,512]{2,1,0:T(8,128)(2,1)}, bf16[2,128,512]{2,1,0:T(8,128)(2,1)}, s32[4,6]{1,0:T(4,128)}, bf16[8,512,128]{2,1,0:T(8,128)(2,1)}, bf16[...) custom-call(s32[4,6]{1,0:T(4,128)} %mask_ref.3, ...), custom_call_target="tpu_custom_call" | custom-call | flops 3221225472 | bytes 12582912 | tf_op jit(solution)/shard_map/pallas_call | solution.py:161
  13.6 3.9 %shard_map.48.refs_7_ = f32[2,8,384,128]{3,2,1,0:T(8,128)S(1)} custom-call(s32[4,6]{1,0:T(4,128)} %get-tuple-element.24.refs_0_, s32[2]{0:T(128)S(1)} %copy-done.2, bf16[8,512,128]{2,1,0:T(8,128)(2,1)S(1)} %copy-done, bf16[8,512,128]{2,1,0:T(8,128)(2,1)S(1)} %collective-permute-done.5.refs_3_, ...), custom_call_target="tpu_custom_call" | custom-call | flops 1207959552 | bytes 3670016 | tf_op jit(solution)/shard_map/pallas_call | solution.py:303
  17.5 11.9 %collective-permute-done.4.refs_2_ = bf16[8,512,128]{2,1,0:T(8,128)(2,1)S(1)} collective-permute-done((bf16[8,512,128]{2,1,0:T(8,128)(2,1)}, bf16[8,512,128]{2,1,0:T(8,128)(2,1)S(1)}, u32[]{:S(2)}, u32[]{:S(2)}) %collective-permute-start.4) | collective-permute-done | bytes 1048608 | tf_op jit(solution)/shard_map/ppermute | solution.py:454
  29.5 0.1 collective-permute-start.6
  29.6 0.5 collective-permute-start.7
  30.1 1.8 collective-permute-start.3
  31.8 0.4 collective-permute-done.7.refs_4_
  32.2 4.9 %shard_map.49 = bf16[6144,128]{1,0:T(8,128)(2,1)} custom-call(s32[4,6]{1,0:T(4,128)} %get-tuple-element.24.refs_0_, s32[2]{0:T(128)S(1)} %copy-done.2, bf16[8,512,128]{2,1,0:T(8,128)(2,1)S(1)} %collective-permute-done.4.refs_2_, bf16[4,512,128]{2,1,0:T(8,128)(2,1)S(1)} %collective-permute-done.6.refs_3_, ...), custom_call_target="tpu_custom_call" | custom-call | flops 1 | bytes 1 | tf_op jit(solution)/shard_map/pallas_call | solution.py:303
  37.1 11.0 %all-to-all-start.1 = ((bf16[768,8,128]{2,1,0:T(8,128)(2,1)}), bf16[768,8,128]{2,1,0:T(8,128)(2,1)}, u32[]{:S(2)}, u32[]{:S(2)}) async-start(bf16[768,8,128]{2,1,0:T(8,128)(2,1)} %bitcast.4), calls=%async_computation.1 | async-start | bytes 3145728 | tf_op jit(solution)/shard_map/all_to_all | solution.py:471
  48.2 7.3 %collective-permute-done.3.refs_3_ = bf16[8,512,128]{2,1,0:T(8,128)(2,1)S(1)} collective-permute-done((bf16[8,512,128]{2,1,0:T(8,128)(2,1)}, bf16[8,512,128]{2,1,0:T(8,128)(2,1)S(1)}, u32[]{:S(2)}, u32[]{:S(2)}) %collective-permute-start.3) | collective-permute-done | bytes 1048608 | tf_op jit(solution)/shard_map/ppermute | solution.py:454
  55.5 0.1 collective-permute-start.9
  55.6 0.5 collective-permute-start.10
  56.1 1.7 collective-permute-start.2
  57.9 0.4 collective-permute-done.10.refs_6_
  58.3 6.2 %shard_map.50 = bf16[6144,128]{1,0:T(8,128)(2,1)} custom-call(s32[4,6]{1,0:T(4,128)} %get-tuple-element.24.refs_0_, s32[2]{0:T(128)S(1)} %copy-done.2, bf16[8,512,128]{2,1,0:T(8,128)(2,1)} %get-tuple-element.28.refs_2_, bf16[8,512,128]{2,1,0:T(8,128)(2,1)S(1)} %collective-permute-done.3.refs_3_, bf16[8,512,128]{2,1,0:T(8,128)(2,1)S(1)} %collective-permute-done.8.refs_4_, ...), custom_call_target="tpu_custom_call" | custom-call | flops 1 | bytes 1 | tf_op jit(solution)/shard_map/pallas_call | solution.py:303
  64.5 7.9 %all-to-all-done.1.refs_0_ = bf16[768,8,128]{2,1,0:T(8,128)(2,1)} async-done(((bf16[768,8,128]{2,1,0:T(8,128)(2,1)}), bf16[768,8,128]{2,1,0:T(8,128)(2,1)}, u32[]{:S(2)}, u32[]{:S(2)}) %all-to-all-start.1) | async-done | bytes 1572896 | tf_op jit(solution)/shard_map/all_to_all | solution.py:471
  72.4 4.6 %all-to-all-start.2 = ((bf16[768,8,128]{2,1,0:T(8,128)(2,1)}), bf16[768,8,128]{2,1,0:T(8,128)(2,1)}, u32[]{:S(2)}, u32[]{:S(2)}) async-start(bf16[768,8,128]{2,1,0:T(8,128)(2,1)} %bitcast.5), calls=%async_computation.2 | async-start | bytes 3145728 | tf_op jit(solution)/shard_map/all_to_all | solution.py:471
  77.1 4.4 %collective-permute-done.2.refs_3_ = bf16[8,512,128]{2,1,0:T(8,128)(2,1)S(1)} collective-permute-done((bf16[8,512,128]{2,1,0:T(8,128)(2,1)}, bf16[8,512,128]{2,1,0:T(8,128)(2,1)S(1)}, u32[]{:S(2)}, u32[]{:S(2)}) %collective-permute-start.2) | collective-permute-done | bytes 1048608 | tf_op jit(solution)/shard_map/ppermute | solution.py:454
  81.6 0.1 collective-permute-start.12
  81.7 0.5 collective-permute-start.13
  82.2 1.7 collective-permute-start.1
  83.9 0.4 collective-permute-done.13.refs_6_
  84.3 6.2 %shard_map.51 = bf16[6144,128]{1,0:T(8,128)(2,1)} custom-call(s32[4,6]{1,0:T(4,128)} %get-tuple-element.24.refs_0_, s32[2]{0:T(128)S(1)} %copy-done.2, bf16[8,512,128]{2,1,0:T(8,128)(2,1)} %get-tuple-element.27.refs_2_, bf16[8,512,128]{2,1,0:T(8,128)(2,1)S(1)} %collective-permute-done.2.refs_3_, bf16[8,512,128]{2,1,0:T(8,128)(2,1)S(1)} %collective-permute-done.11.refs_4_, ...), custom_call_target="tpu_custom_call" | custom-call | flops 1 | bytes 1 | tf_op jit(solution)/shard_map/pallas_call | solution.py:303
  90.5 8.7 %all-to-all-done.2.refs_1_ = bf16[768,8,128]{2,1,0:T(8,128)(2,1)} async-done(((bf16[768,8,128]{2,1,0:T(8,128)(2,1)}), bf16[768,8,128]{2,1,0:T(8,128)(2,1)}, u32[]{:S(2)}, u32[]{:S(2)}) %all-to-all-start.2) | async-done | bytes 1572896 | tf_op jit(solution)/shard_map/all_to_all | solution.py:471
  99.2 5.2 %all-to-all-start.3 = ((bf16[768,8,128]{2,1,0:T(8,128)(2,1)}), bf16[768,8,128]{2,1,0:T(8,128)(2,1)}, u32[]{:S(2)}, u32[]{:S(2)}) async-start(bf16[768,8,128]{2,1,0:T(8,128)(2,1)} %bitcast.6), calls=%async_computation.3 | async-start | bytes 3145728 | tf_op jit(solution)/shard_map/all_to_all | solution.py:471
  104.4 0.1 collective-permute-start.14
  104.5 2.8 %collective-permute-done.1.refs_3_ = bf16[8,512,128]{2,1,0:T(8,128)(2,1)S(1)} collective-permute-done((bf16[8,512,128]{2,1,0:T(8,128)(2,1)S(1)}, bf16[8,512,128]{2,1,0:T(8,128)(2,1)S(1)}, u32[]{:S(2)}, u32[]{:S(2)}) %collective-permute-start.1) | collective-permute-done | bytes 1048608 | tf_op jit(solution)/shard_map/ppermute | solution.py:454
  107.4 0.1 collective-permute-start.15
  107.5 0.5 collective-permute-start.16
  108.0 0.1 collective-permute-start.17
  108.1 1.7 collective-permute-start
  109.8 1.1 collective-permute-done.16.refs_6_
  110.9 6.0 %shard_map.52 = bf16[6144,128]{1,0:T(8,128)(2,1)} custom-call(s32[4,6]{1,0:T(4,128)} %get-tuple-element.24.refs_0_, s32[2]{0:T(128)S(1)} %copy-done.2, bf16[8,512,128]{2,1,0:T(8,128)(2,1)S(1)} %copy-done.1, bf16[8,512,128]{2,1,0:T(8,128)(2,1)S(1)} %collective-permute-done.1.refs_3_, bf16[8,512,128]{2,1,0:T(8,128)(2,1)S(1)} %collective-permute-done.14.refs_4_, ...), custom_call_target="tpu_custom_call" | custom-call | flops 1 | bytes 1 | tf_op jit(solution)/shard_map/pallas_call | solution.py:303
  116.8 9.0 %all-to-all-done.3.refs_2_ = bf16[768,8,128]{2,1,0:T(8,128)(2,1)} async-done(((bf16[768,8,128]{2,1,0:T(8,128)(2,1)}), bf16[768,8,128]{2,1,0:T(8,128)(2,1)}, u32[]{:S(2)}, u32[]{:S(2)}) %all-to-all-start.3) | async-done | bytes 1572896 | tf_op jit(solution)/shard_map/all_to_all | solution.py:471
  125.8 4.8 %all-to-all-start.4 = ((bf16[768,8,128]{2,1,0:T(8,128)(2,1)}), bf16[768,8,128]{2,1,0:T(8,128)(2,1)}, u32[]{:S(2)}, u32[]{:S(2)}) async-start(bf16[768,8,128]{2,1,0:T(8,128)(2,1)} %bitcast.7), calls=%async_computation.4 | async-start | bytes 3145728 | tf_op jit(solution)/shard_map/all_to_all | solution.py:471
  130.6 4.1 %shard_map.53.refs_7_ = f32[2,8,384,128]{3,2,1,0:T(8,128)S(1)} custom-call(s32[4,6]{1,0:T(4,128)} %get-tuple-element.24.refs_0_, s32[2]{0:T(128)S(1)} %copy-done.2, bf16[8,512,128]{2,1,0:T(8,128)(2,1)} %get-tuple-element.36.refs_2_, bf16[8,512,128]{2,1,0:T(8,128)(2,1)} %collective-permute-done.17.refs_3_, ...), custom_call_target="tpu_custom_call" | custom-call | flops 1207959552 | bytes 3670016 | tf_op jit(solution)/shard_map/pallas_call | solution.py:303
  134.9 0.5 collective-permute-start.19
  135.4 1.4 collective-permute-done.18.refs_3_
  136.8 0.7 collective-permute-done.19.refs_4_
  137.6 4.9 %shard_map.54 = bf16[6144,128]{1,0:T(8,128)(2,1)} custom-call(s32[4,6]{1,0:T(4,128)} %get-tuple-element.24.refs_0_, s32[2]{0:T(128)S(1)} %copy-done.2, bf16[8,512,128]{2,1,0:T(8,128)(2,1)S(1)} %collective-permute-done.refs_2_, bf16[4,512,128]{2,1,0:T(8,128)(2,1)S(1)} %collective-permute-done.18.refs_3_, ...), custom_call_target="tpu_custom_call" | custom-call | flops 1 | bytes 1 | tf_op jit(solution)/shard_map/pallas_call | solution.py:303
  142.5 9.4 %all-to-all-done.4.refs_3_ = bf16[768,8,128]{2,1,0:T(8,128)(2,1)} async-done(((bf16[768,8,128]{2,1,0:T(8,128)(2,1)}), bf16[768,8,128]{2,1,0:T(8,128)(2,1)}, u32[]{:S(2)}, u32[]{:S(2)}) %all-to-all-start.4) | async-done | bytes 1572896 | tf_op jit(solution)/shard_map/all_to_all | solution.py:471
  151.9 4.7 %all-to-all-start = ((bf16[768,8,128]{2,1,0:T(8,128)(2,1)}), bf16[768,8,128]{2,1,0:T(8,128)(2,1)S(1)}, u32[]{:S(2)}, u32[]{:S(2)}) async-start(bf16[768,8,128]{2,1,0:T(8,128)(2,1)} %bitcast.3), calls=%async_computation | async-start | bytes 3145728 | tf_op jit(solution)/shard_map/all_to_all | solution.py:471
  156.5 5.7 %shard_map.55._ = bf16[24,8,20480]{2,1,0:T(8,128)(2,1)} custom-call(bf16[768,8,128]{2,1,0:T(8,128)(2,1)} %all-to-all-done.1.refs_0_, bf16[768,8,128]{2,1,0:T(8,128)(2,1)} %all-to-all-done.2.refs_1_, bf16[768,8,128]{2,1,0:T(8,128)(2,1)} %all-to-all-done.3.refs_2_, bf16[768,8,128]{2,1,0:T(8,128)(2,1)} %all-to-all-done.4.refs_3_), custom_call_target="tpu_custom_call" | custom-call | bytes 15728640 | tf_op jit(solution)/shard_map/pallas_call | solution.py:378
  162.2 15.5 %all-to-all-done.part = bf16[768,8,128]{2,1,0:T(8,128)(2,1)S(1)} async-done(((bf16[768,8,128]{2,1,0:T(8,128)(2,1)}), bf16[768,8,128]{2,1,0:T(8,128)(2,1)S(1)}, u32[]{:S(2)}, u32[]{:S(2)}) %all-to-all-start) | async-done | bytes 1572896 | tf_op jit(solution)/shard_map/all_to_all | solution.py:471
  177.7 1.4 shard_map.56
  (25 shorter events, 0.7 us)
Async XLA Ops:
  3.4 10.2 %collective-permute-start.5 = (bf16[8,512,128]{2,1,0:T(8,128)(2,1)}, bf16[8,512,128]{2,1,0:T(8,128)(2,1)S(1)}, u32[]{:S(2)}, u32[]{:S(2)}) collective-permute-start(bf16[8,512,128]{2,1,0:T(8,128)(2,1)} %shard_map.46.refs_2_), channel_id=1, source_target_pairs={{0,32},{32,0},{64,96},{96,64},{1,33},{33,1},{65,97},{97,65},{2,34}... | collective-permute-start | bytes 3145736 | tf_op jit(solution)/shard_map/ppermute | solution.py:456
  3.5 25.9 %collective-permute-start.4 = (bf16[8,512,128]{2,1,0:T(8,128)(2,1)}, bf16[8,512,128]{2,1,0:T(8,128)(2,1)S(1)}, u32[]{:S(2)}, u32[]{:S(2)}) collective-permute-start(bf16[8,512,128]{2,1,0:T(8,128)(2,1)} %shard_map.46.refs_2_), channel_id=1, source_target_pairs={{0,64},{32,96},{64,0},{96,32},{1,65},{33,97},{65,1},{97,33},{2,66}... | collective-permute-start | bytes 3145736 | tf_op jit(solution)/shard_map/ppermute | solution.py:454
  6.1 7.5 %copy-start = (bf16[8,512,128]{2,1,0:T(8,128)(2,1)S(1)}, bf16[8,512,128]{2,1,0:T(8,128)(2,1)}, u32[]{:S(2)}) copy-start(bf16[8,512,128]{2,1,0:T(8,128)(2,1)} %shard_map.46.refs_2_) | copy-start | bytes 3145732
  6.1 7.5 %copy-start.2 = (s32[2]{0:T(128)S(1)}, s32[2]{0:T(128)}, u32[]{:S(2)}) copy-start(s32[2]{0:T(128)} %pad_add_fusion.ids_ref.refs_1_) | copy-start | bytes 28
  29.5 2.4 %collective-permute-start.6 = (bf16[4,512,128]{2,1,0:T(8,128)(2,1)S(1)}, bf16[4,512,128]{2,1,0:T(8,128)(2,1)S(1)}, u32[]{:S(2)}, u32[]{:S(2)}) collective-permute-start(bf16[4,512,128]{2,1,0:T(8,128)(2,1)S(1)} %get-tuple-element.48), channel_id=1, source_target_pairs={{0,32},{32,0},{64,96},{96,64},{1,33},{33,1},{65,97},{97,65},{2,34}... | collective-permute-start | bytes 1572872 | tf_op jit(solution)/shard_map/ppermute | solution.py:466
  29.6 2.6 %collective-permute-start.7 = (bf16[4,512,128]{2,1,0:T(8,128)(2,1)S(1)}, bf16[4,512,128]{2,1,0:T(8,128)(2,1)S(1)}, u32[]{:S(2)}, u32[]{:S(2)}) collective-permute-start(bf16[4,512,128]{2,1,0:T(8,128)(2,1)S(1)} %get-tuple-element.47), channel_id=1, source_target_pairs={{0,32},{32,0},{64,96},{96,64},{1,33},{33,1},{65,97},{97,65},{2,34}... | collective-permute-start | bytes 1572872 | tf_op jit(solution)/shard_map/ppermute | solution.py:466
  30.1 25.4 %collective-permute-start.3 = (bf16[8,512,128]{2,1,0:T(8,128)(2,1)}, bf16[8,512,128]{2,1,0:T(8,128)(2,1)S(1)}, u32[]{:S(2)}, u32[]{:S(2)}) collective-permute-start(bf16[8,512,128]{2,1,0:T(8,128)(2,1)} %get-tuple-element.28.refs_2_), channel_id=1, source_target_pairs={{0,64},{32,96},{64,0},{96,32},{1,65},{33,97},{65,1},{97,33},{2,66}... | collective-permute-start | bytes 3145736 | tf_op jit(solution)/shard_map/ppermute | solution.py:454
  37.1 35.3 %all-to-all-start.1 = ((bf16[768,8,128]{2,1,0:T(8,128)(2,1)}), bf16[768,8,128]{2,1,0:T(8,128)(2,1)}, u32[]{:S(2)}, u32[]{:S(2)}) async-start(bf16[768,8,128]{2,1,0:T(8,128)(2,1)} %bitcast.4), calls=%async_computation.1 | async-start | bytes 3145728 | tf_op jit(solution)/shard_map/all_to_all | solution.py:471
  48.1 9.8 %collective-permute-start.8 = (bf16[8,512,128]{2,1,0:T(8,128)(2,1)}, bf16[8,512,128]{2,1,0:T(8,128)(2,1)S(1)}, u32[]{:S(2)}, u32[]{:S(2)}) collective-permute-start(bf16[8,512,128]{2,1,0:T(8,128)(2,1)} %get-tuple-element.28.refs_2_), channel_id=1, source_target_pairs={{0,32},{32,0},{64,96},{96,64},{1,33},{33,1},{65,97},{97,65},{2,34}... | collective-permute-start | bytes 3145736 | tf_op jit(solution)/shard_map/ppermute | solution.py:456
  55.5 2.3 %collective-permute-start.9 = (bf16[4,512,128]{2,1,0:T(8,128)(2,1)S(1)}, bf16[4,512,128]{2,1,0:T(8,128)(2,1)S(1)}, u32[]{:S(2)}, u32[]{:S(2)}) collective-permute-start(bf16[4,512,128]{2,1,0:T(8,128)(2,1)S(1)} %get-tuple-element.46), channel_id=1, source_target_pairs={{0,32},{32,0},{64,96},{96,64},{1,33},{33,1},{65,97},{97,65},{2,34}... | collective-permute-start | bytes 1572872 | tf_op jit(solution)/shard_map/ppermute | solution.py:466
  55.6 2.6 %collective-permute-start.10 = (bf16[4,512,128]{2,1,0:T(8,128)(2,1)S(1)}, bf16[4,512,128]{2,1,0:T(8,128)(2,1)S(1)}, u32[]{:S(2)}, u32[]{:S(2)}) collective-permute-start(bf16[4,512,128]{2,1,0:T(8,128)(2,1)S(1)} %get-tuple-element.45), channel_id=1, source_target_pairs={{0,32},{32,0},{64,96},{96,64},{1,33},{33,1},{65,97},{97,65},{2,34}... | collective-permute-start | bytes 1572872 | tf_op jit(solution)/shard_map/ppermute | solution.py:466
  56.1 25.4 %collective-permute-start.2 = (bf16[8,512,128]{2,1,0:T(8,128)(2,1)}, bf16[8,512,128]{2,1,0:T(8,128)(2,1)S(1)}, u32[]{:S(2)}, u32[]{:S(2)}) collective-permute-start(bf16[8,512,128]{2,1,0:T(8,128)(2,1)} %get-tuple-element.27.refs_2_), channel_id=1, source_target_pairs={{0,64},{32,96},{64,0},{96,32},{1,65},{33,97},{65,1},{97,33},{2,66}... | collective-permute-start | bytes 3145736 | tf_op jit(solution)/shard_map/ppermute | solution.py:454
  72.4 26.8 %all-to-all-start.2 = ((bf16[768,8,128]{2,1,0:T(8,128)(2,1)}), bf16[768,8,128]{2,1,0:T(8,128)(2,1)}, u32[]{:S(2)}, u32[]{:S(2)}) async-start(bf16[768,8,128]{2,1,0:T(8,128)(2,1)} %bitcast.5), calls=%async_computation.2 | async-start | bytes 3145728 | tf_op jit(solution)/shard_map/all_to_all | solution.py:471
  77.0 5.2 %copy-start.1 = (bf16[8,512,128]{2,1,0:T(8,128)(2,1)S(1)}, bf16[8,512,128]{2,1,0:T(8,128)(2,1)}, u32[]{:S(2)}) copy-start(bf16[8,512,128]{2,1,0:T(8,128)(2,1)} %get-tuple-element.26.refs_2_) | copy-start | bytes 3145732
  77.0 6.9 %collective-permute-start.11 = (bf16[8,512,128]{2,1,0:T(8,128)(2,1)}, bf16[8,512,128]{2,1,0:T(8,128)(2,1)S(1)}, u32[]{:S(2)}, u32[]{:S(2)}) collective-permute-start(bf16[8,512,128]{2,1,0:T(8,128)(2,1)} %get-tuple-element.27.refs_2_), channel_id=1, source_target_pairs={{0,32},{32,0},{64,96},{96,64},{1,33},{33,1},{65,97},{97,65},{2,34}... | collective-permute-start | bytes 3145736 | tf_op jit(solution)/shard_map/ppermute | solution.py:456
  81.6 2.3 %collective-permute-start.12 = (bf16[4,512,128]{2,1,0:T(8,128)(2,1)S(1)}, bf16[4,512,128]{2,1,0:T(8,128)(2,1)S(1)}, u32[]{:S(2)}, u32[]{:S(2)}) collective-permute-start(bf16[4,512,128]{2,1,0:T(8,128)(2,1)S(1)} %get-tuple-element.44), channel_id=1, source_target_pairs={{0,32},{32,0},{64,96},{96,64},{1,33},{33,1},{65,97},{97,65},{2,34}... | collective-permute-start | bytes 1572872 | tf_op jit(solution)/shard_map/ppermute | solution.py:466
  81.7 2.6 %collective-permute-start.13 = (bf16[4,512,128]{2,1,0:T(8,128)(2,1)S(1)}, bf16[4,512,128]{2,1,0:T(8,128)(2,1)S(1)}, u32[]{:S(2)}, u32[]{:S(2)}) collective-permute-start(bf16[4,512,128]{2,1,0:T(8,128)(2,1)S(1)} %get-tuple-element.43), channel_id=1, source_target_pairs={{0,32},{32,0},{64,96},{96,64},{1,33},{33,1},{65,97},{97,65},{2,34}... | collective-permute-start | bytes 1572872 | tf_op jit(solution)/shard_map/ppermute | solution.py:466
  82.2 25.2 %collective-permute-start.1 = (bf16[8,512,128]{2,1,0:T(8,128)(2,1)S(1)}, bf16[8,512,128]{2,1,0:T(8,128)(2,1)S(1)}, u32[]{:S(2)}, u32[]{:S(2)}) collective-permute-start(bf16[8,512,128]{2,1,0:T(8,128)(2,1)S(1)} %copy-done.1), channel_id=1, source_target_pairs={{0,64},{32,96},{64,0},{96,32},{1,65},{33,97},{65,1},{97,33},{2,66}... | collective-permute-start | bytes 3145736 | tf_op jit(solution)/shard_map/ppermute | solution.py:454
  99.2 26.7 %all-to-all-start.3 = ((bf16[768,8,128]{2,1,0:T(8,128)(2,1)}), bf16[768,8,128]{2,1,0:T(8,128)(2,1)}, u32[]{:S(2)}, u32[]{:S(2)}) async-start(bf16[768,8,128]{2,1,0:T(8,128)(2,1)} %bitcast.6), calls=%async_computation.3 | async-start | bytes 3145728 | tf_op jit(solution)/shard_map/all_to_all | solution.py:471
  104.4 5.4 %collective-permute-start.14 = (bf16[8,512,128]{2,1,0:T(8,128)(2,1)S(1)}, bf16[8,512,128]{2,1,0:T(8,128)(2,1)S(1)}, u32[]{:S(2)}, u32[]{:S(2)}) collective-permute-start(bf16[8,512,128]{2,1,0:T(8,128)(2,1)S(1)} %copy-done.1), channel_id=1, source_target_pairs={{0,32},{32,0},{64,96},{96,64},{1,33},{33,1},{65,97},{97,65},{2,34}... | collective-permute-start | bytes 3145736 | tf_op jit(solution)/shard_map/ppermute | solution.py:456
  107.4 2.4 %collective-permute-start.15 = (bf16[4,512,128]{2,1,0:T(8,128)(2,1)S(1)}, bf16[4,512,128]{2,1,0:T(8,128)(2,1)S(1)}, u32[]{:S(2)}, u32[]{:S(2)}) collective-permute-start(bf16[4,512,128]{2,1,0:T(8,128)(2,1)S(1)} %get-tuple-element.42), channel_id=1, source_target_pairs={{0,32},{32,0},{64,96},{96,64},{1,33},{33,1},{65,97},{97,65},{2,34}... | collective-permute-start | bytes 1572872 | tf_op jit(solution)/shard_map/ppermute | solution.py:466
  107.5 3.4 %collective-permute-start.16 = (bf16[4,512,128]{2,1,0:T(8,128)(2,1)S(1)}, bf16[4,512,128]{2,1,0:T(8,128)(2,1)S(1)}, u32[]{:S(2)}, u32[]{:S(2)}) collective-permute-start(bf16[4,512,128]{2,1,0:T(8,128)(2,1)S(1)} %get-tuple-element.41), channel_id=1, source_target_pairs={{0,32},{32,0},{64,96},{96,64},{1,33},{33,1},{65,97},{97,65},{2,34}... | collective-permute-start | bytes 1572872 | tf_op jit(solution)/shard_map/ppermute | solution.py:466
  108.0 22.6 %collective-permute-start.17 = (bf16[8,512,128]{2,1,0:T(8,128)(2,1)}, bf16[8,512,128]{2,1,0:T(8,128)(2,1)}, u32[]{:S(2)}, u32[]{:S(2)}) collective-permute-start(bf16[8,512,128]{2,1,0:T(8,128)(2,1)} %get-tuple-element.36.refs_2_), channel_id=1, source_target_pairs={{0,32},{32,0},{64,96},{96,64},{1,33},{33,1},{65,97},{97,65},{2,34}... | collective-permute-start | bytes 3145736 | tf_op jit(solution)/shard_map/ppermute | solution.py:456
  108.1 26.7 %collective-permute-start = (bf16[8,512,128]{2,1,0:T(8,128)(2,1)}, bf16[8,512,128]{2,1,0:T(8,128)(2,1)S(1)}, u32[]{:S(2)}, u32[]{:S(2)}) collective-permute-start(bf16[8,512,128]{2,1,0:T(8,128)(2,1)} %get-tuple-element.36.refs_2_), channel_id=1, source_target_pairs={{0,64},{32,96},{64,0},{96,32},{1,65},{33,97},{65,1},{97,33},{2,66}... | collective-permute-start | bytes 3145736 | tf_op jit(solution)/shard_map/ppermute | solution.py:454
  125.8 26.0 %all-to-all-start.4 = ((bf16[768,8,128]{2,1,0:T(8,128)(2,1)}), bf16[768,8,128]{2,1,0:T(8,128)(2,1)}, u32[]{:S(2)}, u32[]{:S(2)}) async-start(bf16[768,8,128]{2,1,0:T(8,128)(2,1)} %bitcast.7), calls=%async_computation.4 | async-start | bytes 3145728 | tf_op jit(solution)/shard_map/all_to_all | solution.py:471
  134.8 2.0 %collective-permute-start.18 = (bf16[4,512,128]{2,1,0:T(8,128)(2,1)S(1)}, bf16[4,512,128]{2,1,0:T(8,128)(2,1)S(1)}, u32[]{:S(2)}, u32[]{:S(2)}) collective-permute-start(bf16[4,512,128]{2,1,0:T(8,128)(2,1)S(1)} %get-tuple-element.40), channel_id=1, source_target_pairs={{0,32},{32,0},{64,96},{96,64},{1,33},{33,1},{65,97},{97,65},{2,34}... | collective-permute-start | bytes 1572872 | tf_op jit(solution)/shard_map/ppermute | solution.py:466
  134.9 2.6 %collective-permute-start.19 = (bf16[4,512,128]{2,1,0:T(8,128)(2,1)S(1)}, bf16[4,512,128]{2,1,0:T(8,128)(2,1)S(1)}, u32[]{:S(2)}, u32[]{:S(2)}) collective-permute-start(bf16[4,512,128]{2,1,0:T(8,128)(2,1)S(1)} %get-tuple-element.39), channel_id=1, source_target_pairs={{0,32},{32,0},{64,96},{96,64},{1,33},{33,1},{65,97},{97,65},{2,34}... | collective-permute-start | bytes 1572872 | tf_op jit(solution)/shard_map/ppermute | solution.py:466
  151.9 25.9 %all-to-all-start = ((bf16[768,8,128]{2,1,0:T(8,128)(2,1)}), bf16[768,8,128]{2,1,0:T(8,128)(2,1)S(1)}, u32[]{:S(2)}, u32[]{:S(2)}) async-start(bf16[768,8,128]{2,1,0:T(8,128)(2,1)} %bitcast.3), calls=%async_computation | async-start | bytes 3145728 | tf_op jit(solution)/shard_map/all_to_all | solution.py:471

commit v8 on v7

--- a/solution.py
+++ b/solution.py
@@ -21,6 +21,10 @@
 SPAN = 96
 INNER = 4
 VMEM = 60 << 20
+
+
+def block_of(place, core, blocks):
+    return place + core * (blocks - 1 - 2 * place)
 
 
 def iota(shape, dim):
@@ -278,7 +282,8 @@
                 at = (first + n * GROUP) * OCC
                 result[which, at:at + ROWS, :] = pair[n]
         for b in range(blocks):
-            start = pl.multiple_of((b * HALVES + half) * SPAN * OCC, SPAN * OCC)
+            place = block_of(b * HALVES + half, ids_ref[0] % 2, HALVES * blocks)
+            start = pl.multiple_of(place * SPAN * OCC, SPAN * OCC)
             copy = pltpu.make_async_copy(
                 result.at[which, pl.ds(b * SPAN * OCC, SPAN * OCC), :],
                 out.at[pl.ds(start, SPAN * OCC), :],
@@ -337,8 +342,10 @@
     cols = out.shape[2] // peers
     steps = peers // INNER
 
+    core = lax.axis_index("occ") % 2
+
     def arrivals(n):
-        part = pl.ds(pl.multiple_of(n * INNER * rows, INNER * rows), INNER * rows)
+        part = pl.ds(pl.multiple_of(block_of(n, core, steps) * INNER * rows, INNER * rows), INNER * rows)
         return [
             pltpu.make_async_copy(ref.at[part], arrived.at[k, part], in_sems.at[n, k]) for k, ref in enumerate(ins)
         ]
@@ -356,7 +363,7 @@
         for copy in arrivals(n):
             copy.wait()
         for m in range(INNER):
-            at = pl.multiple_of((n * INNER + m) * rows, rows)
+            at = pl.multiple_of((block_of(n, core, steps) * INNER + m) * rows, rows)
             for k in range(count):
                 first = pl.multiple_of((n * INNER + m) * cols + k * LANES, LANES)
                 whole[:, :, pl.ds(first, LANES)] = arrived[k, pl.ds(at, rows)]
@@ -397,10 +404,12 @@
     rows = out.shape[0]
     peers = part.shape[0] // rows
     cols = out.shape[2] // peers
+    core = lax.axis_index("occ") % 2
     copies = []
     for m in range(peers):
+        place = block_of(m // INNER, core, peers // INNER) * INNER + m % INNER
         copy = pltpu.make_async_copy(
-            part.at[pl.ds(m * rows, rows)],
+            part.at[pl.ds(place * rows, rows)],
             out.at[:, :, pl.ds((m + 1) * cols - LANES, LANES)],
             sems.at[m],
         )
@@ -429,7 +438,8 @@
     for parity in range(2):
         for core in range(2):
             groups.append([
-                (2 * (((k // INNER) % HALVES) ^ parity) + core) * peers + k for k in range(peers)
+                (2 * (((k // INNER) % HALVES) ^ parity) + core) * peers + k
+                for k in (block_of(m // INNER, core, peers // INNER) * INNER + m % INNER for m in range(peers))
             ])
     return groups
 

time: 180 us -> 184 us (1.022)
  starting transfers between devices: 42.6 us -> 54.3 us
  waiting for transfers between devices: 81.2 us -> 72.7 us
    all_to_all x5, starting transfers between devices: 30.3 us -> 41.8 us  [local(): lax.all_to_all(gamma.reshape(virt_count, OCC, -1), ('occ', 'aux'), split_...]
    all_to_all x5, waiting for transfers between devices: 50.4 us -> 42.2 us  [local(): lax.all_to_all(gamma.reshape(virt_count, OCC, -1), ('occ', 'aux'), split_...]
  transfers between devices with their start and end apart: 25 -> 25, of which waited for: 15 -> 15; matrix products, arithmetic and copies ran while one was open for 0% -> 0% of each run, Pallas kernels for 28% -> 27%
where the time goes in v8:
time: 184 us; the launch traced here: 183 us
  waiting for transfers between devices  72.7 us (40%)
  starting transfers between devices  54.3 us (30%)
  Pallas kernels  54.2 us (29%)
    all_to_all x5, waiting for transfers between devices, local(): lax.all_to_all(gamma.reshape(virt_count, OCC, -1), ('occ', 'aux'), split_...  42.2 us
    all_to_all x5, starting transfers between devices, local(): lax.all_to_all(gamma.reshape(virt_count, OCC, -1), ('occ', 'aux'), split_...  41.8 us
    pallas_call x7, Pallas kernels, density(): pl.pallas_call(functools.partial(density_body, slabs, shape_of, begins, e...  36.2 us
    ppermute x5, waiting for transfers between devices, local(): arrivals = [lax.ppermute(part, 'occ', chip_pairs) for part in mine]  26.1 us
    ppermute x5, starting transfers between devices, local(): arrivals = [lax.ppermute(part, 'occ', chip_pairs) for part in mine]  8.98 us
    pallas_call x1, Pallas kernels, rest_pack(): pl.pallas_call(rest_body, out_shape=[jax.ShapeDtypeStruct((2, half_rows,...  7.56 us
    pallas_call x1, Pallas kernels, assemble(): pl.pallas_call(assemble_body, out_shape=jax.ShapeDtypeStruct(shape, jnp.b...  5.72 us
    ppermute x10, waiting for transfers between devices, local(): lax.ppermute(half, 'occ', core_pairs)  4.4 us
  transfers between devices with their start and end apart: 25, of which 15 were waited for; matrix products, arithmetic and copies ran while one was open for 0% of the time, Pallas kernels for 27%

profile of v8, /device:TPU:2, one launch (start us, length us, event | category | flops | bytes accessed | tf_op | source)
XLA Modules:
  0.0 182.5 jit_solution(7445843345283924532)
XLA Ops:
  0.0 3.4 %shard_map.46.refs_2_ = bf16[8,512,128]{2,1,0:T(8,128)(2,1)} custom-call(s32[4,6]{1,0:T(4,128)} %mask_ref.3, bf16[768,8,640]{2,1,0:T(8,128)(2,1)} %x_ref.3), custom_call_target="tpu_custom_call" | custom-call | flops 536870912 | bytes 2097152 | tf_op jit(solution)/shard_map/pallas_call | solution.py:95
  3.5 2.0 %collective-permute-start.4 = (bf16[8,512,128]{2,1,0:T(8,128)(2,1)}, bf16[8,512,128]{2,1,0:T(8,128)(2,1)S(1)}, u32[]{:S(2)}, u32[]{:S(2)}) collective-permute-start(bf16[8,512,128]{2,1,0:T(8,128)(2,1)} %shard_map.46.refs_2_), channel_id=1, source_target_pairs={{0,64},{32,96},{64,0},{96,32},{1,65},{33,97},{65,1},{97,33},{2,66}... | collective-permute-start | bytes 3145736 | tf_op jit(solution)/shard_map/ppermute | solution.py:464
  5.5 0.6 pad_add_fusion.ids_ref.refs_1_
  6.1 7.6 %shard_map.47 = (bf16[2,384,512]{2,1,0:T(8,128)(2,1)}, bf16[2,128,512]{2,1,0:T(8,128)(2,1)}, s32[4,6]{1,0:T(4,128)}, bf16[8,512,128]{2,1,0:T(8,128)(2,1)}, bf16[...) custom-call(s32[4,6]{1,0:T(4,128)} %mask_ref.3, ...), custom_call_target="tpu_custom_call" | custom-call | flops 3221225472 | bytes 12582912 | tf_op jit(solution)/shard_map/pallas_call | solution.py:165
  13.7 3.9 %shard_map.48.refs_7_ = f32[2,8,384,128]{3,2,1,0:T(8,128)S(1)} custom-call(s32[4,6]{1,0:T(4,128)} %get-tuple-element.24.refs_0_, s32[2]{0:T(128)S(1)} %copy-done.2, bf16[8,512,128]{2,1,0:T(8,128)(2,1)S(1)} %copy-done, bf16[8,512,128]{2,1,0:T(8,128)(2,1)S(1)} %collective-permute-done.5.refs_3_, ...), custom_call_target="tpu_custom_call" | custom-call | flops 1207959552 | bytes 3670016 | tf_op jit(solution)/shard_map/pallas_call | solution.py:308
  17.5 11.9 %collective-permute-done.4.refs_2_ = bf16[8,512,128]{2,1,0:T(8,128)(2,1)S(1)} collective-permute-done((bf16[8,512,128]{2,1,0:T(8,128)(2,1)}, bf16[8,512,128]{2,1,0:T(8,128)(2,1)S(1)}, u32[]{:S(2)}, u32[]{:S(2)}) %collective-permute-start.4) | collective-permute-done | bytes 1048608 | tf_op jit(solution)/shard_map/ppermute | solution.py:464
  29.5 0.1 collective-permute-start.6
  29.6 0.5 collective-permute-start.7
  30.1 1.8 collective-permute-start.3
  31.8 0.4 collective-permute-done.7.refs_4_
  32.2 4.9 %shard_map.49 = bf16[6144,128]{1,0:T(8,128)(2,1)} custom-call(s32[4,6]{1,0:T(4,128)} %get-tuple-element.24.refs_0_, s32[2]{0:T(128)S(1)} %copy-done.2, bf16[8,512,128]{2,1,0:T(8,128)(2,1)S(1)} %collective-permute-done.4.refs_2_, bf16[4,512,128]{2,1,0:T(8,128)(2,1)S(1)} %collective-permute-done.6.refs_3_, ...), custom_call_target="tpu_custom_call" | custom-call | flops 1 | bytes 1 | tf_op jit(solution)/shard_map/pallas_call | solution.py:308
  37.1 11.0 %all-to-all-start.1 = ((bf16[768,8,128]{2,1,0:T(8,128)(2,1)}), bf16[768,8,128]{2,1,0:T(8,128)(2,1)}, u32[]{:S(2)}, u32[]{:S(2)}) async-start(bf16[768,8,128]{2,1,0:T(8,128)(2,1)} %bitcast.4), calls=%async_computation.1 | async-start | bytes 3145728 | tf_op jit(solution)/shard_map/all_to_all | solution.py:481
  48.1 0.2 collective-permute-start.8
  48.3 7.1 %collective-permute-done.3.refs_3_ = bf16[8,512,128]{2,1,0:T(8,128)(2,1)S(1)} collective-permute-done((bf16[8,512,128]{2,1,0:T(8,128)(2,1)}, bf16[8,512,128]{2,1,0:T(8,128)(2,1)S(1)}, u32[]{:S(2)}, u32[]{:S(2)}) %collective-permute-start.3) | collective-permute-done | bytes 1048608 | tf_op jit(solution)/shard_map/ppermute | solution.py:464
  55.5 0.1 collective-permute-start.9
  55.6 0.5 collective-permute-start.10
  56.1 1.7 collective-permute-start.2
  57.9 0.4 collective-permute-done.10.refs_6_
  58.3 6.2 %shard_map.50 = bf16[6144,128]{1,0:T(8,128)(2,1)} custom-call(s32[4,6]{1,0:T(4,128)} %get-tuple-element.24.refs_0_, s32[2]{0:T(128)S(1)} %copy-done.2, bf16[8,512,128]{2,1,0:T(8,128)(2,1)} %get-tuple-element.28.refs_2_, bf16[8,512,128]{2,1,0:T(8,128)(2,1)S(1)} %collective-permute-done.3.refs_3_, bf16[8,512,128]{2,1,0:T(8,128)(2,1)S(1)} %collective-permute-done.8.refs_4_, ...), custom_call_target="tpu_custom_call" | custom-call | flops 1 | bytes 1 | tf_op jit(solution)/shard_map/pallas_call | solution.py:308
  64.5 4.6 %all-to-all-done.1.refs_0_ = bf16[768,8,128]{2,1,0:T(8,128)(2,1)} async-done(((bf16[768,8,128]{2,1,0:T(8,128)(2,1)}), bf16[768,8,128]{2,1,0:T(8,128)(2,1)}, u32[]{:S(2)}, u32[]{:S(2)}) %all-to-all-start.1) | async-done | bytes 1572896 | tf_op jit(solution)/shard_map/all_to_all | solution.py:481
  69.1 7.7 %all-to-all-start.2 = ((bf16[768,8,128]{2,1,0:T(8,128)(2,1)}), bf16[768,8,128]{2,1,0:T(8,128)(2,1)}, u32[]{:S(2)}, u32[]{:S(2)}) async-start(bf16[768,8,128]{2,1,0:T(8,128)(2,1)} %bitcast.5), calls=%async_computation.2 | async-start | bytes 3145728 | tf_op jit(solution)/shard_map/all_to_all | solution.py:481
  77.0 4.5 %collective-permute-done.2.refs_3_ = bf16[8,512,128]{2,1,0:T(8,128)(2,1)S(1)} collective-permute-done((bf16[8,512,128]{2,1,0:T(8,128)(2,1)}, bf16[8,512,128]{2,1,0:T(8,128)(2,1)S(1)}, u32[]{:S(2)}, u32[]{:S(2)}) %collective-permute-start.2) | collective-permute-done | bytes 1048608 | tf_op jit(solution)/shard_map/ppermute | solution.py:464
  81.6 0.1 collective-permute-start.12
  81.7 0.5 collective-permute-start.13
  82.2 1.7 collective-permute-start.1
  83.9 0.4 collective-permute-done.13.refs_6_
  84.3 6.2 %shard_map.51 = bf16[6144,128]{1,0:T(8,128)(2,1)} custom-call(s32[4,6]{1,0:T(4,128)} %get-tuple-element.24.refs_0_, s32[2]{0:T(128)S(1)} %copy-done.2, bf16[8,512,128]{2,1,0:T(8,128)(2,1)} %get-tuple-element.27.refs_2_, bf16[8,512,128]{2,1,0:T(8,128)(2,1)S(1)} %collective-permute-done.2.refs_3_, bf16[8,512,128]{2,1,0:T(8,128)(2,1)S(1)} %collective-permute-done.11.refs_4_, ...), custom_call_target="tpu_custom_call" | custom-call | flops 1 | bytes 1 | tf_op jit(solution)/shard_map/pallas_call | solution.py:308
  90.5 6.5 %all-to-all-done.2.refs_1_ = bf16[768,8,128]{2,1,0:T(8,128)(2,1)} async-done(((bf16[768,8,128]{2,1,0:T(8,128)(2,1)}), bf16[768,8,128]{2,1,0:T(8,128)(2,1)}, u32[]{:S(2)}, u32[]{:S(2)}) %all-to-all-start.2) | async-done | bytes 1572896 | tf_op jit(solution)/shard_map/all_to_all | solution.py:481
  96.9 7.7 %all-to-all-start.3 = ((bf16[768,8,128]{2,1,0:T(8,128)(2,1)}), bf16[768,8,128]{2,1,0:T(8,128)(2,1)}, u32[]{:S(2)}, u32[]{:S(2)}) async-start(bf16[768,8,128]{2,1,0:T(8,128)(2,1)} %bitcast.6), calls=%async_computation.3 | async-start | bytes 3145728 | tf_op jit(solution)/shard_map/all_to_all | solution.py:481
  104.7 0.1 collective-permute-start.14
  104.8 2.6 %collective-permute-done.1.refs_3_ = bf16[8,512,128]{2,1,0:T(8,128)(2,1)S(1)} collective-permute-done((bf16[8,512,128]{2,1,0:T(8,128)(2,1)S(1)}, bf16[8,512,128]{2,1,0:T(8,128)(2,1)S(1)}, u32[]{:S(2)}, u32[]{:S(2)}) %collective-permute-start.1) | collective-permute-done | bytes 1048608 | tf_op jit(solution)/shard_map/ppermute | solution.py:464
  107.5 0.5 collective-permute-start.16
  108.0 0.1 collective-permute-start.17
  108.1 1.7 collective-permute-start
  109.8 1.1 collective-permute-done.16.refs_6_
  110.9 6.0 %shard_map.52 = bf16[6144,128]{1,0:T(8,128)(2,1)} custom-call(s32[4,6]{1,0:T(4,128)} %get-tuple-element.24.refs_0_, s32[2]{0:T(128)S(1)} %copy-done.2, bf16[8,512,128]{2,1,0:T(8,128)(2,1)S(1)} %copy-done.1, bf16[8,512,128]{2,1,0:T(8,128)(2,1)S(1)} %collective-permute-done.1.refs_3_, bf16[8,512,128]{2,1,0:T(8,128)(2,1)S(1)} %collective-permute-done.14.refs_4_, ...), custom_call_target="tpu_custom_call" | custom-call | flops 1 | bytes 1 | tf_op jit(solution)/shard_map/pallas_call | solution.py:308
  116.9 8.2 %all-to-all-done.3.refs_2_ = bf16[768,8,128]{2,1,0:T(8,128)(2,1)} async-done(((bf16[768,8,128]{2,1,0:T(8,128)(2,1)}), bf16[768,8,128]{2,1,0:T(8,128)(2,1)}, u32[]{:S(2)}, u32[]{:S(2)}) %all-to-all-start.3) | async-done | bytes 1572896 | tf_op jit(solution)/shard_map/all_to_all | solution.py:481
  125.1 7.7 %all-to-all-start.4 = ((bf16[768,8,128]{2,1,0:T(8,128)(2,1)}), bf16[768,8,128]{2,1,0:T(8,128)(2,1)}, u32[]{:S(2)}, u32[]{:S(2)}) async-start(bf16[768,8,128]{2,1,0:T(8,128)(2,1)} %bitcast.7), calls=%async_computation.4 | async-start | bytes 3145728 | tf_op jit(solution)/shard_map/all_to_all | solution.py:481
  132.8 4.1 %shard_map.53.refs_7_ = f32[2,8,384,128]{3,2,1,0:T(8,128)S(1)} custom-call(s32[4,6]{1,0:T(4,128)} %get-tuple-element.24.refs_0_, s32[2]{0:T(128)S(1)} %copy-done.2, bf16[8,512,128]{2,1,0:T(8,128)(2,1)} %get-tuple-element.36.refs_2_, bf16[8,512,128]{2,1,0:T(8,128)(2,1)} %collective-permute-done.17.refs_3_, ...), custom_call_target="tpu_custom_call" | custom-call | flops 1207959552 | bytes 3670016 | tf_op jit(solution)/shard_map/pallas_call | solution.py:308
  137.1 0.5 collective-permute-start.19
  137.6 1.4 collective-permute-done.18.refs_3_
  139.0 0.7 collective-permute-done.19.refs_4_
  139.7 4.9 %shard_map.54 = bf16[6144,128]{1,0:T(8,128)(2,1)} custom-call(s32[4,6]{1,0:T(4,128)} %get-tuple-element.24.refs_0_, s32[2]{0:T(128)S(1)} %copy-done.2, bf16[8,512,128]{2,1,0:T(8,128)(2,1)S(1)} %collective-permute-done.refs_2_, bf16[4,512,128]{2,1,0:T(8,128)(2,1)S(1)} %collective-permute-done.18.refs_3_, ...), custom_call_target="tpu_custom_call" | custom-call | flops 1 | bytes 1 | tf_op jit(solution)/shard_map/pallas_call | solution.py:308
  144.7 8.4 %all-to-all-done.4.refs_3_ = bf16[768,8,128]{2,1,0:T(8,128)(2,1)} async-done(((bf16[768,8,128]{2,1,0:T(8,128)(2,1)}), bf16[768,8,128]{2,1,0:T(8,128)(2,1)}, u32[]{:S(2)}, u32[]{:S(2)}) %all-to-all-start.4) | async-done | bytes 1572896 | tf_op jit(solution)/shard_map/all_to_all | solution.py:481
  153.1 7.7 %all-to-all-start = ((bf16[768,8,128]{2,1,0:T(8,128)(2,1)}), bf16[768,8,128]{2,1,0:T(8,128)(2,1)S(1)}, u32[]{:S(2)}, u32[]{:S(2)}) async-start(bf16[768,8,128]{2,1,0:T(8,128)(2,1)} %bitcast.3), calls=%async_computation | async-start | bytes 3145728 | tf_op jit(solution)/shard_map/all_to_all | solution.py:481
  160.8 5.7 %shard_map.55._ = bf16[24,8,20480]{2,1,0:T(8,128)(2,1)} custom-call(bf16[768,8,128]{2,1,0:T(8,128)(2,1)} %all-to-all-done.1.refs_0_, bf16[768,8,128]{2,1,0:T(8,128)(2,1)} %all-to-all-done.2.refs_1_, bf16[768,8,128]{2,1,0:T(8,128)(2,1)} %all-to-all-done.3.refs_2_, bf16[768,8,128]{2,1,0:T(8,128)(2,1)} %all-to-all-done.4.refs_3_), custom_call_target="tpu_custom_call" | custom-call | bytes 15728640 | tf_op jit(solution)/shard_map/pallas_call | solution.py:385
  166.5 14.5 %all-to-all-done.part = bf16[768,8,128]{2,1,0:T(8,128)(2,1)S(1)} async-done(((bf16[768,8,128]{2,1,0:T(8,128)(2,1)}), bf16[768,8,128]{2,1,0:T(8,128)(2,1)S(1)}, u32[]{:S(2)}, u32[]{:S(2)}) %all-to-all-start) | async-done | bytes 1572896 | tf_op jit(solution)/shard_map/all_to_all | solution.py:481
  181.0 1.4 shard_map.56
  (25 shorter events, 0.7 us)
Async XLA Ops:
  3.4 10.3 %collective-permute-start.5 = (bf16[8,512,128]{2,1,0:T(8,128)(2,1)}, bf16[8,512,128]{2,1,0:T(8,128)(2,1)S(1)}, u32[]{:S(2)}, u32[]{:S(2)}) collective-permute-start(bf16[8,512,128]{2,1,0:T(8,128)(2,1)} %shard_map.46.refs_2_), channel_id=1, source_target_pairs={{0,32},{32,0},{64,96},{96,64},{1,33},{33,1},{65,97},{97,65},{2,34}... | collective-permute-start | bytes 3145736 | tf_op jit(solution)/shard_map/ppermute | solution.py:466
  3.5 25.9 %collective-permute-start.4 = (bf16[8,512,128]{2,1,0:T(8,128)(2,1)}, bf16[8,512,128]{2,1,0:T(8,128)(2,1)S(1)}, u32[]{:S(2)}, u32[]{:S(2)}) collective-permute-start(bf16[8,512,128]{2,1,0:T(8,128)(2,1)} %shard_map.46.refs_2_), channel_id=1, source_target_pairs={{0,64},{32,96},{64,0},{96,32},{1,65},{33,97},{65,1},{97,33},{2,66}... | collective-permute-start | bytes 3145736 | tf_op jit(solution)/shard_map/ppermute | solution.py:464
  6.1 7.6 %copy-start = (bf16[8,512,128]{2,1,0:T(8,128)(2,1)S(1)}, bf16[8,512,128]{2,1,0:T(8,128)(2,1)}, u32[]{:S(2)}) copy-start(bf16[8,512,128]{2,1,0:T(8,128)(2,1)} %shard_map.46.refs_2_) | copy-start | bytes 3145732
  6.1 7.6 %copy-start.2 = (s32[2]{0:T(128)S(1)}, s32[2]{0:T(128)}, u32[]{:S(2)}) copy-start(s32[2]{0:T(128)} %pad_add_fusion.ids_ref.refs_1_) | copy-start | bytes 28
  29.5 2.4 %collective-permute-start.6 = (bf16[4,512,128]{2,1,0:T(8,128)(2,1)S(1)}, bf16[4,512,128]{2,1,0:T(8,128)(2,1)S(1)}, u32[]{:S(2)}, u32[]{:S(2)}) collective-permute-start(bf16[4,512,128]{2,1,0:T(8,128)(2,1)S(1)} %get-tuple-element.48), channel_id=1, source_target_pairs={{0,32},{32,0},{64,96},{96,64},{1,33},{33,1},{65,97},{97,65},{2,34}... | collective-permute-start | bytes 1572872 | tf_op jit(solution)/shard_map/ppermute | solution.py:476
  29.6 2.6 %collective-permute-start.7 = (bf16[4,512,128]{2,1,0:T(8,128)(2,1)S(1)}, bf16[4,512,128]{2,1,0:T(8,128)(2,1)S(1)}, u32[]{:S(2)}, u32[]{:S(2)}) collective-permute-start(bf16[4,512,128]{2,1,0:T(8,128)(2,1)S(1)} %get-tuple-element.47), channel_id=1, source_target_pairs={{0,32},{32,0},{64,96},{96,64},{1,33},{33,1},{65,97},{97,65},{2,34}... | collective-permute-start | bytes 1572872 | tf_op jit(solution)/shard_map/ppermute | solution.py:476
  30.1 25.4 %collective-permute-start.3 = (bf16[8,512,128]{2,1,0:T(8,128)(2,1)}, bf16[8,512,128]{2,1,0:T(8,128)(2,1)S(1)}, u32[]{:S(2)}, u32[]{:S(2)}) collective-permute-start(bf16[8,512,128]{2,1,0:T(8,128)(2,1)} %get-tuple-element.28.refs_2_), channel_id=1, source_target_pairs={{0,64},{32,96},{64,0},{96,32},{1,65},{33,97},{65,1},{97,33},{2,66}... | collective-permute-start | bytes 3145736 | tf_op jit(solution)/shard_map/ppermute | solution.py:464
  37.1 32.0 %all-to-all-start.1 = ((bf16[768,8,128]{2,1,0:T(8,128)(2,1)}), bf16[768,8,128]{2,1,0:T(8,128)(2,1)}, u32[]{:S(2)}, u32[]{:S(2)}) async-start(bf16[768,8,128]{2,1,0:T(8,128)(2,1)} %bitcast.4), calls=%async_computation.1 | async-start | bytes 3145728 | tf_op jit(solution)/shard_map/all_to_all | solution.py:481
  48.1 9.8 %collective-permute-start.8 = (bf16[8,512,128]{2,1,0:T(8,128)(2,1)}, bf16[8,512,128]{2,1,0:T(8,128)(2,1)S(1)}, u32[]{:S(2)}, u32[]{:S(2)}) collective-permute-start(bf16[8,512,128]{2,1,0:T(8,128)(2,1)} %get-tuple-element.28.refs_2_), channel_id=1, source_target_pairs={{0,32},{32,0},{64,96},{96,64},{1,33},{33,1},{65,97},{97,65},{2,34}... | collective-permute-start | bytes 3145736 | tf_op jit(solution)/shard_map/ppermute | solution.py:466
  55.5 2.3 %collective-permute-start.9 = (bf16[4,512,128]{2,1,0:T(8,128)(2,1)S(1)}, bf16[4,512,128]{2,1,0:T(8,128)(2,1)S(1)}, u32[]{:S(2)}, u32[]{:S(2)}) collective-permute-start(bf16[4,512,128]{2,1,0:T(8,128)(2,1)S(1)} %get-tuple-element.46), channel_id=1, source_target_pairs={{0,32},{32,0},{64,96},{96,64},{1,33},{33,1},{65,97},{97,65},{2,34}... | collective-permute-start | bytes 1572872 | tf_op jit(solution)/shard_map/ppermute | solution.py:476
  55.6 2.6 %collective-permute-start.10 = (bf16[4,512,128]{2,1,0:T(8,128)(2,1)S(1)}, bf16[4,512,128]{2,1,0:T(8,128)(2,1)S(1)}, u32[]{:S(2)}, u32[]{:S(2)}) collective-permute-start(bf16[4,512,128]{2,1,0:T(8,128)(2,1)S(1)} %get-tuple-element.45), channel_id=1, source_target_pairs={{0,32},{32,0},{64,96},{96,64},{1,33},{33,1},{65,97},{97,65},{2,34}... | collective-permute-start | bytes 1572872 | tf_op jit(solution)/shard_map/ppermute | solution.py:476
  56.1 25.4 %collective-permute-start.2 = (bf16[8,512,128]{2,1,0:T(8,128)(2,1)}, bf16[8,512,128]{2,1,0:T(8,128)(2,1)S(1)}, u32[]{:S(2)}, u32[]{:S(2)}) collective-permute-start(bf16[8,512,128]{2,1,0:T(8,128)(2,1)} %get-tuple-element.27.refs_2_), channel_id=1, source_target_pairs={{0,64},{32,96},{64,0},{96,32},{1,65},{33,97},{65,1},{97,33},{2,66}... | collective-permute-start | bytes 3145736 | tf_op jit(solution)/shard_map/ppermute | solution.py:464
  69.1 27.8 %all-to-all-start.2 = ((bf16[768,8,128]{2,1,0:T(8,128)(2,1)}), bf16[768,8,128]{2,1,0:T(8,128)(2,1)}, u32[]{:S(2)}, u32[]{:S(2)}) async-start(bf16[768,8,128]{2,1,0:T(8,128)(2,1)} %bitcast.5), calls=%async_computation.2 | async-start | bytes 3145728 | tf_op jit(solution)/shard_map/all_to_all | solution.py:481
  76.9 5.3 %copy-start.1 = (bf16[8,512,128]{2,1,0:T(8,128)(2,1)S(1)}, bf16[8,512,128]{2,1,0:T(8,128)(2,1)}, u32[]{:S(2)}) copy-start(bf16[8,512,128]{2,1,0:T(8,128)(2,1)} %get-tuple-element.26.refs_2_) | copy-start | bytes 3145732
  76.9 7.0 %collective-permute-start.11 = (bf16[8,512,128]{2,1,0:T(8,128)(2,1)}, bf16[8,512,128]{2,1,0:T(8,128)(2,1)S(1)}, u32[]{:S(2)}, u32[]{:S(2)}) collective-permute-start(bf16[8,512,128]{2,1,0:T(8,128)(2,1)} %get-tuple-element.27.refs_2_), channel_id=1, source_target_pairs={{0,32},{32,0},{64,96},{96,64},{1,33},{33,1},{65,97},{97,65},{2,34}... | collective-permute-start | bytes 3145736 | tf_op jit(solution)/shard_map/ppermute | solution.py:466
  81.6 2.3 %collective-permute-start.12 = (bf16[4,512,128]{2,1,0:T(8,128)(2,1)S(1)}, bf16[4,512,128]{2,1,0:T(8,128)(2,1)S(1)}, u32[]{:S(2)}, u32[]{:S(2)}) collective-permute-start(bf16[4,512,128]{2,1,0:T(8,128)(2,1)S(1)} %get-tuple-element.44), channel_id=1, source_target_pairs={{0,32},{32,0},{64,96},{96,64},{1,33},{33,1},{65,97},{97,65},{2,34}... | collective-permute-start | bytes 1572872 | tf_op jit(solution)/shard_map/ppermute | solution.py:476
  81.7 2.6 %collective-permute-start.13 = (bf16[4,512,128]{2,1,0:T(8,128)(2,1)S(1)}, bf16[4,512,128]{2,1,0:T(8,128)(2,1)S(1)}, u32[]{:S(2)}, u32[]{:S(2)}) collective-permute-start(bf16[4,512,128]{2,1,0:T(8,128)(2,1)S(1)} %get-tuple-element.43), channel_id=1, source_target_pairs={{0,32},{32,0},{64,96},{96,64},{1,33},{33,1},{65,97},{97,65},{2,34}... | collective-permute-start | bytes 1572872 | tf_op jit(solution)/shard_map/ppermute | solution.py:476
  82.2 25.2 %collective-permute-start.1 = (bf16[8,512,128]{2,1,0:T(8,128)(2,1)S(1)}, bf16[8,512,128]{2,1,0:T(8,128)(2,1)S(1)}, u32[]{:S(2)}, u32[]{:S(2)}) collective-permute-start(bf16[8,512,128]{2,1,0:T(8,128)(2,1)S(1)} %copy-done.1), channel_id=1, source_target_pairs={{0,64},{32,96},{64,0},{96,32},{1,65},{33,97},{65,1},{97,33},{2,66}... | collective-permute-start | bytes 3145736 | tf_op jit(solution)/shard_map/ppermute | solution.py:464
  96.9 28.1 %all-to-all-start.3 = ((bf16[768,8,128]{2,1,0:T(8,128)(2,1)}), bf16[768,8,128]{2,1,0:T(8,128)(2,1)}, u32[]{:S(2)}, u32[]{:S(2)}) async-start(bf16[768,8,128]{2,1,0:T(8,128)(2,1)} %bitcast.6), calls=%async_computation.3 | async-start | bytes 3145728 | tf_op jit(solution)/shard_map/all_to_all | solution.py:481
  104.7 5.1 %collective-permute-start.14 = (bf16[8,512,128]{2,1,0:T(8,128)(2,1)S(1)}, bf16[8,512,128]{2,1,0:T(8,128)(2,1)S(1)}, u32[]{:S(2)}, u32[]{:S(2)}) collective-permute-start(bf16[8,512,128]{2,1,0:T(8,128)(2,1)S(1)} %copy-done.1), channel_id=1, source_target_pairs={{0,32},{32,0},{64,96},{96,64},{1,33},{33,1},{65,97},{97,65},{2,34}... | collective-permute-start | bytes 3145736 | tf_op jit(solution)/shard_map/ppermute | solution.py:466
  107.4 2.4 %collective-permute-start.15 = (bf16[4,512,128]{2,1,0:T(8,128)(2,1)S(1)}, bf16[4,512,128]{2,1,0:T(8,128)(2,1)S(1)}, u32[]{:S(2)}, u32[]{:S(2)}) collective-permute-start(bf16[4,512,128]{2,1,0:T(8,128)(2,1)S(1)} %get-tuple-element.42), channel_id=1, source_target_pairs={{0,32},{32,0},{64,96},{96,64},{1,33},{33,1},{65,97},{97,65},{2,34}... | collective-permute-start | bytes 1572872 | tf_op jit(solution)/shard_map/ppermute | solution.py:476
  107.5 3.4 %collective-permute-start.16 = (bf16[4,512,128]{2,1,0:T(8,128)(2,1)S(1)}, bf16[4,512,128]{2,1,0:T(8,128)(2,1)S(1)}, u32[]{:S(2)}, u32[]{:S(2)}) collective-permute-start(bf16[4,512,128]{2,1,0:T(8,128)(2,1)S(1)} %get-tuple-element.41), channel_id=1, source_target_pairs={{0,32},{32,0},{64,96},{96,64},{1,33},{33,1},{65,97},{97,65},{2,34}... | collective-permute-start | bytes 1572872 | tf_op jit(solution)/shard_map/ppermute | solution.py:476
  108.0 24.8 %collective-permute-start.17 = (bf16[8,512,128]{2,1,0:T(8,128)(2,1)}, bf16[8,512,128]{2,1,0:T(8,128)(2,1)}, u32[]{:S(2)}, u32[]{:S(2)}) collective-permute-start(bf16[8,512,128]{2,1,0:T(8,128)(2,1)} %get-tuple-element.36.refs_2_), channel_id=1, source_target_pairs={{0,32},{32,0},{64,96},{96,64},{1,33},{33,1},{65,97},{97,65},{2,34}... | collective-permute-start | bytes 3145736 | tf_op jit(solution)/shard_map/ppermute | solution.py:466
  108.1 28.9 %collective-permute-start = (bf16[8,512,128]{2,1,0:T(8,128)(2,1)}, bf16[8,512,128]{2,1,0:T(8,128)(2,1)S(1)}, u32[]{:S(2)}, u32[]{:S(2)}) collective-permute-start(bf16[8,512,128]{2,1,0:T(8,128)(2,1)} %get-tuple-element.36.refs_2_), channel_id=1, source_target_pairs={{0,64},{32,96},{64,0},{96,32},{1,65},{33,97},{65,1},{97,33},{2,66}... | collective-permute-start | bytes 3145736 | tf_op jit(solution)/shard_map/ppermute | solution.py:464
  125.1 28.0 %all-to-all-start.4 = ((bf16[768,8,128]{2,1,0:T(8,128)(2,1)}), bf16[768,8,128]{2,1,0:T(8,128)(2,1)}, u32[]{:S(2)}, u32[]{:S(2)}) async-start(bf16[768,8,128]{2,1,0:T(8,128)(2,1)} %bitcast.7), calls=%async_computation.4 | async-start | bytes 3145728 | tf_op jit(solution)/shard_map/all_to_all | solution.py:481
  137.0 2.0 %collective-permute-start.18 = (bf16[4,512,128]{2,1,0:T(8,128)(2,1)S(1)}, bf16[4,512,128]{2,1,0:T(8,128)(2,1)S(1)}, u32[]{:S(2)}, u32[]{:S(2)}) collective-permute-start(bf16[4,512,128]{2,1,0:T(8,128)(2,1)S(1)} %get-tuple-element.40), channel_id=1, source_target_pairs={{0,32},{32,0},{64,96},{96,64},{1,33},{33,1},{65,97},{97,65},{2,34}... | collective-permute-start | bytes 1572872 | tf_op jit(solution)/shard_map/ppermute | solution.py:476
  137.1 2.6 %collective-permute-start.19 = (bf16[4,512,128]{2,1,0:T(8,128)(2,1)S(1)}, bf16[4,512,128]{2,1,0:T(8,128)(2,1)S(1)}, u32[]{:S(2)}, u32[]{:S(2)}) collective-permute-start(bf16[4,512,128]{2,1,0:T(8,128)(2,1)S(1)} %get-tuple-element.39), channel_id=1, source_target_pairs={{0,32},{32,0},{64,96},{96,64},{1,33},{33,1},{65,97},{97,65},{2,34}... | collective-permute-start | bytes 1572872 | tf_op jit(solution)/shard_map/ppermute | solution.py:476
  153.1 27.9 %all-to-all-start = ((bf16[768,8,128]{2,1,0:T(8,128)(2,1)}), bf16[768,8,128]{2,1,0:T(8,128)(2,1)S(1)}, u32[]{:S(2)}, u32[]{:S(2)}) async-start(bf16[768,8,128]{2,1,0:T(8,128)(2,1)} %bitcast.3), calls=%async_computation | async-start | bytes 3145728 | tf_op jit(solution)/shard_map/all_to_all | solution.py:481
